TPU v7x, 32 devices: a whole 2x2x4 slice. The times are simulated.
32 devices in a mesh: dp: 4 (over z), ctx: 4 (over x, core), uly: 2 (over y).
Axes of the slice: x: 2, y: 2, z: 4, core: 2. Of those that a mesh axis runs over, the one named last changes fastest.
Arguments:
- layer_input: bfloat16 [8192, 1536], P(('dp', 'ctx', 'uly')), may hold values from -6 to 6
- span_order: int32 [4, 8], P('dp'), may hold values from 0 to 7, as said below
- doc_lengths: int32 [4, 3], P('dp'), may hold values from 1 to 1536, as said below
- pad_mask: int32 [4, 2048], P('dp'), may hold values 0 or 1
- w_qkv: bfloat16 [1536, 2048], P(('dp', 'ctx', 'uly')), may hold values from -0.15625 to 0.15625
- b_qkv: bfloat16 [2048], P(('dp', 'ctx', 'uly')), may hold values from -3 to 3
- w_out: bfloat16 [1536, 1536], P(None, ('dp', 'ctx', 'uly')), may hold values from -2.5 to 2.5
- norm_gain_attn: bfloat16 [1536], P(('dp', 'ctx', 'uly')), may hold values from 0.5 to 1.5
- norm_gain_mlp: bfloat16 [1536], P(('dp', 'ctx', 'uly')), may hold values from 0.5 to 1.5
- w_mlp: bfloat16 [1536, 26880], P(('dp', 'ctx', 'uly')), may hold values from -0.25 to 0.25
- cotangent: bfloat16 [8192, 1536], P(('dp', 'ctx', 'uly')), may hold values from -6 to 6
Outputs:
- block_output: bfloat16 [8192, 1536], P(('dp', 'ctx', 'uly'))
- input_grad: float32 [8192, 1536], P(('dp', 'ctx', 'uly'))
- grad_qkv: float32 [1536, 2048], P(('dp', 'ctx', 'uly'))
- grad_qkv_bias: float32 [2048], P(('dp', 'ctx', 'uly'))
- grad_out: float32 [1536, 1536], P(None, ('dp', 'ctx', 'uly'))
- grad_gain_attn: float32 [1536], P(('dp', 'ctx', 'uly'))
- grad_gain_mlp: float32 [1536], P(('dp', 'ctx', 'uly'))
- grad_mlp: float32 [1536, 26880], P(('dp', 'ctx', 'uly'))
Inputs may be any that keep to these rules, and one draw needn't show every extreme that they name: `span_order`: in each row, entries 2 c and 2 c + 1 are a span i < 4 and 7 - i; each row is a permutation of 0 to 7. `doc_lengths`: each row sums to 2048; the first document has 1024 tokens or more.
All inputs are finite; a program needn't handle non-finite values. No bound on the sum of `pad_mask` on one device may be relied on, other than what follows from the above.
Results may differ from a plain program's by a relative error of at most 0.025.
Values may be sent and summed in bfloat16 or wider, within the bound.
No kernel may reach another device: no remote copies, remote signals or barrier semaphores. Data moves between devices by JAX's collectives and lax.ppermute only.
A program may use at most 704 MiB of HBM per device.

v0:
```python
import functools

import jax
import jax.numpy as jnp
from jax import lax
from jax.experimental import pallas as pl
from jax.experimental.pallas import tpu as pltpu
from jax.sharding import PartitionSpec as P

HEADS = 12
KV_HEADS = 2
HEAD = 128
TOK_DEV = 256
LANES = 128
GROUP = HEADS // KV_HEADS

NORM_EPS = 1e-06
ROPE_BASE = 1000000.0
NEG_FILL = -1e30
LOG2E = 1.4426950408889634
SCALE = HEAD ** (-0.5)
FAR = 1 << 30
PLANE = ("ctx", "uly")
EVERY = ("dp", "ctx", "uly")
VMEM_LIMIT = 56 * 1024 * 1024
SMALL = pl.CostEstimate(flops=1024, bytes_accessed=1024, transcendentals=0)
F32 = jnp.float32
BF16 = jnp.bfloat16


def dot(left, right, left_dim, right_dim):
    return lax.dot_general(
        left, right, (((left_dim,), (right_dim,)), ((), ())), preferred_element_type=F32
    )


def block_bias(kinfo_ref, qinfo_ref, rows):
    info = kinfo_ref[rows, :]
    usable, place = info[:, 0:1], info[:, 1:2]
    q_place, q_begin = qinfo_ref[0:1, :], qinfo_ref[1:2, :]
    allowed = ((usable <= q_place) & (usable >= q_begin)) | (place == q_place)
    return jnp.where(allowed, 0.0, NEG_FILL)


def attn_fwd_kernel(
    need_ref, kinfo_ref, qinfo_ref, q_ref, kv_ref, o_ref, lse_ref, m_ref, l_ref, acc_ref, bias_ref
):
    blocks = kv_ref.shape[0] // TOK_DEV
    m_ref[...] = jnp.full(m_ref.shape, NEG_FILL, F32)
    l_ref[...] = jnp.zeros(l_ref.shape, F32)
    acc_ref[...] = jnp.zeros(acc_ref.shape, F32)

    def one_block(block, carry):
        @pl.when(need_ref[block] > 0)
        def _():
            rows = pl.ds(pl.multiple_of(block * TOK_DEV, TOK_DEV), TOK_DEV)
            bias_ref[...] = block_bias(kinfo_ref, qinfo_ref, rows)
            for group in range(KV_HEADS):
                key = kv_ref[rows, group * HEAD : (group + 1) * HEAD]
                value = kv_ref[rows, (KV_HEADS + group) * HEAD : (KV_HEADS + group + 1) * HEAD]
                value_t = value.T
                for head in range(group * GROUP, (group + 1) * GROUP):
                    span = slice(head * HEAD, (head + 1) * HEAD)
                    scores = dot(key, q_ref[span, :], 1, 0) * (SCALE * LOG2E) + bias_ref[...]
                    old = m_ref[head : head + 1, :]
                    new = jnp.maximum(old, jnp.max(scores, axis=0, keepdims=True))
                    weights = jnp.exp2(scores - new)
                    factor = jnp.exp2(old - new)
                    m_ref[head : head + 1, :] = new
                    l_ref[head : head + 1, :] = l_ref[head : head + 1, :] * factor + jnp.sum(
                        weights, axis=0, keepdims=True
                    )
                    acc_ref[span, :] = acc_ref[span, :] * factor + dot(
                        value_t, weights.astype(BF16), 1, 0
                    )

        return carry

    lax.fori_loop(0, blocks, one_block, 0)
    real = qinfo_ref[2:3, :].astype(F32)
    lse_ref[...] = jnp.zeros(lse_ref.shape, F32)
    for head in range(HEADS):
        span = slice(head * HEAD, (head + 1) * HEAD)
        total = l_ref[head : head + 1, :]
        o_ref[span, :] = (acc_ref[span, :] * (real / total)).astype(BF16)
        lse_ref[head : head + 1, :] = m_ref[head : head + 1, :] + jnp.log(total) * LOG2E


def attn_bwd_kernel(
    need_ref,
    kinfo_ref,
    qinfo_ref,
    cos_ref,
    sin_ref,
    q_ref,
    kv_ref,
    o_ref,
    do_ref,
    lse_ref,
    dq_ref,
    near_ref,
    far_ref,
    dots_ref,
    acc_ref,
    bias_ref,
    low_ref,
):
    blocks = kv_ref.shape[0] // TOK_DEV
    real = qinfo_ref[2:3, :].astype(F32)
    for head in range(HEADS):
        span = slice(head * HEAD, (head + 1) * HEAD)
        grad = do_ref[span, :].astype(F32) * real
        low_ref[span, :] = grad.astype(BF16)
        dots_ref[head : head + 1, :] = jnp.sum(
            grad * o_ref[span, :].astype(F32), axis=0, keepdims=True
        )
    acc_ref[...] = jnp.zeros(acc_ref.shape, F32)

    def one_block(dkv_ref, first, at, carry):
        block = first + at
        rows = pl.ds(pl.multiple_of(block * TOK_DEV, TOK_DEV), TOK_DEV)
        out_rows = pl.ds(pl.multiple_of(at * TOK_DEV, TOK_DEV), TOK_DEV)

        @pl.when(need_ref[block] == 0)
        def _():
            dkv_ref[out_rows, :] = jnp.zeros((TOK_DEV, 2 * KV_HEADS * HEAD), BF16)

        @pl.when(need_ref[block] > 0)
        def _():
            bias_ref[...] = block_bias(kinfo_ref, qinfo_ref, rows)
            for group in range(KV_HEADS):
                key_cols = slice(group * HEAD, (group + 1) * HEAD)
                value_cols = slice((KV_HEADS + group) * HEAD, (KV_HEADS + group + 1) * HEAD)
                key = kv_ref[rows, key_cols]
                value = kv_ref[rows, value_cols]
                key_t = key.T
                key_grad = jnp.zeros((TOK_DEV, HEAD), F32)
                value_grad = jnp.zeros((TOK_DEV, HEAD), F32)
                for head in range(group * GROUP, (group + 1) * GROUP):
                    span = slice(head * HEAD, (head + 1) * HEAD)
                    query, grad = q_ref[span, :], low_ref[span, :]
                    scores = dot(key, query, 1, 0) * (SCALE * LOG2E) + bias_ref[...]
                    probs = jnp.exp2(scores - lse_ref[head : head + 1, :])
                    prob_grad = dot(value, grad, 1, 0)
                    score_grad = (probs * (prob_grad - dots_ref[head : head + 1, :])).astype(BF16)
                    acc_ref[span, :] += dot(key_t, score_grad, 1, 0)
                    key_grad += dot(score_grad, query, 1, 1)
                    value_grad += dot(probs.astype(BF16), grad, 1, 1)
                dkv_ref[out_rows, key_cols] = (key_grad * SCALE).astype(BF16)
                dkv_ref[out_rows, value_cols] = value_grad.astype(BF16)

        return carry

    half_blocks = blocks // 2
    lax.fori_loop(0, half_blocks, functools.partial(one_block, near_ref, 0), 0)
    lax.fori_loop(0, half_blocks, functools.partial(one_block, far_ref, half_blocks), 0)
    cosine, sine = cos_ref[...], sin_ref[...]
    half = HEAD // 2
    for head in range(HEADS):
        start = head * HEAD
        whole = (acc_ref[start : start + HEAD, :] * SCALE).astype(BF16).astype(F32)
        first, second = whole[:half], whole[half:]
        turned = jnp.concatenate(
            [first * cosine + second * sine, second * cosine - first * sine], axis=0
        )
        dq_ref[:, start : start + HEAD] = turned.T.astype(BF16)


def vmem_specs(count):
    return [pl.BlockSpec(memory_space=pltpu.VMEM)] * count


def attention_forward(need, kinfo, qinfo, query_t, kv_all):
    rows = query_t.shape[1]
    return pl.pallas_call(
        attn_fwd_kernel,
        out_shape=(
            jax.ShapeDtypeStruct((HEADS * HEAD, rows), BF16),
            jax.ShapeDtypeStruct((16, rows), F32),
        ),
        in_specs=[pl.BlockSpec(memory_space=pltpu.SMEM)] + vmem_specs(4),
        out_specs=tuple(vmem_specs(2)),
        scratch_shapes=[
            pltpu.VMEM((16, rows), F32),
            pltpu.VMEM((16, rows), F32),
            pltpu.VMEM((HEADS * HEAD, rows), F32),
            pltpu.VMEM((TOK_DEV, rows), F32),
        ],
        compiler_params=pltpu.CompilerParams(vmem_limit_bytes=VMEM_LIMIT),
        cost_estimate=SMALL,
    )(need, kinfo, qinfo, query_t, kv_all)


def attention_backward(need, kinfo, qinfo, cos_t, sin_t, query_t, kv_all, out_t, grad_t, lse):
    rows = query_t.shape[1]
    return pl.pallas_call(
        attn_bwd_kernel,
        out_shape=(
            jax.ShapeDtypeStruct((rows, HEADS * HEAD), BF16),
            jax.ShapeDtypeStruct((kv_all.shape[0] // 2, kv_all.shape[1]), BF16),
            jax.ShapeDtypeStruct((kv_all.shape[0] // 2, kv_all.shape[1]), BF16),
        ),
        in_specs=[pl.BlockSpec(memory_space=pltpu.SMEM)] + vmem_specs(9),
        out_specs=tuple(vmem_specs(3)),
        scratch_shapes=[
            pltpu.VMEM((16, rows), F32),
            pltpu.VMEM((HEADS * HEAD, rows), F32),
            pltpu.VMEM((TOK_DEV, rows), F32),
            pltpu.VMEM((HEADS * HEAD, rows), BF16),
        ],
        compiler_params=pltpu.CompilerParams(vmem_limit_bytes=VMEM_LIMIT),
        cost_estimate=SMALL,
    )(need, kinfo, qinfo, cos_t, sin_t, query_t, kv_all, out_t, grad_t, lse)


def ffn_tile(cols, mid_ref, cot_ref, w_refs, sums, outs, act_refs, acc_refs):
    mid_grad = out = None
    if sums:
        mid_grad, out = sums[0][...].astype(F32), sums[1][...].astype(F32)
    for w_ref, act_ref in zip(w_refs, act_refs):
        both = dot(mid_ref[...], w_ref[:, : 2 * cols], 1, 0)
        hidden_grad = dot(cot_ref[...], w_ref[:, 2 * cols :], 1, 0)
        gate, up = both[:, :cols], both[:, cols:]
        share = 1.0 / (1.0 + jnp.exp(-gate))
        acted = gate * share
        act_ref[:, :cols] = (
            hidden_grad * up * (share * (1.0 + gate * (1.0 - share)))
        ).astype(BF16)
        act_ref[:, cols : 2 * cols] = (hidden_grad * acted).astype(BF16)
        act_ref[:, 2 * cols :] = (acted * up).astype(BF16)
        mid_term = dot(act_ref[:, : 2 * cols], w_ref[:, : 2 * cols], 1, 1)
        out_term = dot(act_ref[:, 2 * cols :], w_ref[:, 2 * cols :], 1, 1)
        mid_grad = mid_term if mid_grad is None else mid_grad + mid_term
        out = out_term if out is None else out + out_term
    outs[0][...] = mid_grad.astype(BF16)
    outs[1][...] = out.astype(BF16)
    for act_ref, acc_ref in zip(act_refs, acc_refs):
        acc_ref[:, : 2 * cols] += dot(mid_ref[...], act_ref[:, : 2 * cols], 0, 0)
        acc_ref[:, 2 * cols :] += dot(cot_ref[...], act_ref[:, 2 * cols :], 0, 0)


def ffn_kernel(cols, count, first, with_grad, *refs):
    mids, cots, w_refs, refs = refs[:2], refs[2:4], refs[4 : 4 + count], refs[4 + count :]
    mid_sums = out_sums = None
    if not first:
        mid_sums, out_sums, refs = refs[:2], refs[2:4], refs[4:]
    mid_outs, out_outs, refs = refs[:2], refs[2:4], refs[4:]
    if with_grad:
        grad_refs, act_refs, acc_refs = refs[:count], refs[count : 2 * count], refs[2 * count :]
    else:
        grad_refs, act_refs, acc_refs = (), refs, ()
    step, last = pl.program_id(0), pl.num_programs(0) - 1
    near = step < pl.num_programs(0) // 2

    @pl.when(step == 0)
    def _():
        for acc_ref in acc_refs:
            acc_ref[...] = jnp.zeros(acc_ref.shape, F32)

    def tile(which):
        sums = () if first else (mid_sums[which], out_sums[which])
        outs = (mid_outs[which], out_outs[which])
        ffn_tile(cols, mids[which], cots[which], w_refs, sums, outs, act_refs, acc_refs)

    pl.when(near)(lambda: tile(0))
    pl.when(jnp.logical_not(near))(lambda: tile(1))

    @pl.when(step == last)
    def _():
        for grad_ref, acc_ref in zip(grad_refs, acc_refs):
            grad_ref[...] = acc_ref[...].astype(BF16)


def feed_forward(mid_halves, cot_halves, weights, sums, with_grad):
    half_tokens, width = mid_halves[0].shape
    count, shape = len(weights), weights[0].shape
    cols = shape[1] // 3
    half = half_tokens // TOK_DEV
    near_spec = pl.BlockSpec((TOK_DEV, width), lambda i: (jnp.minimum(i, half - 1), 0))
    far_spec = pl.BlockSpec((TOK_DEV, width), lambda i: (jnp.maximum(i - half, 0), 0))
    act_spec = pl.BlockSpec((TOK_DEV, 3 * cols), lambda i: (i, 0))
    once = pl.BlockSpec(shape, lambda i: (0, 0), pipeline_mode=pl.Buffered(1))
    row_shape = jax.ShapeDtypeStruct((half_tokens, width), BF16)
    if with_grad:
        last_shape, last_spec = jax.ShapeDtypeStruct(shape, BF16), once
        scratch = [pltpu.VMEM((TOK_DEV, 3 * cols), BF16)] * count
        scratch += [pltpu.VMEM(shape, F32)] * count
    else:
        last_shape, last_spec = jax.ShapeDtypeStruct((2 * half_tokens, 3 * cols), BF16), act_spec
        scratch = []
    return pl.pallas_call(
        functools.partial(ffn_kernel, cols, count, not sums, with_grad),
        grid=(2 * half,),
        out_shape=(row_shape,) * 4 + (last_shape,) * count,
        in_specs=[near_spec, far_spec] * 2
        + [once] * count
        + [near_spec, far_spec] * (len(sums) // 2),
        out_specs=(near_spec, far_spec) * 2 + (last_spec,) * count,
        scratch_shapes=scratch,
        compiler_params=pltpu.CompilerParams(vmem_limit_bytes=VMEM_LIMIT),
        cost_estimate=SMALL,
    )(*mid_halves, *cot_halves, *weights, *sums)


def ffn_grad_kernel(cols, mid_near, mid_far, cot_near, cot_far, act_ref, grad_ref):
    half = mid_near.shape[0]
    for near, far, part in (
        (mid_near, mid_far, slice(0, 2 * cols)),
        (cot_near, cot_far, slice(2 * cols, 3 * cols)),
    ):
        grad_ref[:, part] = (
            dot(near[...], act_ref[:half, part], 0, 0) + dot(far[...], act_ref[half:, part], 0, 0)
        ).astype(BF16)


def split_at(arrays, count):
    return *arrays[:count], list(arrays[count:])


def feed_forward_grad(mid_halves, cot_halves, act):
    half_tokens, width = mid_halves[0].shape
    cols = act.shape[1] // 3
    tile = 512 if width % 512 == 0 else width
    col_spec = pl.BlockSpec((half_tokens, tile), lambda i: (0, i))
    return pl.pallas_call(
        functools.partial(ffn_grad_kernel, cols),
        grid=(width // tile,),
        out_shape=jax.ShapeDtypeStruct((width, 3 * cols), BF16),
        in_specs=[col_spec] * 4
        + [pl.BlockSpec(act.shape, lambda i: (0, 0), pipeline_mode=pl.Buffered(1))],
        out_specs=pl.BlockSpec((tile, 3 * cols), lambda i: (i, 0)),
        compiler_params=pltpu.CompilerParams(vmem_limit_bytes=VMEM_LIMIT),
        cost_estimate=SMALL,
    )(*mid_halves, *cot_halves, act)


def slice_moves(n_plane, chunks, cols, total):
    for device in range(n_plane):
        for chunk in range(chunks):
            start = (device * chunks + chunk) * cols
            for kind in range(3):
                yield device, chunk, kind, kind * total + start, max(0, min(cols, total - start))


def pack_kernel(moves, cols, w_ref, out_ref):
    rows = w_ref.shape[0]
    for device, chunk, kind, source, real in moves:
        there = slice(device * rows, (device + 1) * rows)
        at = (chunk * 3 + kind) * cols
        if real:
            out_ref[there, at : at + real] = w_ref[:, source : source + real]
        if real < cols:
            out_ref[there, at + real : at + cols] = jnp.zeros((rows, cols - real), BF16)


def unpack_kernel(moves, cols, *refs):
    in_refs, out_ref = refs[:-1], refs[-1]
    rows = out_ref.shape[0]
    for device, chunk, kind, source, real in moves:
        if real:
            which = min(chunk, len(in_refs) - 1)
            at = ((chunk - which) * 3 + kind) * cols
            block = in_refs[which][device * rows : (device + 1) * rows, at : at + real]
            out_ref[:, source : source + real] = block.astype(F32)


def pack_slices(w_mlp, n_plane, chunks, cols):
    rows, total = w_mlp.shape[0], w_mlp.shape[1] // 3
    if rows % 16:
        wide = jnp.pad(
            w_mlp.reshape(rows, 3, total), ((0, 0), (0, 0), (0, n_plane * chunks * cols - total))
        )
        wide = wide.reshape(rows, 3, n_plane, chunks, cols).transpose(2, 0, 3, 1, 4)
        return wide.reshape(n_plane * rows, 3 * chunks * cols)
    moves = list(slice_moves(n_plane, chunks, cols, total))
    return pl.pallas_call(
        functools.partial(pack_kernel, moves, cols),
        out_shape=jax.ShapeDtypeStruct((n_plane * rows, 3 * chunks * cols), BF16),
        in_specs=vmem_specs(1),
        out_specs=vmem_specs(1)[0],
        compiler_params=pltpu.CompilerParams(vmem_limit_bytes=VMEM_LIMIT),
        cost_estimate=SMALL,
    )(w_mlp)


def unpack_slices(arrays, rows, total, n_plane, chunks, cols):
    if rows % 16:
        wide = jnp.concatenate(arrays, axis=1).reshape(n_plane, rows, chunks, 3, cols)
        wide = wide.transpose(1, 3, 0, 2, 4).reshape(rows, 3, -1)[:, :, :total]
        return wide.reshape(rows, 3 * total).astype(F32)
    moves = list(slice_moves(n_plane, chunks, cols, total))
    return pl.pallas_call(
        functools.partial(unpack_kernel, moves, cols),
        out_shape=jax.ShapeDtypeStruct((rows, 3 * total), F32),
        in_specs=vmem_specs(len(arrays)),
        out_specs=vmem_specs(1)[0],
        compiler_params=pltpu.CompilerParams(vmem_limit_bytes=VMEM_LIMIT),
        cost_estimate=SMALL,
    )(*arrays)


def weight_grad_kernel(n_dp, local_rows, across, dev_ref, *refs):
    count = len(across)
    lefts, rights = refs[: 2 * count : 2], refs[1 : 2 * count : 2]
    sides, (near_ref, far_ref, turned_ref, block_ref) = refs[2 * count : -4], refs[-4:]
    half = near_ref.shape[0] // (n_dp * local_rows)
    tile = block_ref.shape[1]

    def move(from_ref, at):
        cols = slice(at, at + from_ref.shape[1])
        for slot in range(2 * half):
            out_ref = near_ref if slot < half else far_ref
            for zone in range(n_dp):
                source = (zone * 2 * half + dev_ref[slot]) * local_rows
                source = pl.ds(pl.multiple_of(source, local_rows), local_rows)
                there = ((slot % half) * n_dp + zone) * local_rows
                out_ref[there : there + local_rows, cols] = from_ref[source, :]

    at = 0
    for left, right, is_across in zip(lefts, rights, across):
        turned_ref[...] = left[...].T
        cols = right.shape[0] if is_across else right.shape[1]
        for start in range(0, cols, tile):
            span = slice(start, start + tile)
            if is_across:
                block = dot(turned_ref[...], right[span, :], 1, 1)
            else:
                block = dot(turned_ref[...], right[:, span], 1, 0)
            block_ref[...] = block.astype(BF16)
            move(block_ref, at)
            at += tile
    for side_ref in sides:
        move(side_ref, at)


def weight_grads(plane, local_rows, terms, side=None):
    n_dp = lax.axis_size("dp")
    tokens, width = terms[0][0].shape
    widths = [right.shape[0 if across else 1] for _, right, across in terms]
    if local_rows % 16:
        full = jnp.concatenate(
            [dot(left, right, 0, 1 if across else 0) for left, right, across in terms], axis=1
        ).astype(BF16)
        if side is not None:
            full = jnp.concatenate([full, side], axis=1)
        full = full.reshape(n_dp, plane.count, local_rows, full.shape[1])
        blocks = [
            lax.dynamic_slice_in_dim(full, device, 1, 1).reshape(n_dp * local_rows, -1)
            for device in plane.devices
        ]
        half = plane.count // 2
        return jnp.concatenate(blocks[:half]), jnp.concatenate(blocks[half:])
    tile = 512
    extra = [] if side is None else [side]
    total = sum(widths) + sum(array.shape[1] for array in extra)
    shape = jax.ShapeDtypeStruct((width // 2, total), BF16)
    return pl.pallas_call(
        functools.partial(weight_grad_kernel, n_dp, local_rows, [term[2] for term in terms]),
        out_shape=(shape, shape),
        in_specs=[pl.BlockSpec(memory_space=pltpu.SMEM)]
        + vmem_specs(2 * len(terms) + len(extra)),
        out_specs=tuple(vmem_specs(2)),
        scratch_shapes=[pltpu.VMEM((width, tokens), BF16), pltpu.VMEM((width, tile), BF16)],
        compiler_params=pltpu.CompilerParams(vmem_limit_bytes=VMEM_LIMIT),
        cost_estimate=SMALL,
    )(jnp.stack(plane.devices), *[array for term in terms for array in term[:2]], *extra)


def spread_kernel(q_width, width, kv_cols, sum_ref, qkv_ref, out_ref, *side_refs):
    qkv_ref[:, :q_width] = sum_ref[:, :q_width].astype(F32)
    at = q_width + width
    qkv_ref[:, q_width:] = sum_ref[:, at : at + kv_cols].astype(F32)
    out_ref[...] = sum_ref[:, q_width:at].astype(F32)
    sides = sum_ref[:16, at + kv_cols :].astype(F32)
    for row, side_ref in enumerate(side_refs):
        side_ref[...] = sides[row : row + 1, : side_ref.shape[1]]


def spread_sums(attn_sum, q_width, width, kv_cols, sizes):
    rows = attn_sum.shape[0]
    at = q_width + width
    if rows % 16:
        full = attn_sum.astype(F32)
        grad_qkv = jnp.concatenate([full[:, :q_width], full[:, at : at + kv_cols]], axis=1)
        sides = [full[row, at + kv_cols : at + kv_cols + size] for row, size in enumerate(sizes)]
        return grad_qkv, full[:, q_width:at].T, *sides
    grad_qkv, grad_out, *sides = pl.pallas_call(
        functools.partial(spread_kernel, q_width, width, kv_cols),
        out_shape=(
            jax.ShapeDtypeStruct((rows, q_width + kv_cols), F32),
            jax.ShapeDtypeStruct((rows, width), F32),
            *(jax.ShapeDtypeStruct((1, size), F32) for size in sizes),
        ),
        in_specs=vmem_specs(1),
        out_specs=tuple(vmem_specs(2 + len(sizes))),
        compiler_params=pltpu.CompilerParams(vmem_limit_bytes=VMEM_LIMIT),
        cost_estimate=SMALL,
    )(attn_sum)
    return grad_qkv, grad_out.T, *(side.reshape(-1) for side in sides)


def after(array, *others):
    return lax.optimization_barrier((array, *others))[0]


class Plane:
    def __init__(self):
        ctx, uly = lax.axis_size("ctx"), lax.axis_size("uly")
        self.count = ctx * uly
        assert self.count & (self.count - 1) == 0 and ctx % 2 == 0
        self.me = lax.axis_index("ctx") * uly + lax.axis_index("uly")
        self.core = uly
        near = [1 << i for i in range(uly.bit_length() - 1)]
        far = [self.core << i for i in range(1, (ctx // 2).bit_length())]
        self.orders = (far + near, near + far)
        self.steps = len(near) + len(far)
        mine = (self.me // self.core) % 2 == 0
        masks = [[0], [0]]
        for which in (0, 1):
            for bit in self.orders[which]:
                masks[which] += [bit | mask for mask in masks[which]]
        pairs = list(zip(masks[0], masks[1]))
        near_slots = [jnp.where(mine, a, b) for a, b in pairs]
        far_slots = [jnp.where(mine, b, a) | self.core for a, b in pairs]
        self.devices = [self.me ^ mask for mask in near_slots + far_slots]

    def swap(self, array, step):
        pairs = []
        for i in range(self.count):
            if step == self.steps:
                bit = self.core
            else:
                bit = self.orders[(i // self.core) % 2][step]
            pairs.append((i, i ^ bit))
        return lax.ppermute(array, PLANE, pairs)

    def widen(self, rows, step, *others):
        moved = self.swap(rows, step)
        return jnp.concatenate([after(rows, *others) if others else rows, moved], axis=0)

    def gather(self, rows, late_step=None, *others):
        stages = [rows]
        for step in range(self.steps):
            if step == late_step:
                stages[-1] = after(stages[-1], *others)
            stages.append(self.widen(stages[-1], step))
        return stages + [self.swap(stages[-1], self.steps)]

    def fold(self, near, far, step):
        return (near.astype(F32) + self.swap(far, step).astype(F32)).astype(BF16)

    def fold_rest(self, rows, step):
        half = rows.shape[0] // 2
        return self.fold(rows[:half], rows[half:], step)


def place_info(spans, row_in_span, length_row):
    places = spans * TOK_DEV + row_in_span
    begins = jnp.zeros_like(places)
    end = jnp.int32(0)
    for doc in range(length_row.shape[0]):
        end = end + length_row[doc]
        begins = jnp.where(places >= end, jnp.maximum(begins, end), begins)
    return places, begins


def inverse_rms(values):
    return lax.rsqrt(jnp.mean(values * values, axis=-1, keepdims=True) + NORM_EPS)


def norm_backward(values, inverse, scaled):
    return inverse * scaled - values * (
        inverse**3 * jnp.mean(scaled * values, axis=-1, keepdims=True)
    )


def turn(heads, cosine, sine):
    half = HEAD // 2
    first, second = heads[..., :half], heads[..., half:]
    return jnp.concatenate(
        [first * cosine - second * sine, second * cosine + first * sine], axis=-1
    )


def shards(
    layer_input,
    span_order,
    doc_lengths,
    pad_mask,
    w_qkv,
    b_qkv,
    w_out,
    norm_gain_attn,
    norm_gain_mlp,
    w_mlp,
    cotangent,
):
    tok_rows, width = layer_input.shape
    n_dp = lax.axis_size("dp")
    n_plane = lax.axis_size("ctx") * lax.axis_size("uly")
    n_all = n_dp * n_plane
    plane = Plane()
    ffn_width = w_mlp.shape[1] // 3
    local_rows = w_mlp.shape[0]
    zone = local_rows * n_plane
    q_width, kv_width = HEADS * HEAD, KV_HEADS * HEAD
    qkv_width = q_width + 2 * kv_width
    bias_rows = b_qkv.shape[0]
    slice_tiles = -(-(ffn_width // LANES) // n_plane)
    chunks = max(c for c in (1, 2, 3) if slice_tiles % c == 0)
    chunk_cols = slice_tiles // chunks * LANES
    kv_cols = 2 * kv_width + LANES

    def swap_rows(array):
        return lax.all_to_all(array, PLANE, split_axis=0, concat_axis=0, tiled=True)

    def zone_gather(array):
        return lax.all_gather(array, "dp", axis=0, tiled=True)

    def zone_sum(array):
        return lax.psum_scatter(array, "dp", scatter_dimension=0, tiled=True)

    def whole_rows(pieces):
        cols = pieces[0].shape[1]
        full = jnp.zeros((n_dp, n_plane, local_rows, cols), BF16)
        slots = [block for piece in pieces for block in jnp.split(piece, n_plane // 2)]
        for device, block in zip(plane.devices, slots):
            piece = block.reshape(n_dp, 1, local_rows, cols)
            full = lax.dynamic_update_slice(full, piece, (0, device, 0, 0))
        return full.reshape(n_all * local_rows, cols)

    def device_blocks(array):
        cols = array.shape[1]
        full = array.reshape(n_dp, n_plane, local_rows, cols)
        return [
            lax.dynamic_slice_in_dim(full, device, 1, 1).reshape(n_dp * local_rows, cols)
            for device in plane.devices
        ]

    side = jnp.concatenate(
        [
            norm_gain_attn[:, None],
            norm_gain_mlp[:, None],
            jnp.zeros((local_rows, 62), BF16),
            jnp.pad(b_qkv[None, :], ((0, local_rows - 1), (0, 64 - bias_rows))),
        ],
        axis=1,
    )
    my_dp = lax.axis_index("dp")

    def zone_rows(array):
        full = jnp.zeros((n_dp, *array.shape), BF16)
        for step in range(n_dp):
            moved = array
            if step:
                moved = lax.ppermute(array, "dp", [(i, (i + step) % n_dp) for i in range(n_dp)])
            full = lax.dynamic_update_slice(
                full, moved[None], ((my_dp + n_dp - step) % n_dp, 0, 0)
            )
        return full.reshape(n_dp * array.shape[0], array.shape[1])

    kv_local = jnp.concatenate([w_qkv[:, q_width:], side], axis=1)
    attn_local = jnp.concatenate([kv_local, w_qkv[:, :q_width], w_out.T], axis=1)
    attn_zone = zone_rows(attn_local)
    kv_zone = attn_zone[:, : kv_local.shape[1]]
    big_zone = attn_zone[:, kv_local.shape[1] :]

    packed = pack_slices(after(w_mlp, attn_local), n_plane, chunks, chunk_cols)
    chunk_width = 3 * chunk_cols
    mlp_zone = swap_rows(packed)
    mlp_weights = [
        zone_gather(mlp_zone[:, chunk * chunk_width : (chunk + 1) * chunk_width])
        for chunk in range(chunks)
    ]

    w_kv_stages = plane.gather(kv_zone, 1, mlp_zone)
    w_q_stages = plane.gather(after(big_zone[:, :q_width], w_kv_stages[1]))
    w_out_near = after(big_zone[:, q_width:], w_q_stages[-2])
    w_out_near = plane.widen(w_out_near, 0)

    order_row, length_row, mask_row = after(
        (span_order[0], doc_lengths[0], pad_mask[0]), packed
    )
    row_in_span = jnp.arange(tok_rows, dtype=jnp.int32)
    stored_block = jnp.stack(plane.devices)
    spans = order_row[stored_block]
    own_place, own_begin = place_info(spans[0], row_in_span, length_row)
    flags = mask_row.reshape(n_plane, tok_rows)[stored_block]
    key_place = spans[:, None] * TOK_DEV + row_in_span[None, :]
    kinfo = jnp.stack(
        [jnp.where(flags == 1, key_place, FAR).reshape(-1), key_place.reshape(-1)], axis=1
    )
    qinfo = jnp.concatenate(
        [
            own_place[None],
            own_begin[None],
            flags[0][None],
            jnp.zeros((5, tok_rows), jnp.int32),
        ],
        axis=0,
    )
    need = ((spans <= spans[0]) & ((spans + 1) * TOK_DEV > own_begin[0])).astype(jnp.int32)

    inner = (own_place - own_begin).astype(F32)
    half = HEAD // 2
    frequency = ROPE_BASE ** (-(jnp.arange(half, dtype=F32) * 2.0) / HEAD)
    angles_t = frequency[:, None] * inner[None, :]
    cos_t, sin_t = jnp.cos(angles_t), jnp.sin(angles_t)
    cos_r, sin_r = cos_t.T[:, None, :], sin_t.T[:, None, :]

    w_kv_all = whole_rows(w_kv_stages[-2:])
    side_all = w_kv_all[:, 2 * kv_width :].astype(F32)
    gain_attn = side_all[:, 0]
    gain_mlp = side_all[:, 1]
    bias_all = side_all.reshape(n_all, local_rows, LANES)[:, 0, 64 : 64 + bias_rows].reshape(-1)

    inputs = layer_input.astype(F32)
    in_inverse = inverse_rms(inputs)
    normed_in = (inputs * in_inverse * gain_attn).astype(BF16)

    kv_proj = dot(normed_in, w_kv_all[:, : 2 * kv_width], 1, 0) + bias_all[q_width:]
    key_own = turn(kv_proj[:, :kv_width].reshape(tok_rows, KV_HEADS, HEAD), cos_r, sin_r)
    kv_own = jnp.concatenate([key_own.reshape(tok_rows, kv_width), kv_proj[:, kv_width:]], axis=1)
    kv_own = after(kv_own.astype(BF16), w_q_stages[-2])
    kv_stages = plane.gather(kv_own, 1, w_out_near)
    kv_all = jnp.concatenate(kv_stages[-2:], axis=0)
    w_q_all = whole_rows(w_q_stages[-2:])

    q_proj = dot(w_q_all, normed_in, 0, 1) + bias_all[:q_width, None]
    q_heads = q_proj.reshape(HEADS, 2, half, tok_rows)
    q_first, q_second = q_heads[:, 0], q_heads[:, 1]
    query_t = (
        jnp.stack(
            [q_first * cos_t - q_second * sin_t, q_second * cos_t + q_first * sin_t], axis=1
        )
        .reshape(q_width, tok_rows)
        .astype(BF16)
    )
    cot_near = plane.widen(after(cotangent, kv_stages[-2]), 0)
    need = after(need, w_out_near, cot_near)
    attended_t, lse = attention_forward(need, kinfo, qinfo, query_t, kv_all)
    for step in range(1, plane.steps):
        w_out_near = plane.widen(after(w_out_near, kv_stages[-2]), step, attended_t)
    w_out_all = whole_rows([w_out_near, plane.swap(w_out_near, plane.steps)])
    for step in range(1, plane.steps):
        cot_near = plane.widen(cot_near, step, attended_t)
    attended_t = after(attended_t, cot_near)

    middle = inputs + dot(attended_t, w_out_all, 0, 1)
    mid_inverse = inverse_rms(middle)
    normed_mid = (middle * mid_inverse * gain_mlp).astype(BF16)

    mid_near = normed_mid
    for step in range(plane.steps):
        mid_near = plane.widen(mid_near, step)
    cot_halves = cot_near, plane.swap(cot_near, plane.steps)
    mid_near = after(mid_near, mlp_weights[0])
    mid_halves = mid_near, plane.swap(mid_near, plane.steps)
    sums, chunk_grads = (), []
    if chunks > 1:
        *sums, chunk_grads = split_at(
            feed_forward(mid_halves, cot_halves, mlp_weights[:-1], (), True), 4
        )
    *sums, (extra,) = split_at(
        feed_forward(mid_halves, cot_halves, mlp_weights[-1:], tuple(sums), False), 4
    )

    def token_blocks(array):
        return [array[k * tok_rows : (k + 1) * tok_rows] for k in range(n_plane)]

    chunk_sums = [zone_sum(grad) for grad in chunk_grads]
    mid_fold = plane.fold(sums[0], sums[1], plane.steps)
    chunk_grads.append(feed_forward_grad(mid_halves, cot_halves, after(extra, mid_fold)))
    chunk_sums.append(zone_sum(chunk_grads[-1]))
    for step in range(plane.steps - 1, -1, -1):
        half = mid_fold.shape[0] // 2
        kept, sent = mid_fold[:half], mid_fold[half:]
        if step == plane.steps - 1:
            kept = after(kept, chunk_grads[-1])
        mid_fold = plane.fold(kept, sent, step)
        if step == 0:
            out_fold = plane.fold(after(sums[2], kept), sums[3], plane.steps)
    mid_grad = after(mid_fold, *chunk_sums[:-1][:1]).astype(F32)

    out_grad = cotangent.astype(F32)
    gain_mlp_grad = jnp.sum(mid_grad * (middle * mid_inverse), axis=0)
    middle_grad = out_grad + norm_backward(middle, mid_inverse, mid_grad * gain_mlp)
    middle_low = middle_grad.astype(BF16)
    attended_grad_t = dot(w_out_all, middle_low, 0, 1).astype(BF16)
    attended_grad_t = after(attended_grad_t, out_fold)
    query_grad, *kv_grads = attention_backward(
        need, kinfo, qinfo, cos_t, sin_t, query_t, kv_all, attended_t, attended_grad_t, lse
    )
    kv_fold = plane.fold(*kv_grads, plane.steps)
    mlp_out = after(out_fold, mid_fold)
    for step in range(plane.steps - 1, 0, -1):
        mlp_out = plane.fold_rest(mlp_out, step)
    big_grads = weight_grads(
        plane,
        local_rows,
        [
            (after(normed_in, mlp_out, kv_fold), query_grad, False),
            (middle_low, attended_t, True),
        ],
    )
    big_fold = plane.fold(*big_grads, plane.steps)
    mlp_out = plane.fold_rest(after(mlp_out, kv_fold), 0)
    for step in range(plane.steps - 1, -1, -1):
        rows = kv_fold.shape[0] // 2
        kept, sent = kv_fold[:rows], kv_fold[rows:]
        if step == plane.steps - 1:
            kept = after(kept, big_fold, *chunk_sums[1:-1])
        kv_fold = plane.fold(kept, sent, step)
    kv_back = after(kv_fold, mlp_out)
    kv_back = kv_back.astype(F32)
    key_back = turn(kv_back[:, :kv_width].reshape(tok_rows, KV_HEADS, HEAD), cos_r, -sin_r)
    projected_grad = jnp.concatenate(
        [query_grad, key_back.reshape(tok_rows, kv_width).astype(BF16), kv_back[:, kv_width:].astype(BF16)],
        axis=1,
    )
    in_grad = dot(projected_grad[:, :q_width], w_q_all, 1, 1) + dot(
        projected_grad[:, q_width:], w_kv_all[:, : 2 * kv_width], 1, 1
    )
    first_swapped = [swap_rows(after(array, in_grad)) for array in chunk_sums[:-1][:1]]
    gain_attn_grad = jnp.sum(in_grad * (inputs * in_inverse), axis=0)
    input_grad = middle_grad + norm_backward(inputs, in_inverse, in_grad * gain_attn)
    qkv_bias_grad = jnp.sum(projected_grad.astype(F32), axis=0)

    def side_rows(array):
        array = array.reshape(n_dp, n_plane, 1, -1)
        return jnp.pad(array, ((0, 0), (0, 0), (0, 0), (0, LANES - array.shape[-1])))

    side_grad = jnp.concatenate(
        [side_rows(gain_attn_grad), side_rows(gain_mlp_grad), side_rows(qkv_bias_grad)]
        + [jnp.zeros((n_dp, n_plane, 1, LANES), F32)] * 5,
        axis=2,
    )
    side_grad = jnp.pad(side_grad, ((0, 0), (0, 0), (0, local_rows - 8), (0, 0)))
    side_grad = side_grad.reshape(n_all * local_rows, LANES).astype(BF16)
    for step in range(plane.steps - 1, 0, -1):
        big_fold = plane.fold_rest(big_fold, step)
    small_grads = weight_grads(
        plane,
        local_rows,
        [(after(normed_in, big_fold), projected_grad[:, q_width:], False)],
        side_grad,
    )
    big_fold = plane.fold_rest(big_fold, 0)
    small_fold = plane.fold(*small_grads, plane.steps)
    for step in range(plane.steps - 1, -1, -1):
        rows = small_fold.shape[0] // 2
        kept, sent = small_fold[:rows], small_fold[rows:]
        if step == 0:
            kept = after(kept, chunk_sums[-1], *first_swapped)
        small_fold = plane.fold(kept, sent, step)
    attn_plane = jnp.concatenate([big_fold, small_fold], axis=1)
    grad_qkv, grad_out, grad_gain_attn, grad_gain_mlp, grad_bias = spread_sums(
        zone_sum(attn_plane), q_width, width, 2 * kv_width, (local_rows, local_rows, bias_rows)
    )

    late_sums = jnp.concatenate(chunk_sums[len(first_swapped) :], axis=1)
    swapped = first_swapped + [swap_rows(after(late_sums, attn_plane))]
    grad_mlp = unpack_slices(swapped, local_rows, ffn_width, n_plane, chunks, chunk_cols)
    block_output = (middle + mlp_out.astype(F32)).astype(BF16)
    return (
        block_output,
        input_grad,
        grad_qkv,
        grad_bias,
        grad_out,
        grad_gain_attn,
        grad_gain_mlp,
        grad_mlp,
    )


def solution(mesh):
    rows = P(EVERY, None)
    flat = P(EVERY)
    columns = P(None, EVERY)
    batch = P("dp", None)
    return jax.shard_map(
        shards,
        mesh=mesh,
        in_specs=(rows, batch, batch, batch, rows, flat, columns, flat, flat, rows, rows),
        out_specs=(rows, rows, rows, flat, columns, flat, flat, rows),
        check_vma=False,
    )
```

profile of v0, /device:TPU:0, one launch (start us, length us, event | category | flops | bytes accessed | tf_op | source)
XLA Modules:
  0.0 542.9 jit_solution(13687520856987421036)
XLA Ops:
  12.8 5.0 collective-permute-start.2
  18.9 3.5 shard_map.170
  22.4 3.9 all-to-all-start
  38.0 4.1 collective-permute-done
  43.1 5.5 %collective-permute-done.1 = bf16[48,3712]{1,0:T(8,128)(2,1)} collective-permute-done((bf16[48,3712]{1,0:T(8,128)(2,1)}, bf16[48,3712]{1,0:T(8,128)(2,1)}, u32[]{:S(2)}, u32[]{:S(2)}) %collective-permute-start.1) | collective-permute-done | bytes 356384 | tf_op jit(solution)/shard_map/ppermute | solution.py:656
  53.2 4.8 all-to-all-done
  64.3 11.4 %collective-permute-done.7 = bf16[384,640]{1,0:T(8,128)(2,1)S(1)} collective-permute-done((bf16[384,640]{1,0:T(8,128)(2,1)S(1)}, bf16[384,640]{1,0:T(8,128)(2,1)S(1)}, u32[]{:S(2)}, u32[]{:S(2)}) %collective-permute-start.7) | collective-permute-done | bytes 491552 | tf_op jit(solution)/shard_map/ppermute | solution.py:535
  86.5 7.7 %collective-permute-done.5 = bf16[384,1536]{1,0:T(8,128)(2,1)} collective-permute-done((bf16[384,1536]{1,0:T(8,128)(2,1)}, bf16[384,1536]{1,0:T(8,128)(2,1)}, u32[]{:S(2)}, u32[]{:S(2)}) %collective-permute-start.5) | collective-permute-done | bytes 1179680 | tf_op jit(solution)/shard_map/ppermute | solution.py:535
  105.1 4.5 collective-permute-done.6
  116.7 3.5 collective-permute-done.10
  124.9 15.1 %collective-permute-done.11 = bf16[256,1536]{1,0:T(8,128)(2,1)S(1)} collective-permute-done((bf16[256,1536]{1,0:T(8,128)(2,1)S(1)}, bf16[256,1536]{1,0:T(8,128)(2,1)S(1)}, u32[]{:S(2)}, u32[]{:S(2)}) %collective-permute-start.11) | collective-permute-done | bytes 786464 | tf_op jit(solution)/shard_map/ppermute | solution.py:535
  148.4 6.9 %shard_map.171 = (bf16[1536,256]{1,0:T(8,128)(2,1)}, f32[16,256]{1,0:T(8,128)}) custom-call(s32[8]{0:T(128)} %and_convert_fusion.need_ref, s32[2048,2]{1,0:T(8,128)} %copy.31.kinfo_ref, s32[8,256]{1,0:T(8,128)} %add_add_fusion.qinfo_ref, bf16[1536,256]{1,0:T(8,128)(2,1)} %bitcast.118, bf16[2048,512]{1,0:T(8,128)(2,1)} %copy-done.7), custom_call_target="tpu_custom_call" | custom-call | flops 1024 | bytes 1024 | tf_op jit(solution)/shard_map/pallas_call | solution.py:175
  155.4 4.5 collective-permute-start.16
  169.3 6.5 %collective-permute-start.17 = (bf16[256,1536]{1,0:T(8,128)(2,1)S(1)}, bf16[256,1536]{1,0:T(8,128)(2,1)S(1)}, u32[]{:S(2)}, u32[]{:S(2)}) collective-permute-start(bf16[256,1536]{1,0:T(8,128)(2,1)S(1)} %multiply_convert_fusion), channel_id=1, source_target_pairs={{0,4},{1,5},{2,3},{3,2},{4,0},{5,1},{6,7},{7,6},{8,12},{9,13},{10,... | collective-permute-start | bytes 2359304 | tf_op jit(solution)/shard_map/ppermute | solution.py:535
  175.8 9.9 %collective-permute-done.17 = bf16[256,1536]{1,0:T(8,128)(2,1)S(1)} collective-permute-done((bf16[256,1536]{1,0:T(8,128)(2,1)S(1)}, bf16[256,1536]{1,0:T(8,128)(2,1)S(1)}, u32[]{:S(2)}, u32[]{:S(2)}) %collective-permute-start.17) | collective-permute-done | bytes 786464 | tf_op jit(solution)/shard_map/ppermute | solution.py:535
  185.8 5.3 collective-permute-start.18
  191.2 18.4 %collective-permute-done.18 = bf16[512,1536]{1,0:T(8,128)(2,1)S(1)} collective-permute-done((bf16[512,1536]{1,0:T(8,128)(2,1)S(1)}, bf16[512,1536]{1,0:T(8,128)(2,1)S(1)}, u32[]{:S(2)}, u32[]{:S(2)}) %collective-permute-start.18) | collective-permute-done | bytes 1572896 | tf_op jit(solution)/shard_map/ppermute | solution.py:535
  211.3 5.7 %collective-permute-done.19.refs_1_.mid_far = bf16[1024,1536]{1,0:T(8,128)(2,1)} collective-permute-done((bf16[1024,1536]{1,0:T(8,128)(2,1)S(1)}, bf16[1024,1536]{1,0:T(8,128)(2,1)}, u32[]{:S(2)}, u32[]{:S(2)}) %collective-permute-start.19) | collective-permute-done | bytes 3145760 | tf_op jit(solution)/shard_map/ppermute | solution.py:535
  217.0 61.3 %shard_map.172 = (bf16[1024,1536]{1,0:T(8,128)(2,1)}, bf16[1024,1536]{1,0:T(8,128)(2,1)}, bf16[1024,1536]{1,0:T(8,128)(2,1)}, bf16[1024,1536]{1,0:T(8,128)(2,1)}...) custom-call(bf16[1024,1536]{1,0:T(8,128)(2,1)} %copy-done.2, ...), custom_call_target="tpu_custom_call" | custom-call | flops 1024 | bytes 1024 | tf_op jit(solution)/shard_map/pallas_call | solution.py:291
  278.5 25.3 %shard_map.173 = (bf16[1024,1536]{1,0:T(8,128)(2,1)}, bf16[1024,1536]{1,0:T(8,128)(2,1)}, bf16[1024,1536]{1,0:T(8,128)(2,1)}, bf16[1024,1536]{1,0:T(8,128)(2,1)}, bf16[2048,1152]{1,0:T(8,128)(2,1)}) custom-call(bf16[1024,1536]{1,0:T(8,128)(2,1)} %copy-done.2, bf16[1024,1536]{1,0:T(8,128)(2,1)} %collective-permute-done.19.refs_1_.mid_far, ...), custom_call_target="tpu_custom_call" | custom-call | flops 1024 | bytes 1024 | tf_op jit(solution)/shard_map/pallas_call | solution.py:291
  304.3 7.4 %collective-permute-done.21 = bf16[1024,1536]{1,0:T(8,128)(2,1)S(1)} collective-permute-done((bf16[1024,1536]{1,0:T(8,128)(2,1)}, bf16[1024,1536]{1,0:T(8,128)(2,1)S(1)}, u32[]{:S(2)}, u32[]{:S(2)}) %collective-permute-start.21) | collective-permute-done | bytes 3145760 | tf_op jit(solution)/shard_map/ppermute | solution.py:535
  311.7 2.9 add_convert_fusion.2
  316.0 3.3 collective-permute-start.22
  319.3 13.9 %shard_map.174 = bf16[1536,1152]{1,0:T(8,128)(2,1)} custom-call(bf16[1024,1536]{1,0:T(8,128)(2,1)} %copy-done.2, bf16[1024,1536]{1,0:T(8,128)(2,1)} %collective-permute-done.19.refs_1_.mid_far, bf16[1024,1536]{1,0:T(8,128)(2,1)} %constant_dynamic-update-slice_fusion.12.refs_2_.cot_near, bf16[1024,1536]{1,0:T(8,128)(2,1)} %collective-permute-done.20.refs_3_.cot_far, ...), custom_call_target="tpu_custom_call" | custom-call | flops 1024 | bytes 1024 | tf_op jit(solution)/shard_map/pallas_call | solution.py:325
  333.2 4.6 collective-permute-done.22
  342.5 3.7 add_convert_fusion.1
  346.2 6.0 %collective-permute-done.24 = bf16[256,1536]{1,0:T(8,128)(2,1)S(1)} collective-permute-done((bf16[256,1536]{1,0:T(8,128)(2,1)S(1)}, bf16[256,1536]{1,0:T(8,128)(2,1)S(1)}, u32[]{:S(2)}, u32[]{:S(2)}) %collective-permute-start.24) | collective-permute-done | bytes 786464 | tf_op jit(solution)/shard_map/ppermute | solution.py:535
  356.7 4.9 convolution_convert_fusion.do_ref
  361.6 9.0 %shard_map.175 = (bf16[256,1536]{1,0:T(8,128)(2,1)}, bf16[1024,512]{1,0:T(8,128)(2,1)}, bf16[1024,512]{1,0:T(8,128)(2,1)}) custom-call(s32[8]{0:T(128)} %and_convert_fusion.need_ref, s32[2048,2]{1,0:T(8,128)} %copy.31.kinfo_ref, s32[8,256]{1,0:T(8,128)} %add_add_fusion.qinfo_ref, f32[64,256]{1,0:T(8,128)} %copy-done.38, ...), custom_call_target="tpu_custom_call" | custom-call | flops 1024 | bytes 1024 | tf_op jit(solution)/shard_map/pallas_call | solution.py:196
  370.6 5.8 %collective-permute-start.26 = (bf16[1024,512]{1,0:T(8,128)(2,1)}, bf16[1024,512]{1,0:T(8,128)(2,1)}, u32[]{:S(2)}, u32[]{:S(2)}) collective-permute-start(bf16[1024,512]{1,0:T(8,128)(2,1)} %get-tuple-element.98), channel_id=1, source_target_pairs={{0,2},{1,3},{2,0},{3,1},{4,6},{5,7},{6,4},{7,5},{8,10},{9,11},{10,... | collective-permute-start | bytes 3145736 | tf_op jit(solution)/shard_map/ppermute | solution.py:535
  377.0 3.5 add_convert_fusion.4
  383.1 9.0 %shard_map.176 = (bf16[768,3072]{1,0:T(8,128)(2,1)}, bf16[768,3072]{1,0:T(8,128)(2,1)}) custom-call(s32[8]{0:T(128)} %stack.91.dev_ref, bf16[256,1536]{1,0:T(8,128)(2,1)} %copy-done.18, bf16[256,1536]{1,0:T(8,128)(2,1)} %get-tuple-element.100.refs_1_, bf16[256,1536]{1,0:T(8,128)(2,1)} %copy-done.31, bf16[1536,256]{1,0:T(8,128)(2,1)} %get-tuple-element.76.o_ref.refs_3_), custom_call_target="tpu_custom_call" | custom-call | flops 1024 | bytes 1024 | tf_op jit(solution)/shard_map/pallas_call | solution.py:457
  395.8 2.7 collective-permute-start.29
  399.4 9.5 %collective-permute-start.27 = (bf16[256,1536]{1,0:T(8,128)(2,1)}, bf16[256,1536]{1,0:T(8,128)(2,1)}, u32[]{:S(2)}, u32[]{:S(2)}) collective-permute-start(bf16[256,1536]{1,0:T(8,128)(2,1)} %slice.199), channel_id=1, source_target_pairs={{0,4},{1,5},{2,3},{3,2},{4,0},{5,1},{6,7},{7,6},{8,12},{9,13},{10,... | collective-permute-start | bytes 2359304 | tf_op jit(solution)/shard_map/ppermute | solution.py:535
  408.9 5.8 %add_convert_fusion = bf16[768,3072]{1,0:T(8,128)(2,1)S(1)} fusion(bf16[768,3072]{1,0:T(8,128)(2,1)} %collective-permute-done.28, bf16[768,3072]{1,0:T(8,128)(2,1)} %get-tuple-element.102), kind=kLoop, calls=%fused_computation.2 | loop fusion | flops 9437184 | bytes 14155776 | tf_op jit(solution)/shard_map/convert_element_type | solution.py:550
  434.7 5.0 fusion.5
  442.8 8.8 %collective-permute-done.31 = bf16[384,3072]{1,0:T(8,128)(2,1)} collective-permute-done((bf16[384,3072]{1,0:T(8,128)(2,1)}, bf16[384,3072]{1,0:T(8,128)(2,1)}, u32[]{:S(2)}, u32[]{:S(2)}) %collective-permute-start.31) | collective-permute-done | bytes 2359328 | tf_op jit(solution)/shard_map/ppermute | solution.py:535
  451.6 3.3 add_convert_fusion.3
  454.9 4.4 shard_map.177
  465.6 4.2 all-to-all-start.1
  469.9 9.1 %collective-permute-done.34 = bf16[384,640]{1,0:T(8,128)(2,1)} collective-permute-done((bf16[384,640]{1,0:T(8,128)(2,1)}, bf16[384,640]{1,0:T(8,128)(2,1)}, u32[]{:S(2)}, u32[]{:S(2)}) %collective-permute-start.34) | collective-permute-done | bytes 491552 | tf_op jit(solution)/shard_map/ppermute | solution.py:535
  482.6 4.9 collective-permute-done.32
  492.3 2.6 collective-permute-done.35
  498.4 2.8 pad_maximum_fusion.2
  501.2 4.5 all-to-all-start.2
  505.7 3.7 fusion.13
  509.5 18.5 %all-to-all-done.2 = bf16[8,48,2304]{2,1,0:T(8,128)(2,1)} async-done(((bf16[8,48,2304]{2,1,0:T(8,128)(2,1)}), bf16[8,48,2304]{2,1,0:T(8,128)(2,1)}, u32[]{:S(2)}, u32[]{:S(2)}) %all-to-all-start.2) | async-done | bytes 1769504 | tf_op jit(solution)/shard_map/all_to_all | solution.py:615
  528.0 4.4 shard_map.179
  (343 shorter events, 143.4 us)
Async XLA Ops:
  12.8 36.8 %collective-permute-start.2 = (bf16[48,3712]{1,0:T(8,128)(2,1)}, bf16[48,3712]{1,0:T(8,128)(2,1)}, u32[]{:S(2)}, u32[]{:S(2)}) collective-permute-start(bf16[48,3712]{1,0:T(8,128)(2,1)} %concatenate.98), channel_id=1, source_target_pairs={{0,24},{8,0},{16,8},{24,16},{1,25},{9,1},{17,9},{25,17},{2,26},{10... | collective-permute-start | bytes 1069064 | tf_op jit(solution)/shard_map/ppermute | solution.py:656
  17.9 30.7 %collective-permute-start.1 = (bf16[48,3712]{1,0:T(8,128)(2,1)}, bf16[48,3712]{1,0:T(8,128)(2,1)}, u32[]{:S(2)}, u32[]{:S(2)}) collective-permute-start(bf16[48,3712]{1,0:T(8,128)(2,1)} %concatenate.98), channel_id=1, source_target_pairs={{0,16},{8,24},{16,0},{24,8},{1,17},{9,25},{17,1},{25,9},{2,18},{10... | collective-permute-start | bytes 1069064 | tf_op jit(solution)/shard_map/ppermute | solution.py:656
  17.9 24.2 %collective-permute-start = (bf16[48,3712]{1,0:T(8,128)(2,1)}, bf16[48,3712]{1,0:T(8,128)(2,1)}, u32[]{:S(2)}, u32[]{:S(2)}) collective-permute-start(bf16[48,3712]{1,0:T(8,128)(2,1)} %concatenate.98), channel_id=1, source_target_pairs={{0,8},{8,16},{16,24},{24,0},{1,9},{9,17},{17,25},{25,1},{2,10},{10... | collective-permute-start | bytes 1069064 | tf_op jit(solution)/shard_map/ppermute | solution.py:656
  22.4 35.6 %all-to-all-start = ((bf16[8,48,3456]{2,1,0:T(8,128)(2,1)}), bf16[8,48,3456]{2,1,0:T(8,128)(2,1)S(1)}, u32[]{:S(2)}, u32[]{:S(2)}) async-start(bf16[8,48,3456]{2,1,0:T(8,128)(2,1)} %bitcast.109), calls=%async_computation | async-start | bytes 5308416 | tf_op jit(solution)/shard_map/all_to_all | solution.py:615
  26.2 184.9 %all-gather.4.cloned.1.call-start = ((), (), s32[]{:S(2)}) async-start(), calls=%async_computation.7 | async-start | bytes 4423680 | tf_op jit(solution)/shard_map/all_gather | solution.py:618
  36.1 111.1 %copy-start.38 = (f32[64,256]{1,0:T(8,128)}, f32[64,256]{1,0:T(8,128)S(1)}, u32[]{:S(2)}) copy-start(f32[64,256]{1,0:T(8,128)S(1)} %get-tuple-element.176.cos_ref) | copy-start | bytes 196612
  38.0 45.9 %copy-start.35 = (f32[256,64]{1,0:T(8,128)}, f32[256,64]{1,0:T(8,128)S(1)}, u32[]{:S(2)}) copy-start(f32[256,64]{1,0:T(8,128)S(1)} %get-tuple-element.175) | copy-start | bytes 196612
  51.7 10.0 %collective-permute-start.3 = (bf16[192,640]{1,0:T(8,128)(2,1)S(1)}, bf16[192,640]{1,0:T(8,128)(2,1)S(1)}, u32[]{:S(2)}, u32[]{:S(2)}) collective-permute-start(bf16[192,640]{1,0:T(8,128)(2,1)S(1)} %slice.222), channel_id=1, source_target_pairs={{0,4},{1,5},{2,3},{3,2},{4,0},{5,1},{6,7},{7,6},{8,12},{9,13},{10,... | collective-permute-start | bytes 737288 | tf_op jit(solution)/shard_map/ppermute | solution.py:535
  59.6 151.7 %all-gather.8.cloned.1.call-start = ((), (), s32[]{:S(2)}) async-start(), calls=%async_computation.9 | async-start | bytes 4423680 | tf_op jit(solution)/shard_map/all_gather | solution.py:618
  61.8 13.8 %collective-permute-start.7 = (bf16[384,640]{1,0:T(8,128)(2,1)S(1)}, bf16[384,640]{1,0:T(8,128)(2,1)S(1)}, u32[]{:S(2)}, u32[]{:S(2)}) collective-permute-start(bf16[384,640]{1,0:T(8,128)(2,1)S(1)} %pad_maximum_fusion.9), channel_id=1, source_target_pairs={{0,1},{1,0},{2,6},{3,7},{4,5},{5,4},{6,2},{7,3},{8,9},{9,8},{10,14... | collective-permute-start | bytes 1474568 | tf_op jit(solution)/shard_map/ppermute | solution.py:535
  63.4 13.2 %collective-permute-start.4 = (bf16[192,1536]{1,0:T(8,128)(2,1)S(1)}, bf16[192,1536]{1,0:T(8,128)(2,1)S(1)}, u32[]{:S(2)}, u32[]{:S(2)}) collective-permute-start(bf16[192,1536]{1,0:T(8,128)(2,1)S(1)} %get-tuple-element.67), channel_id=1, source_target_pairs={{0,4},{1,5},{2,3},{3,2},{4,0},{5,1},{6,7},{7,6},{8,12},{9,13},{10,... | collective-permute-start | bytes 1769480 | tf_op jit(solution)/shard_map/ppermute | solution.py:535
  75.7 3.2 collective-permute-start.8
  77.7 16.5 %collective-permute-start.5 = (bf16[384,1536]{1,0:T(8,128)(2,1)}, bf16[384,1536]{1,0:T(8,128)(2,1)}, u32[]{:S(2)}, u32[]{:S(2)}) collective-permute-start(bf16[384,1536]{1,0:T(8,128)(2,1)} %pad_maximum_fusion.5), channel_id=1, source_target_pairs={{0,1},{1,0},{2,6},{3,7},{4,5},{5,4},{6,2},{7,3},{8,9},{9,8},{10,14... | collective-permute-start | bytes 3538952 | tf_op jit(solution)/shard_map/ppermute | solution.py:535
  96.6 6.7 %collective-permute-start.9 = (bf16[256,512]{1,0:T(8,128)(2,1)}, bf16[256,512]{1,0:T(8,128)(2,1)}, u32[]{:S(2)}, u32[]{:S(2)}) collective-permute-start(bf16[256,512]{1,0:T(8,128)(2,1)} %pad_maximum_fusion.10), channel_id=1, source_target_pairs={{0,4},{1,5},{2,3},{3,2},{4,0},{5,1},{6,7},{7,6},{8,12},{9,13},{10,... | collective-permute-start | bytes 786440 | tf_op jit(solution)/shard_map/ppermute | solution.py:535
  97.6 12.0 %collective-permute-start.6 = (bf16[192,1536]{1,0:T(8,128)(2,1)S(1)}, bf16[192,1536]{1,0:T(8,128)(2,1)}, u32[]{:S(2)}, u32[]{:S(2)}) collective-permute-start(bf16[192,1536]{1,0:T(8,128)(2,1)S(1)} %copy-done.34), channel_id=1, source_target_pairs={{0,4},{1,5},{2,3},{3,2},{4,0},{5,1},{6,7},{7,6},{8,12},{9,13},{10,... | collective-permute-start | bytes 1769480 | tf_op jit(solution)/shard_map/ppermute | solution.py:535
  101.2 177.2 %all-gather.6.cloned.1.call-start = ((), (), s32[]{:S(2)}) async-start(), calls=%async_computation.8 | async-start | bytes 4423680 | tf_op jit(solution)/shard_map/all_gather | solution.py:618
  101.5 40.3 %collective-permute-start.12 = (bf16[768,1536]{1,0:T(8,128)(2,1)}, bf16[768,1536]{1,0:T(8,128)(2,1)}, u32[]{:S(2)}, u32[]{:S(2)}) collective-permute-start(bf16[768,1536]{1,0:T(8,128)(2,1)} %constant_dynamic-update-slice_fusion), channel_id=1, source_target_pairs={{0,2},{1,3},{2,0},{3,1},{4,6},{5,7},{6,4},{7,5},{8,10},{9,11},{10,... | collective-permute-start | bytes 7077896 | tf_op jit(solution)/shard_map/ppermute | solution.py:535
  110.7 9.6 %collective-permute-start.10 = (bf16[512,512]{1,0:T(8,128)(2,1)}, bf16[512,512]{1,0:T(8,128)(2,1)}, u32[]{:S(2)}, u32[]{:S(2)}) collective-permute-start(bf16[512,512]{1,0:T(8,128)(2,1)} %pad_maximum_fusion.8), channel_id=1, source_target_pairs={{0,1},{1,0},{2,6},{3,7},{4,5},{5,4},{6,2},{7,3},{8,9},{9,8},{10,14... | collective-permute-start | bytes 1572872 | tf_op jit(solution)/shard_map/ppermute | solution.py:535
  121.4 20.3 %collective-permute-start.13 = (bf16[1024,512]{1,0:T(8,128)(2,1)S(1)}, bf16[1024,512]{1,0:T(8,128)(2,1)S(1)}, u32[]{:S(2)}, u32[]{:S(2)}) collective-permute-start(bf16[1024,512]{1,0:T(8,128)(2,1)S(1)} %get-tuple-element.160), channel_id=1, source_target_pairs={{0,2},{1,3},{2,0},{3,1},{4,6},{5,7},{6,4},{7,5},{8,10},{9,11},{10,... | collective-permute-start | bytes 3145736 | tf_op jit(solution)/shard_map/ppermute | solution.py:535
  121.5 18.5 %collective-permute-start.11 = (bf16[256,1536]{1,0:T(8,128)(2,1)S(1)}, bf16[256,1536]{1,0:T(8,128)(2,1)S(1)}, u32[]{:S(2)}, u32[]{:S(2)}) collective-permute-start(bf16[256,1536]{1,0:T(8,128)(2,1)S(1)} %copy-done.11), channel_id=1, source_target_pairs={{0,4},{1,5},{2,3},{3,2},{4,0},{5,1},{6,7},{7,6},{8,12},{9,13},{10,... | collective-permute-start | bytes 2359304 | tf_op jit(solution)/shard_map/ppermute | solution.py:535
  124.0 31.3 %collective-permute-start.15 = (bf16[384,1536]{1,0:T(8,128)(2,1)S(1)}, bf16[384,1536]{1,0:T(8,128)(2,1)S(1)}, u32[]{:S(2)}, u32[]{:S(2)}) collective-permute-start(bf16[384,1536]{1,0:T(8,128)(2,1)S(1)} %constant_dynamic-update-slice_fusion.3), channel_id=1, source_target_pairs={{0,1},{1,0},{2,6},{3,7},{4,5},{5,4},{6,2},{7,3},{8,9},{9,8},{10,14... | collective-permute-start | bytes 3538952 | tf_op jit(solution)/shard_map/ppermute | solution.py:535
  140.1 22.4 %collective-permute-start.14 = (bf16[512,1536]{1,0:T(8,128)(2,1)S(1)}, bf16[512,1536]{1,0:T(8,128)(2,1)S(1)}, u32[]{:S(2)}, u32[]{:S(2)}) collective-permute-start(bf16[512,1536]{1,0:T(8,128)(2,1)S(1)} %constant_dynamic-update-slice_fusion.7), channel_id=1, source_target_pairs={{0,1},{1,0},{2,6},{3,7},{4,5},{5,4},{6,2},{7,3},{8,9},{9,8},{10,14... | collective-permute-start | bytes 4718600 | tf_op jit(solution)/shard_map/ppermute | solution.py:535
  155.4 8.7 %collective-permute-start.16 = (bf16[768,1536]{1,0:T(8,128)(2,1)S(1)}, bf16[768,1536]{1,0:T(8,128)(2,1)S(1)}, u32[]{:S(2)}, u32[]{:S(2)}) collective-permute-start(bf16[768,1536]{1,0:T(8,128)(2,1)S(1)} %pad_maximum_fusion.1), channel_id=1, source_target_pairs={{0,2},{1,3},{2,0},{3,1},{4,6},{5,7},{6,4},{7,5},{8,10},{9,11},{10,... | collective-permute-start | bytes 7077896 | tf_op jit(solution)/shard_map/ppermute | solution.py:535
  169.3 16.4 %collective-permute-start.17 = (bf16[256,1536]{1,0:T(8,128)(2,1)S(1)}, bf16[256,1536]{1,0:T(8,128)(2,1)S(1)}, u32[]{:S(2)}, u32[]{:S(2)}) collective-permute-start(bf16[256,1536]{1,0:T(8,128)(2,1)S(1)} %multiply_convert_fusion), channel_id=1, source_target_pairs={{0,4},{1,5},{2,3},{3,2},{4,0},{5,1},{6,7},{7,6},{8,12},{9,13},{10,... | collective-permute-start | bytes 2359304 | tf_op jit(solution)/shard_map/ppermute | solution.py:535
  175.8 179.9 %reduce-scatter.5.cloned.1.call-start = ((), (), s32[]{:S(2)}) async-start(), calls=%async_computation.10 | async-start | bytes 4423680 | tf_op jit(solution)/shard_map/reduce_scatter | solution.py:621
  185.8 23.7 %collective-permute-start.18 = (bf16[512,1536]{1,0:T(8,128)(2,1)S(1)}, bf16[512,1536]{1,0:T(8,128)(2,1)S(1)}, u32[]{:S(2)}, u32[]{:S(2)}) collective-permute-start(bf16[512,1536]{1,0:T(8,128)(2,1)S(1)} %pad_maximum_fusion.3), channel_id=1, source_target_pairs={{0,1},{1,0},{2,6},{3,7},{4,5},{5,4},{6,2},{7,3},{8,9},{9,8},{10,14... | collective-permute-start | bytes 4718600 | tf_op jit(solution)/shard_map/ppermute | solution.py:535
  191.2 20.1 %collective-permute-start.20 = (bf16[1024,1536]{1,0:T(8,128)(2,1)}, bf16[1024,1536]{1,0:T(8,128)(2,1)}, u32[]{:S(2)}, u32[]{:S(2)}) collective-permute-start(bf16[1024,1536]{1,0:T(8,128)(2,1)} %constant_dynamic-update-slice_fusion.12.refs_2_.cot_near), channel_id=1, source_target_pairs={{0,2},{1,3},{2,0},{3,1},{4,6},{5,7},{6,4},{7,5},{8,10},{9,11},{10,... | collective-permute-start | bytes 9437192 | tf_op jit(solution)/shard_map/ppermute | solution.py:535
  211.2 5.9 %collective-permute-start.19 = (bf16[1024,1536]{1,0:T(8,128)(2,1)S(1)}, bf16[1024,1536]{1,0:T(8,128)(2,1)}, u32[]{:S(2)}, u32[]{:S(2)}) collective-permute-start(bf16[1024,1536]{1,0:T(8,128)(2,1)S(1)} %pad_maximum_fusion.refs_0_.mid_near), channel_id=1, source_target_pairs={{0,2},{1,3},{2,0},{3,1},{4,6},{5,7},{6,4},{7,5},{8,10},{9,11},{10,... | collective-permute-start | bytes 9437192 | tf_op jit(solution)/shard_map/ppermute | solution.py:535
  278.4 140.1 %reduce-scatter.7.cloned.1.call-start = ((), (), s32[]{:S(2)}) async-start(), calls=%async_computation.11 | async-start | bytes 4423680 | tf_op jit(solution)/shard_map/reduce_scatter | solution.py:621
  303.7 7.9 %collective-permute-start.21 = (bf16[1024,1536]{1,0:T(8,128)(2,1)}, bf16[1024,1536]{1,0:T(8,128)(2,1)S(1)}, u32[]{:S(2)}, u32[]{:S(2)}) collective-permute-start(bf16[1024,1536]{1,0:T(8,128)(2,1)} %get-tuple-element.86), channel_id=1, source_target_pairs={{0,2},{1,3},{2,0},{3,1},{4,6},{5,7},{6,4},{7,5},{8,10},{9,11},{10,... | collective-permute-start | bytes 9437192 | tf_op jit(solution)/shard_map/ppermute | solution.py:535
  304.1 38.4 %collective-permute-start.23 = (bf16[1024,1536]{1,0:T(8,128)(2,1)}, bf16[1024,1536]{1,0:T(8,128)(2,1)}, u32[]{:S(2)}, u32[]{:S(2)}) collective-permute-start(bf16[1024,1536]{1,0:T(8,128)(2,1)} %get-tuple-element.91), channel_id=1, source_target_pairs={{0,2},{1,3},{2,0},{3,1},{4,6},{5,7},{6,4},{7,5},{8,10},{9,11},{10,... | collective-permute-start | bytes 9437192 | tf_op jit(solution)/shard_map/ppermute | solution.py:535
  316.0 21.8 %collective-permute-start.22 = (bf16[512,1536]{1,0:T(8,128)(2,1)S(1)}, bf16[512,1536]{1,0:T(8,128)(2,1)}, u32[]{:S(2)}, u32[]{:S(2)}) collective-permute-start(bf16[512,1536]{1,0:T(8,128)(2,1)S(1)} %get-tuple-element.129), channel_id=1, source_target_pairs={{0,1},{1,0},{2,6},{3,7},{4,5},{5,4},{6,2},{7,3},{8,9},{9,8},{10,14... | collective-permute-start | bytes 4718600 | tf_op jit(solution)/shard_map/ppermute | solution.py:535
  340.1 12.1 %collective-permute-start.24 = (bf16[256,1536]{1,0:T(8,128)(2,1)S(1)}, bf16[256,1536]{1,0:T(8,128)(2,1)S(1)}, u32[]{:S(2)}, u32[]{:S(2)}) collective-permute-start(bf16[256,1536]{1,0:T(8,128)(2,1)S(1)} %slice.242), channel_id=1, source_target_pairs={{0,4},{1,5},{2,3},{3,2},{4,0},{5,1},{6,7},{7,6},{8,12},{9,13},{10,... | collective-permute-start | bytes 2359304 | tf_op jit(solution)/shard_map/ppermute | solution.py:535
  342.2 147.9 %reduce-scatter.9.cloned.1.call-start = ((), (), s32[]{:S(2)}) async-start(), calls=%async_computation.12 | async-start | bytes 4423680 | tf_op jit(solution)/shard_map/reduce_scatter | solution.py:621
  353.7 23.4 %collective-permute-start.25 = (bf16[512,1536]{1,0:T(8,128)(2,1)}, bf16[512,1536]{1,0:T(8,128)(2,1)}, u32[]{:S(2)}, u32[]{:S(2)}) collective-permute-start(bf16[512,1536]{1,0:T(8,128)(2,1)} %slice.197), channel_id=1, source_target_pairs={{0,1},{1,0},{2,6},{3,7},{4,5},{5,4},{6,2},{7,3},{8,9},{9,8},{10,14... | collective-permute-start | bytes 4718600 | tf_op jit(solution)/shard_map/ppermute | solution.py:535
  370.6 9.9 %collective-permute-start.26 = (bf16[1024,512]{1,0:T(8,128)(2,1)}, bf16[1024,512]{1,0:T(8,128)(2,1)}, u32[]{:S(2)}, u32[]{:S(2)}) collective-permute-start(bf16[1024,512]{1,0:T(8,128)(2,1)} %get-tuple-element.98), channel_id=1, source_target_pairs={{0,2},{1,3},{2,0},{3,1},{4,6},{5,7},{6,4},{7,5},{8,10},{9,11},{10,... | collective-permute-start | bytes 3145736 | tf_op jit(solution)/shard_map/ppermute | solution.py:535
  392.0 16.9 %collective-permute-start.28 = (bf16[768,3072]{1,0:T(8,128)(2,1)}, bf16[768,3072]{1,0:T(8,128)(2,1)}, u32[]{:S(2)}, u32[]{:S(2)}) collective-permute-start(bf16[768,3072]{1,0:T(8,128)(2,1)} %get-tuple-element.103), channel_id=1, source_target_pairs={{0,2},{1,3},{2,0},{3,1},{4,6},{5,7},{6,4},{7,5},{8,10},{9,11},{10,... | collective-permute-start | bytes 14155784 | tf_op jit(solution)/shard_map/ppermute | solution.py:535
  395.8 22.7 %collective-permute-start.29 = (bf16[512,512]{1,0:T(8,128)(2,1)}, bf16[512,512]{1,0:T(8,128)(2,1)}, u32[]{:S(2)}, u32[]{:S(2)}) collective-permute-start(bf16[512,512]{1,0:T(8,128)(2,1)} %get-tuple-element.152), channel_id=1, source_target_pairs={{0,1},{1,0},{2,6},{3,7},{4,5},{5,4},{6,2},{7,3},{8,9},{9,8},{10,14... | collective-permute-start | bytes 1572872 | tf_op jit(solution)/shard_map/ppermute | solution.py:535
  399.4 25.0 %collective-permute-start.27 = (bf16[256,1536]{1,0:T(8,128)(2,1)}, bf16[256,1536]{1,0:T(8,128)(2,1)}, u32[]{:S(2)}, u32[]{:S(2)}) collective-permute-start(bf16[256,1536]{1,0:T(8,128)(2,1)} %slice.199), channel_id=1, source_target_pairs={{0,4},{1,5},{2,3},{3,2},{4,0},{5,1},{6,7},{7,6},{8,12},{9,13},{10,... | collective-permute-start | bytes 2359304 | tf_op jit(solution)/shard_map/ppermute | solution.py:535
  420.0 8.7 %collective-permute-start.30 = (bf16[256,512]{1,0:T(8,128)(2,1)S(1)}, bf16[256,512]{1,0:T(8,128)(2,1)S(1)}, u32[]{:S(2)}, u32[]{:S(2)}) collective-permute-start(bf16[256,512]{1,0:T(8,128)(2,1)S(1)} %slice.246), channel_id=1, source_target_pairs={{0,4},{1,5},{2,3},{3,2},{4,0},{5,1},{6,7},{7,6},{8,12},{9,13},{10,... | collective-permute-start | bytes 786440 | tf_op jit(solution)/shard_map/ppermute | solution.py:535
  422.2 29.4 %collective-permute-start.31 = (bf16[384,3072]{1,0:T(8,128)(2,1)}, bf16[384,3072]{1,0:T(8,128)(2,1)}, u32[]{:S(2)}, u32[]{:S(2)}) collective-permute-start(bf16[384,3072]{1,0:T(8,128)(2,1)} %slice.250), channel_id=1, source_target_pairs={{0,1},{1,0},{2,6},{3,7},{4,5},{5,4},{6,2},{7,3},{8,9},{9,8},{10,14... | collective-permute-start | bytes 7077896 | tf_op jit(solution)/shard_map/ppermute | solution.py:535
  459.4 3.6 collective-permute-start.33
  460.9 26.5 %collective-permute-start.32 = (bf16[192,3072]{1,0:T(8,128)(2,1)}, bf16[192,3072]{1,0:T(8,128)(2,1)}, u32[]{:S(2)}, u32[]{:S(2)}) collective-permute-start(bf16[192,3072]{1,0:T(8,128)(2,1)} %slice.252), channel_id=1, source_target_pairs={{0,4},{1,5},{2,3},{3,2},{4,0},{5,1},{6,7},{7,6},{8,12},{9,13},{10,... | collective-permute-start | bytes 3538952 | tf_op jit(solution)/shard_map/ppermute | solution.py:535
  464.4 14.6 %collective-permute-start.34 = (bf16[384,640]{1,0:T(8,128)(2,1)}, bf16[384,640]{1,0:T(8,128)(2,1)}, u32[]{:S(2)}, u32[]{:S(2)}) collective-permute-start(bf16[384,640]{1,0:T(8,128)(2,1)} %slice.254), channel_id=1, source_target_pairs={{0,1},{1,0},{2,6},{3,7},{4,5},{5,4},{6,2},{7,3},{8,9},{9,8},{10,14... | collective-permute-start | bytes 1474568 | tf_op jit(solution)/shard_map/ppermute | solution.py:535
  465.6 26.7 %all-to-all-start.1 = ((bf16[8,48,1152]{2,1,0:T(8,128)(2,1)}), bf16[8,48,1152]{2,1,0:T(8,128)(2,1)}, u32[]{:S(2)}, u32[]{:S(2)}) async-start(bf16[8,48,1152]{2,1,0:T(8,128)(2,1)} %bitcast.154), calls=%async_computation.4 | async-start | bytes 1769472 | tf_op jit(solution)/shard_map/all_to_all | solution.py:615
  469.8 63.9 %reduce-scatter.11.cloned.1.call-start = ((), (), s32[]{:S(2)}) async-start(), calls=%async_computation.13 | async-start | bytes 1781760 | tf_op jit(solution)/shard_map/reduce_scatter | solution.py:621
  481.1 13.8 %collective-permute-start.35 = (bf16[192,640]{1,0:T(8,128)(2,1)}, bf16[192,640]{1,0:T(8,128)(2,1)}, u32[]{:S(2)}, u32[]{:S(2)}) collective-permute-start(bf16[192,640]{1,0:T(8,128)(2,1)} %get-tuple-element.166), channel_id=1, source_target_pairs={{0,4},{1,5},{2,3},{3,2},{4,0},{5,1},{6,7},{7,6},{8,12},{9,13},{10,... | collective-permute-start | bytes 737288 | tf_op jit(solution)/shard_map/ppermute | solution.py:535
  501.2 26.7 %all-to-all-start.2 = ((bf16[8,48,2304]{2,1,0:T(8,128)(2,1)}), bf16[8,48,2304]{2,1,0:T(8,128)(2,1)}, u32[]{:S(2)}, u32[]{:S(2)}) async-start(bf16[8,48,2304]{2,1,0:T(8,128)(2,1)} %bitcast.117), calls=%async_computation.6 | async-start | bytes 3538944 | tf_op jit(solution)/shard_map/all_to_all | solution.py:615
  (55 other events, 323.3 us)
Sparse Core Ops, SparseCore 0:
  59.7 69.4 all-gather.3
  130.8 68.5 all-gather.7
  201.0 68.5 all-gather.5
  278.5 68.1 reduce-scatter.4
  348.8 66.6 reduce-scatter.6
  417.7 66.6 reduce-scatter.8
  498.6 35.0 reduce-scatter.10
where the time goes:
time: 553 us; the launch traced here: 543 us
  waiting for transfers between devices  161 us (29%)
  Pallas kernels  139 us (25%)
  starting transfers between devices  83.1 us (15%)
  other arithmetic  63.5 us (11%)
  local copies, waits for them, and re-layouts  61.4 us (11%)
  between operations  18.7 us (3%)
  matrix products  15.7 us (3%)
    ppermute x33, waiting for transfers between devices, swap(): return lax.ppermute(array, PLANE, pairs)  124 us
    pallas_call x2, Pallas kernels, feed_forward(): pl.pallas_call(functools.partial(ffn_kernel, cols, count, not sums, with_...  86.6 us
    ppermute x33, starting transfers between devices, swap(): return lax.ppermute(array, PLANE, pairs)  63.8 us
    convert_element_type x14, other arithmetic, fold(): return (near.astype(F32) + self.swap(far, step).astype(F32)).astype(BF16)  30.9 us
    all_to_all x3, waiting for transfers between devices, swap_rows(): return lax.all_to_all(array, PLANE, split_axis=0, concat_axis=0, tiled=True)  25.5 us
    unnamed x125, local copies, waits for them, and re-layouts  16.1 us
    dot_general x6, matrix products, dot(): lax.dot_general(left, right, (((left_dim,), (right_dim,)), ((), ())), pre...  15.7 us
    pallas_call x1, Pallas kernels, feed_forward_grad(): pl.pallas_call(functools.partial(ffn_grad_kernel, cols), grid=(width // t...  13.9 us
  transfers between devices with their start and end apart: 46, of which 26 were waited for; matrix products, arithmetic and copies ran while one was open for 22% of the time, Pallas kernels for 25%

commit v1 on v0

--- a/solution.py
+++ b/solution.py
@@ -42,10 +42,21 @@
     return jnp.where(allowed, 0.0, NEG_FILL)
 
 
+def beside(array_ref, wide_ref):
+    cols = array_ref.shape[1]
+    for head in range(HEADS):
+        group, place = divmod(head, GROUP)
+        wide_ref[group * HEAD : (group + 1) * HEAD, place * cols : (place + 1) * cols] = array_ref[
+            head * HEAD : (head + 1) * HEAD, :
+        ]
+
+
 def attn_fwd_kernel(
-    need_ref, kinfo_ref, qinfo_ref, q_ref, kv_ref, o_ref, lse_ref, m_ref, l_ref, acc_ref, bias_ref
+    need_ref, kinfo_ref, qinfo_ref, q_ref, kv_ref, o_ref, lse_ref, m_ref, l_ref, acc_ref, wide_ref
 ):
     blocks = kv_ref.shape[0] // TOK_DEV
+    cols = q_ref.shape[1]
+    beside(q_ref, wide_ref)
     m_ref[...] = jnp.full(m_ref.shape, NEG_FILL, F32)
     l_ref[...] = jnp.zeros(l_ref.shape, F32)
     acc_ref[...] = jnp.zeros(acc_ref.shape, F32)
@@ -54,36 +65,36 @@
         @pl.when(need_ref[block] > 0)
         def _():
             rows = pl.ds(pl.multiple_of(block * TOK_DEV, TOK_DEV), TOK_DEV)
-            bias_ref[...] = block_bias(kinfo_ref, qinfo_ref, rows)
+            bias = jnp.concatenate([block_bias(kinfo_ref, qinfo_ref, rows)] * GROUP, axis=1)
             for group in range(KV_HEADS):
                 key = kv_ref[rows, group * HEAD : (group + 1) * HEAD]
                 value = kv_ref[rows, (KV_HEADS + group) * HEAD : (KV_HEADS + group + 1) * HEAD]
-                value_t = value.T
-                for head in range(group * GROUP, (group + 1) * GROUP):
-                    span = slice(head * HEAD, (head + 1) * HEAD)
-                    scores = dot(key, q_ref[span, :], 1, 0) * (SCALE * LOG2E) + bias_ref[...]
-                    old = m_ref[head : head + 1, :]
-                    new = jnp.maximum(old, jnp.max(scores, axis=0, keepdims=True))
-                    weights = jnp.exp2(scores - new)
-                    factor = jnp.exp2(old - new)
-                    m_ref[head : head + 1, :] = new
-                    l_ref[head : head + 1, :] = l_ref[head : head + 1, :] * factor + jnp.sum(
-                        weights, axis=0, keepdims=True
-                    )
-                    acc_ref[span, :] = acc_ref[span, :] * factor + dot(
-                        value_t, weights.astype(BF16), 1, 0
-                    )
+                span = slice(group * HEAD, (group + 1) * HEAD)
+                row = slice(group, group + 1)
+                scores = dot(key, wide_ref[span, :], 1, 0) * (SCALE * LOG2E) + bias
+                old = m_ref[row, :]
+                new = jnp.maximum(old, jnp.max(scores, axis=0, keepdims=True))
+                weights = jnp.exp2(scores - new)
+                factor = jnp.exp2(old - new)
+                m_ref[row, :] = new
+                l_ref[row, :] = l_ref[row, :] * factor + jnp.sum(weights, axis=0, keepdims=True)
+                acc_ref[span, :] = acc_ref[span, :] * factor + dot(
+                    value.T, weights.astype(BF16), 1, 0
+                )
 
         return carry
 
     lax.fori_loop(0, blocks, one_block, 0)
     real = qinfo_ref[2:3, :].astype(F32)
     lse_ref[...] = jnp.zeros(lse_ref.shape, F32)
+    lse_ref[:KV_HEADS, :] = m_ref[:KV_HEADS, :] + jnp.log(l_ref[:KV_HEADS, :]) * LOG2E
     for head in range(HEADS):
-        span = slice(head * HEAD, (head + 1) * HEAD)
-        total = l_ref[head : head + 1, :]
-        o_ref[span, :] = (acc_ref[span, :] * (real / total)).astype(BF16)
-        lse_ref[head : head + 1, :] = m_ref[head : head + 1, :] + jnp.log(total) * LOG2E
+        group, place = divmod(head, GROUP)
+        there = slice(place * cols, (place + 1) * cols)
+        total = l_ref[group : group + 1, there]
+        o_ref[head * HEAD : (head + 1) * HEAD, :] = (
+            acc_ref[group * HEAD : (group + 1) * HEAD, there] * (real / total)
+        ).astype(BF16)
 
 
 def attn_bwd_kernel(
@@ -102,16 +113,20 @@
     far_ref,
     dots_ref,
     acc_ref,
-    bias_ref,
+    wide_ref,
     low_ref,
 ):
     blocks = kv_ref.shape[0] // TOK_DEV
+    cols = q_ref.shape[1]
     real = qinfo_ref[2:3, :].astype(F32)
+    beside(q_ref, wide_ref)
     for head in range(HEADS):
+        group, place = divmod(head, GROUP)
+        there = slice(place * cols, (place + 1) * cols)
         span = slice(head * HEAD, (head + 1) * HEAD)
         grad = do_ref[span, :].astype(F32) * real
-        low_ref[span, :] = grad.astype(BF16)
-        dots_ref[head : head + 1, :] = jnp.sum(
+        low_ref[group * HEAD : (group + 1) * HEAD, there] = grad.astype(BF16)
+        dots_ref[group : group + 1, there] = jnp.sum(
             grad * o_ref[span, :].astype(F32), axis=0, keepdims=True
         )
     acc_ref[...] = jnp.zeros(acc_ref.shape, F32)
@@ -127,27 +142,21 @@
 
         @pl.when(need_ref[block] > 0)
         def _():
-            bias_ref[...] = block_bias(kinfo_ref, qinfo_ref, rows)
+            bias = jnp.concatenate([block_bias(kinfo_ref, qinfo_ref, rows)] * GROUP, axis=1)
             for group in range(KV_HEADS):
                 key_cols = slice(group * HEAD, (group + 1) * HEAD)
                 value_cols = slice((KV_HEADS + group) * HEAD, (KV_HEADS + group + 1) * HEAD)
                 key = kv_ref[rows, key_cols]
                 value = kv_ref[rows, value_cols]
-                key_t = key.T
-                key_grad = jnp.zeros((TOK_DEV, HEAD), F32)
-                value_grad = jnp.zeros((TOK_DEV, HEAD), F32)
-                for head in range(group * GROUP, (group + 1) * GROUP):
-                    span = slice(head * HEAD, (head + 1) * HEAD)
-                    query, grad = q_ref[span, :], low_ref[span, :]
-                    scores = dot(key, query, 1, 0) * (SCALE * LOG2E) + bias_ref[...]
-                    probs = jnp.exp2(scores - lse_ref[head : head + 1, :])
-                    prob_grad = dot(value, grad, 1, 0)
-                    score_grad = (probs * (prob_grad - dots_ref[head : head + 1, :])).astype(BF16)
-                    acc_ref[span, :] += dot(key_t, score_grad, 1, 0)
-                    key_grad += dot(score_grad, query, 1, 1)
-                    value_grad += dot(probs.astype(BF16), grad, 1, 1)
-                dkv_ref[out_rows, key_cols] = (key_grad * SCALE).astype(BF16)
-                dkv_ref[out_rows, value_cols] = value_grad.astype(BF16)
+                query, grad = wide_ref[key_cols, :], low_ref[key_cols, :]
+                row = slice(group, group + 1)
+                scores = dot(key, query, 1, 0) * (SCALE * LOG2E) + bias
+                probs = jnp.exp2(scores - lse_ref[row, :])
+                prob_grad = dot(value, grad, 1, 0)
+                score_grad = (probs * (prob_grad - dots_ref[row, :])).astype(BF16)
+                acc_ref[key_cols, :] += dot(key.T, score_grad, 1, 0)
+                dkv_ref[out_rows, key_cols] = (dot(score_grad, query, 1, 1) * SCALE).astype(BF16)
+                dkv_ref[out_rows, value_cols] = dot(probs.astype(BF16), grad, 1, 1).astype(BF16)
 
         return carry
 
@@ -157,13 +166,15 @@
     cosine, sine = cos_ref[...], sin_ref[...]
     half = HEAD // 2
     for head in range(HEADS):
-        start = head * HEAD
-        whole = (acc_ref[start : start + HEAD, :] * SCALE).astype(BF16).astype(F32)
+        group, place = divmod(head, GROUP)
+        there = slice(place * cols, (place + 1) * cols)
+        whole = acc_ref[group * HEAD : (group + 1) * HEAD, there] * SCALE
+        whole = whole.astype(BF16).astype(F32)
         first, second = whole[:half], whole[half:]
         turned = jnp.concatenate(
             [first * cosine + second * sine, second * cosine - first * sine], axis=0
         )
-        dq_ref[:, start : start + HEAD] = turned.T.astype(BF16)
+        dq_ref[:, head * HEAD : (head + 1) * HEAD] = turned.T.astype(BF16)
 
 
 def vmem_specs(count):
@@ -176,15 +187,15 @@
         attn_fwd_kernel,
         out_shape=(
             jax.ShapeDtypeStruct((HEADS * HEAD, rows), BF16),
-            jax.ShapeDtypeStruct((16, rows), F32),
+            jax.ShapeDtypeStruct((8, GROUP * rows), F32),
         ),
         in_specs=[pl.BlockSpec(memory_space=pltpu.SMEM)] + vmem_specs(4),
         out_specs=tuple(vmem_specs(2)),
         scratch_shapes=[
-            pltpu.VMEM((16, rows), F32),
-            pltpu.VMEM((16, rows), F32),
-            pltpu.VMEM((HEADS * HEAD, rows), F32),
-            pltpu.VMEM((TOK_DEV, rows), F32),
+            pltpu.VMEM((8, GROUP * rows), F32),
+            pltpu.VMEM((8, GROUP * rows), F32),
+            pltpu.VMEM((KV_HEADS * HEAD, GROUP * rows), F32),
+            pltpu.VMEM((KV_HEADS * HEAD, GROUP * rows), BF16),
         ],
         compiler_params=pltpu.CompilerParams(vmem_limit_bytes=VMEM_LIMIT),
         cost_estimate=SMALL,
@@ -203,10 +214,10 @@
         in_specs=[pl.BlockSpec(memory_space=pltpu.SMEM)] + vmem_specs(9),
         out_specs=tuple(vmem_specs(3)),
         scratch_shapes=[
-            pltpu.VMEM((16, rows), F32),
-            pltpu.VMEM((HEADS * HEAD, rows), F32),
-            pltpu.VMEM((TOK_DEV, rows), F32),
-            pltpu.VMEM((HEADS * HEAD, rows), BF16),
+            pltpu.VMEM((8, GROUP * rows), F32),
+            pltpu.VMEM((KV_HEADS * HEAD, GROUP * rows), F32),
+            pltpu.VMEM((KV_HEADS * HEAD, GROUP * rows), BF16),
+            pltpu.VMEM((KV_HEADS * HEAD, GROUP * rows), BF16),
         ],
         compiler_params=pltpu.CompilerParams(vmem_limit_bytes=VMEM_LIMIT),
         cost_estimate=SMALL,

time: 553 us -> 536 us (0.969)
  starting transfers between devices: 83.1 us -> 63.2 us
  waiting for transfers between devices: 161 us -> 167 us
    ppermute x33, starting transfers between devices: 63.8 us -> 44.1 us  [swap(): return lax.ppermute(array, PLANE, pairs)]
    ppermute x33, waiting for transfers between devices: 124 us -> 131 us  [swap(): return lax.ppermute(array, PLANE, pairs)]
  transfers between devices with their start and end apart: 46 -> 46, of which waited for: 26 -> 25; matrix products, arithmetic and copies ran while one was open for 22% -> 23% of each run, Pallas kernels for 25% -> 26%
where the time goes in v1:
time: 536 us; the launch traced here: 528 us
  waiting for transfers between devices  167 us (31%)
  Pallas kernels  140 us (26%)
  starting transfers between devices  63.2 us (12%)
  other arithmetic  63.2 us (12%)
  local copies, waits for them, and re-layouts  61.4 us (11%)
  between operations  18.6 us (3%)
  matrix products  15.7 us (3%)
    ppermute x33, waiting for transfers between devices, swap(): return lax.ppermute(array, PLANE, pairs)  131 us
    pallas_call x2, Pallas kernels, feed_forward(): pl.pallas_call(functools.partial(ffn_kernel, cols, count, not sums, with_...  86.2 us
    ppermute x33, starting transfers between devices, swap(): return lax.ppermute(array, PLANE, pairs)  44.1 us
    convert_element_type x14, other arithmetic, fold(): return (near.astype(F32) + self.swap(far, step).astype(F32)).astype(BF16)  30.9 us
    all_to_all x3, waiting for transfers between devices, swap_rows(): return lax.all_to_all(array, PLANE, split_axis=0, concat_axis=0, tiled=True)  25.7 us
    unnamed x125, local copies, waits for them, and re-layouts  16.1 us
    dot_general x6, matrix products, dot(): lax.dot_general(left, right, (((left_dim,), (right_dim,)), ((), ())), pre...  15.7 us
    pallas_call x1, Pallas kernels, feed_forward_grad(): pl.pallas_call(functools.partial(ffn_grad_kernel, cols), grid=(width // t...  13.8 us
  transfers between devices with their start and end apart: 46, of which 25 were waited for; matrix products, arithmetic and copies ran while one was open for 23% of the time, Pallas kernels for 26%

profile of v1, /device:TPU:0, one launch (start us, length us, event | category | flops | bytes accessed | tf_op | source)
XLA Modules:
  0.0 528.4 jit_solution(10518032113033682361)
XLA Ops:
  12.8 5.0 collective-permute-start.2
  18.9 3.5 shard_map.170
  22.4 3.9 all-to-all-start
  38.0 4.1 collective-permute-done
  43.1 5.5 %collective-permute-done.1 = bf16[48,3712]{1,0:T(8,128)(2,1)} collective-permute-done((bf16[48,3712]{1,0:T(8,128)(2,1)}, bf16[48,3712]{1,0:T(8,128)(2,1)}, u32[]{:S(2)}, u32[]{:S(2)}) %collective-permute-start.1) | collective-permute-done | bytes 356384 | tf_op jit(solution)/shard_map/ppermute | solution.py:667
  53.2 4.8 all-to-all-done
  64.3 11.4 %collective-permute-done.7 = bf16[384,640]{1,0:T(8,128)(2,1)S(1)} collective-permute-done((bf16[384,640]{1,0:T(8,128)(2,1)S(1)}, bf16[384,640]{1,0:T(8,128)(2,1)S(1)}, u32[]{:S(2)}, u32[]{:S(2)}) %collective-permute-start.7) | collective-permute-done | bytes 491552 | tf_op jit(solution)/shard_map/ppermute | solution.py:546
  86.5 7.7 %collective-permute-done.5 = bf16[384,1536]{1,0:T(8,128)(2,1)} collective-permute-done((bf16[384,1536]{1,0:T(8,128)(2,1)}, bf16[384,1536]{1,0:T(8,128)(2,1)}, u32[]{:S(2)}, u32[]{:S(2)}) %collective-permute-start.5) | collective-permute-done | bytes 1179680 | tf_op jit(solution)/shard_map/ppermute | solution.py:546
  105.1 4.5 collective-permute-done.6
  116.7 3.5 collective-permute-done.10
  124.9 15.1 %collective-permute-done.11 = bf16[256,1536]{1,0:T(8,128)(2,1)S(1)} collective-permute-done((bf16[256,1536]{1,0:T(8,128)(2,1)S(1)}, bf16[256,1536]{1,0:T(8,128)(2,1)S(1)}, u32[]{:S(2)}, u32[]{:S(2)}) %collective-permute-start.11) | collective-permute-done | bytes 786464 | tf_op jit(solution)/shard_map/ppermute | solution.py:546
  141.8 2.5 fusion.37
  148.4 6.6 %shard_map.171 = (bf16[1536,256]{1,0:T(8,128)(2,1)}, f32[8,1536]{1,0:T(8,128)}) custom-call(s32[8]{0:T(128)} %and_convert_fusion.need_ref, s32[2048,2]{1,0:T(8,128)} %copy.31.kinfo_ref, s32[8,256]{1,0:T(8,128)} %add_add_fusion.qinfo_ref, bf16[1536,256]{1,0:T(8,128)(2,1)} %bitcast.118, bf16[2048,512]{1,0:T(8,128)(2,1)} %copy-done.7), custom_call_target="tpu_custom_call" | custom-call | flops 1024 | bytes 1024 | tf_op jit(solution)/shard_map/pallas_call | solution.py:186
  158.0 4.4 collective-permute-done.14
  170.2 10.9 %collective-permute-done.17 = bf16[256,1536]{1,0:T(8,128)(2,1)S(1)} collective-permute-done((bf16[256,1536]{1,0:T(8,128)(2,1)S(1)}, bf16[256,1536]{1,0:T(8,128)(2,1)S(1)}, u32[]{:S(2)}, u32[]{:S(2)}) %collective-permute-start.17) | collective-permute-done | bytes 786464 | tf_op jit(solution)/shard_map/ppermute | solution.py:546
  183.3 18.4 %collective-permute-done.18 = bf16[512,1536]{1,0:T(8,128)(2,1)S(1)} collective-permute-done((bf16[512,1536]{1,0:T(8,128)(2,1)S(1)}, bf16[512,1536]{1,0:T(8,128)(2,1)S(1)}, u32[]{:S(2)}, u32[]{:S(2)}) %collective-permute-start.18) | collective-permute-done | bytes 1572896 | tf_op jit(solution)/shard_map/ppermute | solution.py:546
  203.4 5.7 %collective-permute-done.19.refs_1_.mid_far = bf16[1024,1536]{1,0:T(8,128)(2,1)} collective-permute-done((bf16[1024,1536]{1,0:T(8,128)(2,1)S(1)}, bf16[1024,1536]{1,0:T(8,128)(2,1)}, u32[]{:S(2)}, u32[]{:S(2)}) %collective-permute-start.19) | collective-permute-done | bytes 3145760 | tf_op jit(solution)/shard_map/ppermute | solution.py:546
  209.2 61.3 %shard_map.172 = (bf16[1024,1536]{1,0:T(8,128)(2,1)}, bf16[1024,1536]{1,0:T(8,128)(2,1)}, bf16[1024,1536]{1,0:T(8,128)(2,1)}, bf16[1024,1536]{1,0:T(8,128)(2,1)}...) custom-call(bf16[1024,1536]{1,0:T(8,128)(2,1)} %copy-done.2, ...), custom_call_target="tpu_custom_call" | custom-call | flops 1024 | bytes 1024 | tf_op jit(solution)/shard_map/pallas_call | solution.py:302
  270.6 24.9 %shard_map.173 = (bf16[1024,1536]{1,0:T(8,128)(2,1)}, bf16[1024,1536]{1,0:T(8,128)(2,1)}, bf16[1024,1536]{1,0:T(8,128)(2,1)}, bf16[1024,1536]{1,0:T(8,128)(2,1)}, bf16[2048,1152]{1,0:T(8,128)(2,1)}) custom-call(bf16[1024,1536]{1,0:T(8,128)(2,1)} %copy-done.2, bf16[1024,1536]{1,0:T(8,128)(2,1)} %collective-permute-done.19.refs_1_.mid_far, ...), custom_call_target="tpu_custom_call" | custom-call | flops 1024 | bytes 1024 | tf_op jit(solution)/shard_map/pallas_call | solution.py:302
  296.1 8.6 %collective-permute-done.21 = bf16[1024,1536]{1,0:T(8,128)(2,1)S(1)} collective-permute-done((bf16[1024,1536]{1,0:T(8,128)(2,1)}, bf16[1024,1536]{1,0:T(8,128)(2,1)S(1)}, u32[]{:S(2)}, u32[]{:S(2)}) %collective-permute-start.21) | collective-permute-done | bytes 3145760 | tf_op jit(solution)/shard_map/ppermute | solution.py:546
  304.7 3.0 add_convert_fusion.2
  310.9 13.8 %shard_map.174 = bf16[1536,1152]{1,0:T(8,128)(2,1)} custom-call(bf16[1024,1536]{1,0:T(8,128)(2,1)} %copy-done.2, bf16[1024,1536]{1,0:T(8,128)(2,1)} %collective-permute-done.19.refs_1_.mid_far, bf16[1024,1536]{1,0:T(8,128)(2,1)} %constant_dynamic-update-slice_fusion.12.refs_2_.cot_near, bf16[1024,1536]{1,0:T(8,128)(2,1)} %collective-permute-done.20.refs_3_.cot_far, ...), custom_call_target="tpu_custom_call" | custom-call | flops 1024 | bytes 1024 | tf_op jit(solution)/shard_map/pallas_call | solution.py:336
  324.7 4.9 collective-permute-done.22
  333.9 3.7 add_convert_fusion.1
  337.6 6.3 %collective-permute-done.24 = bf16[256,1536]{1,0:T(8,128)(2,1)S(1)} collective-permute-done((bf16[256,1536]{1,0:T(8,128)(2,1)S(1)}, bf16[256,1536]{1,0:T(8,128)(2,1)S(1)}, u32[]{:S(2)}, u32[]{:S(2)}) %collective-permute-start.24) | collective-permute-done | bytes 786464 | tf_op jit(solution)/shard_map/ppermute | solution.py:546
  348.3 4.9 convolution_convert_fusion.do_ref
  353.2 9.8 %shard_map.175 = (bf16[256,1536]{1,0:T(8,128)(2,1)}, bf16[1024,512]{1,0:T(8,128)(2,1)}, bf16[1024,512]{1,0:T(8,128)(2,1)}) custom-call(s32[8]{0:T(128)} %and_convert_fusion.need_ref, s32[2048,2]{1,0:T(8,128)} %copy.31.kinfo_ref, s32[8,256]{1,0:T(8,128)} %add_add_fusion.qinfo_ref, f32[64,256]{1,0:T(8,128)} %copy-done.38, ...), custom_call_target="tpu_custom_call" | custom-call | flops 1024 | bytes 1024 | tf_op jit(solution)/shard_map/pallas_call | solution.py:207
  363.1 3.0 collective-permute-start.26
  366.6 3.5 add_convert_fusion.4
  370.1 2.6 add_convert_fusion.7
  372.7 8.9 %shard_map.176 = (bf16[768,3072]{1,0:T(8,128)(2,1)}, bf16[768,3072]{1,0:T(8,128)(2,1)}) custom-call(s32[8]{0:T(128)} %stack.91.dev_ref, bf16[256,1536]{1,0:T(8,128)(2,1)} %copy-done.18, bf16[256,1536]{1,0:T(8,128)(2,1)} %get-tuple-element.100.refs_1_, bf16[256,1536]{1,0:T(8,128)(2,1)} %copy-done.31, bf16[1536,256]{1,0:T(8,128)(2,1)} %get-tuple-element.76.o_ref.refs_3_), custom_call_target="tpu_custom_call" | custom-call | flops 1024 | bytes 1024 | tf_op jit(solution)/shard_map/pallas_call | solution.py:468
  385.3 4.1 collective-permute-start.29
  390.4 5.4 %collective-permute-start.27 = (bf16[256,1536]{1,0:T(8,128)(2,1)}, bf16[256,1536]{1,0:T(8,128)(2,1)}, u32[]{:S(2)}, u32[]{:S(2)}) collective-permute-start(bf16[256,1536]{1,0:T(8,128)(2,1)} %slice.199), channel_id=1, source_target_pairs={{0,4},{1,5},{2,3},{3,2},{4,0},{5,1},{6,7},{7,6},{8,12},{9,13},{10,... | collective-permute-start | bytes 2359304 | tf_op jit(solution)/shard_map/ppermute | solution.py:546
  395.8 5.7 %add_convert_fusion = bf16[768,3072]{1,0:T(8,128)(2,1)S(1)} fusion(bf16[768,3072]{1,0:T(8,128)(2,1)} %collective-permute-done.28, bf16[768,3072]{1,0:T(8,128)(2,1)} %get-tuple-element.102), kind=kLoop, calls=%fused_computation.2 | loop fusion | flops 9437184 | bytes 14155776 | tf_op jit(solution)/shard_map/convert_element_type | solution.py:561
  421.8 5.1 fusion.5
  430.0 8.5 %collective-permute-done.31 = bf16[384,3072]{1,0:T(8,128)(2,1)} collective-permute-done((bf16[384,3072]{1,0:T(8,128)(2,1)}, bf16[384,3072]{1,0:T(8,128)(2,1)}, u32[]{:S(2)}, u32[]{:S(2)}) %collective-permute-start.31) | collective-permute-done | bytes 2359328 | tf_op jit(solution)/shard_map/ppermute | solution.py:546
  438.5 3.3 add_convert_fusion.3
  441.8 4.4 shard_map.177
  452.4 4.2 all-to-all-start.1
  456.7 9.1 %collective-permute-done.34 = bf16[384,640]{1,0:T(8,128)(2,1)} collective-permute-done((bf16[384,640]{1,0:T(8,128)(2,1)}, bf16[384,640]{1,0:T(8,128)(2,1)}, u32[]{:S(2)}, u32[]{:S(2)}) %collective-permute-start.34) | collective-permute-done | bytes 491552 | tf_op jit(solution)/shard_map/ppermute | solution.py:546
  469.4 4.9 collective-permute-done.32
  474.4 2.6 add_convert_fusion.6
  479.2 2.6 collective-permute-done.35
  485.3 2.8 pad_maximum_fusion.2
  488.1 4.5 all-to-all-start.2
  492.6 3.5 fusion.13
  496.2 18.7 %all-to-all-done.2 = bf16[8,48,2304]{2,1,0:T(8,128)(2,1)} async-done(((bf16[8,48,2304]{2,1,0:T(8,128)(2,1)}), bf16[8,48,2304]{2,1,0:T(8,128)(2,1)}, u32[]{:S(2)}, u32[]{:S(2)}) %all-to-all-start.2) | async-done | bytes 1769504 | tf_op jit(solution)/shard_map/all_to_all | solution.py:626
  514.9 4.4 shard_map.179
  (343 shorter events, 139.3 us)
Async XLA Ops:
  12.8 36.8 %collective-permute-start.2 = (bf16[48,3712]{1,0:T(8,128)(2,1)}, bf16[48,3712]{1,0:T(8,128)(2,1)}, u32[]{:S(2)}, u32[]{:S(2)}) collective-permute-start(bf16[48,3712]{1,0:T(8,128)(2,1)} %concatenate.98), channel_id=1, source_target_pairs={{0,24},{8,0},{16,8},{24,16},{1,25},{9,1},{17,9},{25,17},{2,26},{10... | collective-permute-start | bytes 1069064 | tf_op jit(solution)/shard_map/ppermute | solution.py:667
  17.9 30.7 %collective-permute-start.1 = (bf16[48,3712]{1,0:T(8,128)(2,1)}, bf16[48,3712]{1,0:T(8,128)(2,1)}, u32[]{:S(2)}, u32[]{:S(2)}) collective-permute-start(bf16[48,3712]{1,0:T(8,128)(2,1)} %concatenate.98), channel_id=1, source_target_pairs={{0,16},{8,24},{16,0},{24,8},{1,17},{9,25},{17,1},{25,9},{2,18},{10... | collective-permute-start | bytes 1069064 | tf_op jit(solution)/shard_map/ppermute | solution.py:667
  17.9 24.2 %collective-permute-start = (bf16[48,3712]{1,0:T(8,128)(2,1)}, bf16[48,3712]{1,0:T(8,128)(2,1)}, u32[]{:S(2)}, u32[]{:S(2)}) collective-permute-start(bf16[48,3712]{1,0:T(8,128)(2,1)} %concatenate.98), channel_id=1, source_target_pairs={{0,8},{8,16},{16,24},{24,0},{1,9},{9,17},{17,25},{25,1},{2,10},{10... | collective-permute-start | bytes 1069064 | tf_op jit(solution)/shard_map/ppermute | solution.py:667
  22.4 35.6 %all-to-all-start = ((bf16[8,48,3456]{2,1,0:T(8,128)(2,1)}), bf16[8,48,3456]{2,1,0:T(8,128)(2,1)S(1)}, u32[]{:S(2)}, u32[]{:S(2)}) async-start(bf16[8,48,3456]{2,1,0:T(8,128)(2,1)} %bitcast.109), calls=%async_computation | async-start | bytes 5308416 | tf_op jit(solution)/shard_map/all_to_all | solution.py:626
  26.2 177.1 %all-gather.4.cloned.1.call-start = ((), (), s32[]{:S(2)}) async-start(), calls=%async_computation.7 | async-start | bytes 4423680 | tf_op jit(solution)/shard_map/all_gather | solution.py:629
  36.1 111.1 %copy-start.38 = (f32[64,256]{1,0:T(8,128)}, f32[64,256]{1,0:T(8,128)S(1)}, u32[]{:S(2)}) copy-start(f32[64,256]{1,0:T(8,128)S(1)} %get-tuple-element.176.cos_ref) | copy-start | bytes 196612
  38.0 45.9 %copy-start.35 = (f32[256,64]{1,0:T(8,128)}, f32[256,64]{1,0:T(8,128)S(1)}, u32[]{:S(2)}) copy-start(f32[256,64]{1,0:T(8,128)S(1)} %get-tuple-element.175) | copy-start | bytes 196612
  51.7 10.0 %collective-permute-start.3 = (bf16[192,640]{1,0:T(8,128)(2,1)S(1)}, bf16[192,640]{1,0:T(8,128)(2,1)S(1)}, u32[]{:S(2)}, u32[]{:S(2)}) collective-permute-start(bf16[192,640]{1,0:T(8,128)(2,1)S(1)} %slice.222), channel_id=1, source_target_pairs={{0,4},{1,5},{2,3},{3,2},{4,0},{5,1},{6,7},{7,6},{8,12},{9,13},{10,... | collective-permute-start | bytes 737288 | tf_op jit(solution)/shard_map/ppermute | solution.py:546
  59.6 143.8 %all-gather.8.cloned.1.call-start = ((), (), s32[]{:S(2)}) async-start(), calls=%async_computation.9 | async-start | bytes 4423680 | tf_op jit(solution)/shard_map/all_gather | solution.py:629
  61.8 13.8 %collective-permute-start.7 = (bf16[384,640]{1,0:T(8,128)(2,1)S(1)}, bf16[384,640]{1,0:T(8,128)(2,1)S(1)}, u32[]{:S(2)}, u32[]{:S(2)}) collective-permute-start(bf16[384,640]{1,0:T(8,128)(2,1)S(1)} %pad_maximum_fusion.9), channel_id=1, source_target_pairs={{0,1},{1,0},{2,6},{3,7},{4,5},{5,4},{6,2},{7,3},{8,9},{9,8},{10,14... | collective-permute-start | bytes 1474568 | tf_op jit(solution)/shard_map/ppermute | solution.py:546
  63.4 13.2 %collective-permute-start.4 = (bf16[192,1536]{1,0:T(8,128)(2,1)S(1)}, bf16[192,1536]{1,0:T(8,128)(2,1)S(1)}, u32[]{:S(2)}, u32[]{:S(2)}) collective-permute-start(bf16[192,1536]{1,0:T(8,128)(2,1)S(1)} %get-tuple-element.67), channel_id=1, source_target_pairs={{0,4},{1,5},{2,3},{3,2},{4,0},{5,1},{6,7},{7,6},{8,12},{9,13},{10,... | collective-permute-start | bytes 1769480 | tf_op jit(solution)/shard_map/ppermute | solution.py:546
  75.7 3.2 collective-permute-start.8
  77.7 16.5 %collective-permute-start.5 = (bf16[384,1536]{1,0:T(8,128)(2,1)}, bf16[384,1536]{1,0:T(8,128)(2,1)}, u32[]{:S(2)}, u32[]{:S(2)}) collective-permute-start(bf16[384,1536]{1,0:T(8,128)(2,1)} %pad_maximum_fusion.5), channel_id=1, source_target_pairs={{0,1},{1,0},{2,6},{3,7},{4,5},{5,4},{6,2},{7,3},{8,9},{9,8},{10,14... | collective-permute-start | bytes 3538952 | tf_op jit(solution)/shard_map/ppermute | solution.py:546
  96.6 6.7 %collective-permute-start.9 = (bf16[256,512]{1,0:T(8,128)(2,1)}, bf16[256,512]{1,0:T(8,128)(2,1)}, u32[]{:S(2)}, u32[]{:S(2)}) collective-permute-start(bf16[256,512]{1,0:T(8,128)(2,1)} %pad_maximum_fusion.10), channel_id=1, source_target_pairs={{0,4},{1,5},{2,3},{3,2},{4,0},{5,1},{6,7},{7,6},{8,12},{9,13},{10,... | collective-permute-start | bytes 786440 | tf_op jit(solution)/shard_map/ppermute | solution.py:546
  97.6 12.0 %collective-permute-start.6 = (bf16[192,1536]{1,0:T(8,128)(2,1)S(1)}, bf16[192,1536]{1,0:T(8,128)(2,1)}, u32[]{:S(2)}, u32[]{:S(2)}) collective-permute-start(bf16[192,1536]{1,0:T(8,128)(2,1)S(1)} %copy-done.34), channel_id=1, source_target_pairs={{0,4},{1,5},{2,3},{3,2},{4,0},{5,1},{6,7},{7,6},{8,12},{9,13},{10,... | collective-permute-start | bytes 1769480 | tf_op jit(solution)/shard_map/ppermute | solution.py:546
  101.2 169.4 %all-gather.6.cloned.1.call-start = ((), (), s32[]{:S(2)}) async-start(), calls=%async_computation.8 | async-start | bytes 4423680 | tf_op jit(solution)/shard_map/all_gather | solution.py:629
  101.5 40.3 %collective-permute-start.12 = (bf16[768,1536]{1,0:T(8,128)(2,1)}, bf16[768,1536]{1,0:T(8,128)(2,1)}, u32[]{:S(2)}, u32[]{:S(2)}) collective-permute-start(bf16[768,1536]{1,0:T(8,128)(2,1)} %constant_dynamic-update-slice_fusion), channel_id=1, source_target_pairs={{0,2},{1,3},{2,0},{3,1},{4,6},{5,7},{6,4},{7,5},{8,10},{9,11},{10,... | collective-permute-start | bytes 7077896 | tf_op jit(solution)/shard_map/ppermute | solution.py:546
  110.7 9.6 %collective-permute-start.10 = (bf16[512,512]{1,0:T(8,128)(2,1)}, bf16[512,512]{1,0:T(8,128)(2,1)}, u32[]{:S(2)}, u32[]{:S(2)}) collective-permute-start(bf16[512,512]{1,0:T(8,128)(2,1)} %pad_maximum_fusion.8), channel_id=1, source_target_pairs={{0,1},{1,0},{2,6},{3,7},{4,5},{5,4},{6,2},{7,3},{8,9},{9,8},{10,14... | collective-permute-start | bytes 1572872 | tf_op jit(solution)/shard_map/ppermute | solution.py:546
  121.4 20.3 %collective-permute-start.13 = (bf16[1024,512]{1,0:T(8,128)(2,1)S(1)}, bf16[1024,512]{1,0:T(8,128)(2,1)S(1)}, u32[]{:S(2)}, u32[]{:S(2)}) collective-permute-start(bf16[1024,512]{1,0:T(8,128)(2,1)S(1)} %get-tuple-element.160), channel_id=1, source_target_pairs={{0,2},{1,3},{2,0},{3,1},{4,6},{5,7},{6,4},{7,5},{8,10},{9,11},{10,... | collective-permute-start | bytes 3145736 | tf_op jit(solution)/shard_map/ppermute | solution.py:546
  121.5 18.5 %collective-permute-start.11 = (bf16[256,1536]{1,0:T(8,128)(2,1)S(1)}, bf16[256,1536]{1,0:T(8,128)(2,1)S(1)}, u32[]{:S(2)}, u32[]{:S(2)}) collective-permute-start(bf16[256,1536]{1,0:T(8,128)(2,1)S(1)} %copy-done.11), channel_id=1, source_target_pairs={{0,4},{1,5},{2,3},{3,2},{4,0},{5,1},{6,7},{7,6},{8,12},{9,13},{10,... | collective-permute-start | bytes 2359304 | tf_op jit(solution)/shard_map/ppermute | solution.py:546
  124.0 31.0 %collective-permute-start.15 = (bf16[384,1536]{1,0:T(8,128)(2,1)S(1)}, bf16[384,1536]{1,0:T(8,128)(2,1)S(1)}, u32[]{:S(2)}, u32[]{:S(2)}) collective-permute-start(bf16[384,1536]{1,0:T(8,128)(2,1)S(1)} %constant_dynamic-update-slice_fusion.3), channel_id=1, source_target_pairs={{0,1},{1,0},{2,6},{3,7},{4,5},{5,4},{6,2},{7,3},{8,9},{9,8},{10,14... | collective-permute-start | bytes 3538952 | tf_op jit(solution)/shard_map/ppermute | solution.py:546
  140.1 22.4 %collective-permute-start.14 = (bf16[512,1536]{1,0:T(8,128)(2,1)S(1)}, bf16[512,1536]{1,0:T(8,128)(2,1)S(1)}, u32[]{:S(2)}, u32[]{:S(2)}) collective-permute-start(bf16[512,1536]{1,0:T(8,128)(2,1)S(1)} %constant_dynamic-update-slice_fusion.7), channel_id=1, source_target_pairs={{0,1},{1,0},{2,6},{3,7},{4,5},{5,4},{6,2},{7,3},{8,9},{9,8},{10,14... | collective-permute-start | bytes 4718600 | tf_op jit(solution)/shard_map/ppermute | solution.py:546
  155.2 8.6 %collective-permute-start.16 = (bf16[768,1536]{1,0:T(8,128)(2,1)S(1)}, bf16[768,1536]{1,0:T(8,128)(2,1)S(1)}, u32[]{:S(2)}, u32[]{:S(2)}) collective-permute-start(bf16[768,1536]{1,0:T(8,128)(2,1)S(1)} %pad_maximum_fusion.1), channel_id=1, source_target_pairs={{0,2},{1,3},{2,0},{3,1},{4,6},{5,7},{6,4},{7,5},{8,10},{9,11},{10,... | collective-permute-start | bytes 7077896 | tf_op jit(solution)/shard_map/ppermute | solution.py:546
  169.0 12.1 %collective-permute-start.17 = (bf16[256,1536]{1,0:T(8,128)(2,1)S(1)}, bf16[256,1536]{1,0:T(8,128)(2,1)S(1)}, u32[]{:S(2)}, u32[]{:S(2)}) collective-permute-start(bf16[256,1536]{1,0:T(8,128)(2,1)S(1)} %multiply_convert_fusion), channel_id=1, source_target_pairs={{0,4},{1,5},{2,3},{3,2},{4,0},{5,1},{6,7},{7,6},{8,12},{9,13},{10,... | collective-permute-start | bytes 2359304 | tf_op jit(solution)/shard_map/ppermute | solution.py:546
  170.1 177.2 %reduce-scatter.5.cloned.1.call-start = ((), (), s32[]{:S(2)}) async-start(), calls=%async_computation.10 | async-start | bytes 4423680 | tf_op jit(solution)/shard_map/reduce_scatter | solution.py:632
  181.1 20.5 %collective-permute-start.18 = (bf16[512,1536]{1,0:T(8,128)(2,1)S(1)}, bf16[512,1536]{1,0:T(8,128)(2,1)S(1)}, u32[]{:S(2)}, u32[]{:S(2)}) collective-permute-start(bf16[512,1536]{1,0:T(8,128)(2,1)S(1)} %pad_maximum_fusion.3), channel_id=1, source_target_pairs={{0,1},{1,0},{2,6},{3,7},{4,5},{5,4},{6,2},{7,3},{8,9},{9,8},{10,14... | collective-permute-start | bytes 4718600 | tf_op jit(solution)/shard_map/ppermute | solution.py:546
  183.3 20.1 %collective-permute-start.20 = (bf16[1024,1536]{1,0:T(8,128)(2,1)}, bf16[1024,1536]{1,0:T(8,128)(2,1)}, u32[]{:S(2)}, u32[]{:S(2)}) collective-permute-start(bf16[1024,1536]{1,0:T(8,128)(2,1)} %constant_dynamic-update-slice_fusion.12.refs_2_.cot_near), channel_id=1, source_target_pairs={{0,2},{1,3},{2,0},{3,1},{4,6},{5,7},{6,4},{7,5},{8,10},{9,11},{10,... | collective-permute-start | bytes 9437192 | tf_op jit(solution)/shard_map/ppermute | solution.py:546
  203.3 5.9 %collective-permute-start.19 = (bf16[1024,1536]{1,0:T(8,128)(2,1)S(1)}, bf16[1024,1536]{1,0:T(8,128)(2,1)}, u32[]{:S(2)}, u32[]{:S(2)}) collective-permute-start(bf16[1024,1536]{1,0:T(8,128)(2,1)S(1)} %pad_maximum_fusion.refs_0_.mid_near), channel_id=1, source_target_pairs={{0,2},{1,3},{2,0},{3,1},{4,6},{5,7},{6,4},{7,5},{8,10},{9,11},{10,... | collective-permute-start | bytes 9437192 | tf_op jit(solution)/shard_map/ppermute | solution.py:546
  270.5 135.1 %reduce-scatter.7.cloned.1.call-start = ((), (), s32[]{:S(2)}) async-start(), calls=%async_computation.11 | async-start | bytes 4423680 | tf_op jit(solution)/shard_map/reduce_scatter | solution.py:632
  295.5 9.2 %collective-permute-start.21 = (bf16[1024,1536]{1,0:T(8,128)(2,1)}, bf16[1024,1536]{1,0:T(8,128)(2,1)S(1)}, u32[]{:S(2)}, u32[]{:S(2)}) collective-permute-start(bf16[1024,1536]{1,0:T(8,128)(2,1)} %get-tuple-element.86), channel_id=1, source_target_pairs={{0,2},{1,3},{2,0},{3,1},{4,6},{5,7},{6,4},{7,5},{8,10},{9,11},{10,... | collective-permute-start | bytes 9437192 | tf_op jit(solution)/shard_map/ppermute | solution.py:546
  295.7 38.2 %collective-permute-start.23 = (bf16[1024,1536]{1,0:T(8,128)(2,1)}, bf16[1024,1536]{1,0:T(8,128)(2,1)}, u32[]{:S(2)}, u32[]{:S(2)}) collective-permute-start(bf16[1024,1536]{1,0:T(8,128)(2,1)} %get-tuple-element.91), channel_id=1, source_target_pairs={{0,2},{1,3},{2,0},{3,1},{4,6},{5,7},{6,4},{7,5},{8,10},{9,11},{10,... | collective-permute-start | bytes 9437192 | tf_op jit(solution)/shard_map/ppermute | solution.py:546
  309.1 20.5 %collective-permute-start.22 = (bf16[512,1536]{1,0:T(8,128)(2,1)S(1)}, bf16[512,1536]{1,0:T(8,128)(2,1)}, u32[]{:S(2)}, u32[]{:S(2)}) collective-permute-start(bf16[512,1536]{1,0:T(8,128)(2,1)S(1)} %get-tuple-element.129), channel_id=1, source_target_pairs={{0,1},{1,0},{2,6},{3,7},{4,5},{5,4},{6,2},{7,3},{8,9},{9,8},{10,14... | collective-permute-start | bytes 4718600 | tf_op jit(solution)/shard_map/ppermute | solution.py:546
  331.9 12.1 %collective-permute-start.24 = (bf16[256,1536]{1,0:T(8,128)(2,1)S(1)}, bf16[256,1536]{1,0:T(8,128)(2,1)S(1)}, u32[]{:S(2)}, u32[]{:S(2)}) collective-permute-start(bf16[256,1536]{1,0:T(8,128)(2,1)S(1)} %slice.242), channel_id=1, source_target_pairs={{0,4},{1,5},{2,3},{3,2},{4,0},{5,1},{6,7},{7,6},{8,12},{9,13},{10,... | collective-permute-start | bytes 2359304 | tf_op jit(solution)/shard_map/ppermute | solution.py:546
  333.9 143.1 %reduce-scatter.9.cloned.1.call-start = ((), (), s32[]{:S(2)}) async-start(), calls=%async_computation.12 | async-start | bytes 4423680 | tf_op jit(solution)/shard_map/reduce_scatter | solution.py:632
  345.5 21.2 %collective-permute-start.25 = (bf16[512,1536]{1,0:T(8,128)(2,1)}, bf16[512,1536]{1,0:T(8,128)(2,1)}, u32[]{:S(2)}, u32[]{:S(2)}) collective-permute-start(bf16[512,1536]{1,0:T(8,128)(2,1)} %slice.197), channel_id=1, source_target_pairs={{0,1},{1,0},{2,6},{3,7},{4,5},{5,4},{6,2},{7,3},{8,9},{9,8},{10,14... | collective-permute-start | bytes 4718600 | tf_op jit(solution)/shard_map/ppermute | solution.py:546
  363.1 7.1 %collective-permute-start.26 = (bf16[1024,512]{1,0:T(8,128)(2,1)}, bf16[1024,512]{1,0:T(8,128)(2,1)}, u32[]{:S(2)}, u32[]{:S(2)}) collective-permute-start(bf16[1024,512]{1,0:T(8,128)(2,1)} %get-tuple-element.98), channel_id=1, source_target_pairs={{0,2},{1,3},{2,0},{3,1},{4,6},{5,7},{6,4},{7,5},{8,10},{9,11},{10,... | collective-permute-start | bytes 3145736 | tf_op jit(solution)/shard_map/ppermute | solution.py:546
  381.6 14.2 %collective-permute-start.28 = (bf16[768,3072]{1,0:T(8,128)(2,1)}, bf16[768,3072]{1,0:T(8,128)(2,1)}, u32[]{:S(2)}, u32[]{:S(2)}) collective-permute-start(bf16[768,3072]{1,0:T(8,128)(2,1)} %get-tuple-element.103), channel_id=1, source_target_pairs={{0,2},{1,3},{2,0},{3,1},{4,6},{5,7},{6,4},{7,5},{8,10},{9,11},{10,... | collective-permute-start | bytes 14155784 | tf_op jit(solution)/shard_map/ppermute | solution.py:546
  385.3 20.3 %collective-permute-start.29 = (bf16[512,512]{1,0:T(8,128)(2,1)}, bf16[512,512]{1,0:T(8,128)(2,1)}, u32[]{:S(2)}, u32[]{:S(2)}) collective-permute-start(bf16[512,512]{1,0:T(8,128)(2,1)} %get-tuple-element.152), channel_id=1, source_target_pairs={{0,1},{1,0},{2,6},{3,7},{4,5},{5,4},{6,2},{7,3},{8,9},{9,8},{10,14... | collective-permute-start | bytes 1572872 | tf_op jit(solution)/shard_map/ppermute | solution.py:546
  390.4 21.0 %collective-permute-start.27 = (bf16[256,1536]{1,0:T(8,128)(2,1)}, bf16[256,1536]{1,0:T(8,128)(2,1)}, u32[]{:S(2)}, u32[]{:S(2)}) collective-permute-start(bf16[256,1536]{1,0:T(8,128)(2,1)} %slice.199), channel_id=1, source_target_pairs={{0,4},{1,5},{2,3},{3,2},{4,0},{5,1},{6,7},{7,6},{8,12},{9,13},{10,... | collective-permute-start | bytes 2359304 | tf_op jit(solution)/shard_map/ppermute | solution.py:546
  407.1 8.8 %collective-permute-start.30 = (bf16[256,512]{1,0:T(8,128)(2,1)S(1)}, bf16[256,512]{1,0:T(8,128)(2,1)S(1)}, u32[]{:S(2)}, u32[]{:S(2)}) collective-permute-start(bf16[256,512]{1,0:T(8,128)(2,1)S(1)} %slice.246), channel_id=1, source_target_pairs={{0,4},{1,5},{2,3},{3,2},{4,0},{5,1},{6,7},{7,6},{8,12},{9,13},{10,... | collective-permute-start | bytes 786440 | tf_op jit(solution)/shard_map/ppermute | solution.py:546
  409.1 29.4 %collective-permute-start.31 = (bf16[384,3072]{1,0:T(8,128)(2,1)}, bf16[384,3072]{1,0:T(8,128)(2,1)}, u32[]{:S(2)}, u32[]{:S(2)}) collective-permute-start(bf16[384,3072]{1,0:T(8,128)(2,1)} %slice.250), channel_id=1, source_target_pairs={{0,1},{1,0},{2,6},{3,7},{4,5},{5,4},{6,2},{7,3},{8,9},{9,8},{10,14... | collective-permute-start | bytes 7077896 | tf_op jit(solution)/shard_map/ppermute | solution.py:546
  446.2 3.5 collective-permute-start.33
  447.8 26.5 %collective-permute-start.32 = (bf16[192,3072]{1,0:T(8,128)(2,1)}, bf16[192,3072]{1,0:T(8,128)(2,1)}, u32[]{:S(2)}, u32[]{:S(2)}) collective-permute-start(bf16[192,3072]{1,0:T(8,128)(2,1)} %slice.252), channel_id=1, source_target_pairs={{0,4},{1,5},{2,3},{3,2},{4,0},{5,1},{6,7},{7,6},{8,12},{9,13},{10,... | collective-permute-start | bytes 3538952 | tf_op jit(solution)/shard_map/ppermute | solution.py:546
  451.2 14.6 %collective-permute-start.34 = (bf16[384,640]{1,0:T(8,128)(2,1)}, bf16[384,640]{1,0:T(8,128)(2,1)}, u32[]{:S(2)}, u32[]{:S(2)}) collective-permute-start(bf16[384,640]{1,0:T(8,128)(2,1)} %slice.254), channel_id=1, source_target_pairs={{0,1},{1,0},{2,6},{3,7},{4,5},{5,4},{6,2},{7,3},{8,9},{9,8},{10,14... | collective-permute-start | bytes 1474568 | tf_op jit(solution)/shard_map/ppermute | solution.py:546
  452.4 26.8 %all-to-all-start.1 = ((bf16[8,48,1152]{2,1,0:T(8,128)(2,1)}), bf16[8,48,1152]{2,1,0:T(8,128)(2,1)}, u32[]{:S(2)}, u32[]{:S(2)}) async-start(bf16[8,48,1152]{2,1,0:T(8,128)(2,1)} %bitcast.154), calls=%async_computation.4 | async-start | bytes 1769472 | tf_op jit(solution)/shard_map/all_to_all | solution.py:626
  456.7 62.6 %reduce-scatter.11.cloned.1.call-start = ((), (), s32[]{:S(2)}) async-start(), calls=%async_computation.13 | async-start | bytes 1781760 | tf_op jit(solution)/shard_map/reduce_scatter | solution.py:632
  467.8 14.0 %collective-permute-start.35 = (bf16[192,640]{1,0:T(8,128)(2,1)}, bf16[192,640]{1,0:T(8,128)(2,1)}, u32[]{:S(2)}, u32[]{:S(2)}) collective-permute-start(bf16[192,640]{1,0:T(8,128)(2,1)} %get-tuple-element.166), channel_id=1, source_target_pairs={{0,4},{1,5},{2,3},{3,2},{4,0},{5,1},{6,7},{7,6},{8,12},{9,13},{10,... | collective-permute-start | bytes 737288 | tf_op jit(solution)/shard_map/ppermute | solution.py:546
  488.1 26.8 %all-to-all-start.2 = ((bf16[8,48,2304]{2,1,0:T(8,128)(2,1)}), bf16[8,48,2304]{2,1,0:T(8,128)(2,1)}, u32[]{:S(2)}, u32[]{:S(2)}) async-start(bf16[8,48,2304]{2,1,0:T(8,128)(2,1)} %bitcast.117), calls=%async_computation.6 | async-start | bytes 3538944 | tf_op jit(solution)/shard_map/all_to_all | solution.py:626
  (55 other events, 315.7 us)
Sparse Core Ops, SparseCore 0:
  59.7 69.4 all-gather.3
  130.8 68.5 all-gather.7
  201.0 68.5 all-gather.5
  271.7 64.9 reduce-scatter.4
  338.9 66.6 reduce-scatter.6
  407.8 66.6 reduce-scatter.8
  485.5 32.8 reduce-scatter.10

commit v2 on v1

--- a/solution.py
+++ b/solution.py
@@ -803,6 +803,7 @@
         need, kinfo, qinfo, cos_t, sin_t, query_t, kv_all, attended_t, attended_grad_t, lse
     )
     kv_fold = plane.fold(*kv_grads, plane.steps)
+    first_swapped = [swap_rows(after(array, mid_fold)) for array in chunk_sums[:-1][:1]]
     mlp_out = after(out_fold, mid_fold)
     for step in range(plane.steps - 1, 0, -1):
         mlp_out = plane.fold_rest(mlp_out, step)
@@ -810,7 +811,7 @@
         plane,
         local_rows,
         [
-            (after(normed_in, mlp_out, kv_fold), query_grad, False),
+            (after(normed_in, mlp_out, kv_fold, *first_swapped), query_grad, False),
             (middle_low, attended_t, True),
         ],
     )
@@ -832,7 +833,6 @@
     in_grad = dot(projected_grad[:, :q_width], w_q_all, 1, 1) + dot(
         projected_grad[:, q_width:], w_kv_all[:, : 2 * kv_width], 1, 1
     )
-    first_swapped = [swap_rows(after(array, in_grad)) for array in chunk_sums[:-1][:1]]
     gain_attn_grad = jnp.sum(in_grad * (inputs * in_inverse), axis=0)
     input_grad = middle_grad + norm_backward(inputs, in_inverse, in_grad * gain_attn)
     qkv_bias_grad = jnp.sum(projected_grad.astype(F32), axis=0)
@@ -862,7 +862,7 @@
         rows = small_fold.shape[0] // 2
         kept, sent = small_fold[:rows], small_fold[rows:]
         if step == 0:
-            kept = after(kept, chunk_sums[-1], *first_swapped)
+            kept = after(kept, chunk_sums[-1])
         small_fold = plane.fold(kept, sent, step)
     attn_plane = jnp.concatenate([big_fold, small_fold], axis=1)
     grad_qkv, grad_out, grad_gain_attn, grad_gain_mlp, grad_bias = spread_sums(

time: 536 us -> 534 us (level)
  waiting for transfers between devices: 167 us -> 176 us
  starting transfers between devices: 63.2 us -> 54.3 us
    ppermute x33, starting transfers between devices: 44.1 us -> 30 us  [swap(): return lax.ppermute(array, PLANE, pairs)]
    unnamed x125 -> x119, local copies, waits for them, and re-layouts: 16.1 us -> 16 us
  transfers between devices with their start and end apart: 46 -> 46, of which waited for: 25 -> 27; matrix products, arithmetic and copies ran while one was open for 23% -> 22% of each run, Pallas kernels for 26% -> 27%
where the time goes in v2:
time: 534 us; the launch traced here: 527 us
  waiting for transfers between devices  176 us (33%)
  Pallas kernels  142 us (27%)
  other arithmetic  60.9 us (11%)
  local copies, waits for them, and re-layouts  59.4 us (11%)
  starting transfers between devices  54.3 us (10%)
  between operations  18.6 us (3%)
  matrix products  15.7 us (3%)
    ppermute x33, waiting for transfers between devices, swap(): return lax.ppermute(array, PLANE, pairs)  136 us
    pallas_call x2, Pallas kernels, feed_forward(): pl.pallas_call(functools.partial(ffn_kernel, cols, count, not sums, with_...  86.5 us
    all_to_all x3, waiting for transfers between devices, swap_rows(): return lax.all_to_all(array, PLANE, split_axis=0, concat_axis=0, tiled=True)  30.9 us
    ppermute x33, starting transfers between devices, swap(): return lax.ppermute(array, PLANE, pairs)  30 us
    convert_element_type x14, other arithmetic, fold(): return (near.astype(F32) + self.swap(far, step).astype(F32)).astype(BF16)  28.6 us
    all_to_all x3, starting transfers between devices, swap_rows(): return lax.all_to_all(array, PLANE, split_axis=0, concat_axis=0, tiled=True)  17.5 us
    unnamed x119, local copies, waits for them, and re-layouts  16 us
    dot_general x6, matrix products, dot(): lax.dot_general(left, right, (((left_dim,), (right_dim,)), ((), ())), pre...  15.7 us
  transfers between devices with their start and end apart: 46, of which 27 were waited for; matrix products, arithmetic and copies ran while one was open for 22% of the time, Pallas kernels for 27%

profile of v2, /device:TPU:0, one launch (start us, length us, event | category | flops | bytes accessed | tf_op | source)
XLA Modules:
  0.0 527.4 jit_solution(3429281536484555668)
XLA Ops:
  12.8 5.0 collective-permute-start.2
  18.9 3.5 shard_map.170
  22.4 3.9 all-to-all-start
  37.9 4.2 collective-permute-done
  43.1 5.5 %collective-permute-done.1 = bf16[48,3712]{1,0:T(8,128)(2,1)} collective-permute-done((bf16[48,3712]{1,0:T(8,128)(2,1)}, bf16[48,3712]{1,0:T(8,128)(2,1)}, u32[]{:S(2)}, u32[]{:S(2)}) %collective-permute-start.1) | collective-permute-done | bytes 356384 | tf_op jit(solution)/shard_map/ppermute | solution.py:667
  53.2 4.8 all-to-all-done
  64.3 11.4 %collective-permute-done.7 = bf16[384,640]{1,0:T(8,128)(2,1)S(1)} collective-permute-done((bf16[384,640]{1,0:T(8,128)(2,1)S(1)}, bf16[384,640]{1,0:T(8,128)(2,1)S(1)}, u32[]{:S(2)}, u32[]{:S(2)}) %collective-permute-start.7) | collective-permute-done | bytes 491552 | tf_op jit(solution)/shard_map/ppermute | solution.py:546
  86.6 7.6 %collective-permute-done.5 = bf16[384,1536]{1,0:T(8,128)(2,1)} collective-permute-done((bf16[384,1536]{1,0:T(8,128)(2,1)}, bf16[384,1536]{1,0:T(8,128)(2,1)}, u32[]{:S(2)}, u32[]{:S(2)}) %collective-permute-start.5) | collective-permute-done | bytes 1179680 | tf_op jit(solution)/shard_map/ppermute | solution.py:546
  94.3 2.4 constant_dynamic-update-slice_fusion
  105.3 4.5 collective-permute-done.6
  116.9 3.5 collective-permute-done.10
  125.0 15.1 %collective-permute-done.11 = bf16[256,1536]{1,0:T(8,128)(2,1)S(1)} collective-permute-done((bf16[256,1536]{1,0:T(8,128)(2,1)S(1)}, bf16[256,1536]{1,0:T(8,128)(2,1)S(1)}, u32[]{:S(2)}, u32[]{:S(2)}) %collective-permute-start.11) | collective-permute-done | bytes 786464 | tf_op jit(solution)/shard_map/ppermute | solution.py:546
  141.9 2.5 fusion.37
  148.6 8.1 %shard_map.171 = (bf16[1536,256]{1,0:T(8,128)(2,1)}, f32[8,1536]{1,0:T(8,128)}) custom-call(s32[8]{0:T(128)} %and_convert_fusion.need_ref, s32[2048,2]{1,0:T(8,128)} %copy.31.kinfo_ref, s32[8,256]{1,0:T(8,128)} %add_add_fusion.qinfo_ref, bf16[1536,256]{1,0:T(8,128)(2,1)} %bitcast.118, bf16[2048,512]{1,0:T(8,128)(2,1)} %copy-done.7), custom_call_target="tpu_custom_call" | custom-call | flops 1024 | bytes 1024 | tf_op jit(solution)/shard_map/pallas_call | solution.py:186
  159.1 3.5 collective-permute-done.14
  170.3 10.9 %collective-permute-done.17 = bf16[256,1536]{1,0:T(8,128)(2,1)S(1)} collective-permute-done((bf16[256,1536]{1,0:T(8,128)(2,1)S(1)}, bf16[256,1536]{1,0:T(8,128)(2,1)S(1)}, u32[]{:S(2)}, u32[]{:S(2)}) %collective-permute-start.17) | collective-permute-done | bytes 786464 | tf_op jit(solution)/shard_map/ppermute | solution.py:546
  181.3 2.7 collective-permute-start.18
  183.9 18.4 %collective-permute-done.18 = bf16[512,1536]{1,0:T(8,128)(2,1)S(1)} collective-permute-done((bf16[512,1536]{1,0:T(8,128)(2,1)S(1)}, bf16[512,1536]{1,0:T(8,128)(2,1)S(1)}, u32[]{:S(2)}, u32[]{:S(2)}) %collective-permute-start.18) | collective-permute-done | bytes 1572896 | tf_op jit(solution)/shard_map/ppermute | solution.py:546
  204.1 5.7 %collective-permute-done.19.refs_1_.mid_far = bf16[1024,1536]{1,0:T(8,128)(2,1)} collective-permute-done((bf16[1024,1536]{1,0:T(8,128)(2,1)S(1)}, bf16[1024,1536]{1,0:T(8,128)(2,1)}, u32[]{:S(2)}, u32[]{:S(2)}) %collective-permute-start.19) | collective-permute-done | bytes 3145760 | tf_op jit(solution)/shard_map/ppermute | solution.py:546
  209.8 61.5 %shard_map.172 = (bf16[1024,1536]{1,0:T(8,128)(2,1)}, bf16[1024,1536]{1,0:T(8,128)(2,1)}, bf16[1024,1536]{1,0:T(8,128)(2,1)}, bf16[1024,1536]{1,0:T(8,128)(2,1)}...) custom-call(bf16[1024,1536]{1,0:T(8,128)(2,1)} %copy-done.2, ...), custom_call_target="tpu_custom_call" | custom-call | flops 1024 | bytes 1024 | tf_op jit(solution)/shard_map/pallas_call | solution.py:302
  271.4 25.0 %shard_map.173 = (bf16[1024,1536]{1,0:T(8,128)(2,1)}, bf16[1024,1536]{1,0:T(8,128)(2,1)}, bf16[1024,1536]{1,0:T(8,128)(2,1)}, bf16[1024,1536]{1,0:T(8,128)(2,1)}, bf16[2048,1152]{1,0:T(8,128)(2,1)}) custom-call(bf16[1024,1536]{1,0:T(8,128)(2,1)} %copy-done.2, bf16[1024,1536]{1,0:T(8,128)(2,1)} %collective-permute-done.19.refs_1_.mid_far, ...), custom_call_target="tpu_custom_call" | custom-call | flops 1024 | bytes 1024 | tf_op jit(solution)/shard_map/pallas_call | solution.py:302
  297.0 8.2 %collective-permute-done.21 = bf16[1024,1536]{1,0:T(8,128)(2,1)S(1)} collective-permute-done((bf16[1024,1536]{1,0:T(8,128)(2,1)}, bf16[1024,1536]{1,0:T(8,128)(2,1)S(1)}, u32[]{:S(2)}, u32[]{:S(2)}) %collective-permute-start.21) | collective-permute-done | bytes 3145760 | tf_op jit(solution)/shard_map/ppermute | solution.py:546
  305.2 2.9 add_convert_fusion.2
  311.9 13.9 %shard_map.174 = bf16[1536,1152]{1,0:T(8,128)(2,1)} custom-call(bf16[1024,1536]{1,0:T(8,128)(2,1)} %copy-done.2, bf16[1024,1536]{1,0:T(8,128)(2,1)} %collective-permute-done.19.refs_1_.mid_far, bf16[1024,1536]{1,0:T(8,128)(2,1)} %constant_dynamic-update-slice_fusion.12.refs_2_.cot_near, bf16[1024,1536]{1,0:T(8,128)(2,1)} %collective-permute-done.20.refs_3_.cot_far, ...), custom_call_target="tpu_custom_call" | custom-call | flops 1024 | bytes 1024 | tf_op jit(solution)/shard_map/pallas_call | solution.py:336
  325.7 4.6 collective-permute-done.22
  333.1 3.8 add_convert_fusion.1
  336.9 7.8 %collective-permute-done.24 = bf16[256,1536]{1,0:T(8,128)(2,1)S(1)} collective-permute-done((bf16[256,1536]{1,0:T(8,128)(2,1)S(1)}, bf16[256,1536]{1,0:T(8,128)(2,1)S(1)}, u32[]{:S(2)}, u32[]{:S(2)}) %collective-permute-start.24) | collective-permute-done | bytes 786464 | tf_op jit(solution)/shard_map/ppermute | solution.py:546
  349.3 4.9 convolution_convert_fusion.do_ref
  354.2 11.9 %shard_map.175 = (bf16[256,1536]{1,0:T(8,128)(2,1)}, bf16[1024,512]{1,0:T(8,128)(2,1)}, bf16[1024,512]{1,0:T(8,128)(2,1)}) custom-call(s32[8]{0:T(128)} %and_convert_fusion.need_ref, s32[2048,2]{1,0:T(8,128)} %copy.31.kinfo_ref, s32[8,256]{1,0:T(8,128)} %add_add_fusion.qinfo_ref, f32[64,256]{1,0:T(8,128)} %copy-done.35, ...), custom_call_target="tpu_custom_call" | custom-call | flops 1024 | bytes 1024 | tf_op jit(solution)/shard_map/pallas_call | solution.py:207
  366.8 9.1 %all-to-all-start.1 = ((bf16[8,48,1152]{2,1,0:T(8,128)(2,1)}), bf16[8,48,1152]{2,1,0:T(8,128)(2,1)}, u32[]{:S(2)}, u32[]{:S(2)}) async-start(bf16[8,48,1152]{2,1,0:T(8,128)(2,1)} %bitcast.154), calls=%async_computation.2 | async-start | bytes 1769472 | tf_op jit(solution)/shard_map/all_to_all | solution.py:626
  376.0 3.6 add_convert_fusion.4
  379.5 2.6 add_convert_fusion.7
  382.1 7.5 %all-to-all-done.1 = bf16[8,48,1152]{2,1,0:T(8,128)(2,1)} async-done(((bf16[8,48,1152]{2,1,0:T(8,128)(2,1)}), bf16[8,48,1152]{2,1,0:T(8,128)(2,1)}, u32[]{:S(2)}, u32[]{:S(2)}) %all-to-all-start.1) | async-done | bytes 884768 | tf_op jit(solution)/shard_map/all_to_all | solution.py:626
  389.6 8.9 %shard_map.176 = (bf16[768,3072]{1,0:T(8,128)(2,1)}, bf16[768,3072]{1,0:T(8,128)(2,1)}) custom-call(s32[8]{0:T(128)} %stack.91.dev_ref, bf16[256,1536]{1,0:T(8,128)(2,1)} %copy-done.16, bf16[256,1536]{1,0:T(8,128)(2,1)} %get-tuple-element.100.refs_1_, bf16[256,1536]{1,0:T(8,128)(2,1)} %copy-done.28, bf16[1536,256]{1,0:T(8,128)(2,1)} %get-tuple-element.76.o_ref.refs_3_), custom_call_target="tpu_custom_call" | custom-call | flops 1024 | bytes 1024 | tf_op jit(solution)/shard_map/pallas_call | solution.py:468
  406.8 5.8 %add_convert_fusion = bf16[768,3072]{1,0:T(8,128)(2,1)S(1)} fusion(bf16[768,3072]{1,0:T(8,128)(2,1)} %collective-permute-done.28, bf16[768,3072]{1,0:T(8,128)(2,1)} %get-tuple-element.103), kind=kLoop, calls=%fused_computation.2 | loop fusion | flops 9437184 | bytes 14155776 | tf_op jit(solution)/shard_map/convert_element_type | solution.py:561
  423.5 4.1 collective-permute-done.30
  433.6 5.1 fusion.5
  441.7 7.1 %collective-permute-done.31 = bf16[384,3072]{1,0:T(8,128)(2,1)} collective-permute-done((bf16[384,3072]{1,0:T(8,128)(2,1)}, bf16[384,3072]{1,0:T(8,128)(2,1)}, u32[]{:S(2)}, u32[]{:S(2)}) %collective-permute-start.31) | collective-permute-done | bytes 2359328 | tf_op jit(solution)/shard_map/ppermute | solution.py:546
  448.9 3.3 add_convert_fusion.3
  452.2 3.3 shard_map.177
  460.4 13.0 %collective-permute-done.34 = bf16[384,640]{1,0:T(8,128)(2,1)S(1)} collective-permute-done((bf16[384,640]{1,0:T(8,128)(2,1)S(1)}, bf16[384,640]{1,0:T(8,128)(2,1)S(1)}, u32[]{:S(2)}, u32[]{:S(2)}) %collective-permute-start.34) | collective-permute-done | bytes 491552 | tf_op jit(solution)/shard_map/ppermute | solution.py:546
  475.1 3.0 collective-permute-done.32
  481.8 2.5 pad_maximum_fusion.4
  484.3 2.8 pad_maximum_fusion.2
  487.1 4.5 all-to-all-start.2
  491.7 3.5 fusion.13
  495.2 18.7 %all-to-all-done.2 = bf16[8,48,2304]{2,1,0:T(8,128)(2,1)} async-done(((bf16[8,48,2304]{2,1,0:T(8,128)(2,1)}), bf16[8,48,2304]{2,1,0:T(8,128)(2,1)}, u32[]{:S(2)}, u32[]{:S(2)}) %all-to-all-start.2) | async-done | bytes 1769504 | tf_op jit(solution)/shard_map/all_to_all | solution.py:626
  513.9 4.4 shard_map.179
  (337 shorter events, 128.4 us)
Async XLA Ops:
  12.8 36.8 %collective-permute-start.2 = (bf16[48,3712]{1,0:T(8,128)(2,1)}, bf16[48,3712]{1,0:T(8,128)(2,1)}, u32[]{:S(2)}, u32[]{:S(2)}) collective-permute-start(bf16[48,3712]{1,0:T(8,128)(2,1)} %concatenate.98), channel_id=1, source_target_pairs={{0,24},{8,0},{16,8},{24,16},{1,25},{9,1},{17,9},{25,17},{2,26},{10... | collective-permute-start | bytes 1069064 | tf_op jit(solution)/shard_map/ppermute | solution.py:667
  17.9 30.7 %collective-permute-start.1 = (bf16[48,3712]{1,0:T(8,128)(2,1)}, bf16[48,3712]{1,0:T(8,128)(2,1)}, u32[]{:S(2)}, u32[]{:S(2)}) collective-permute-start(bf16[48,3712]{1,0:T(8,128)(2,1)} %concatenate.98), channel_id=1, source_target_pairs={{0,16},{8,24},{16,0},{24,8},{1,17},{9,25},{17,1},{25,9},{2,18},{10... | collective-permute-start | bytes 1069064 | tf_op jit(solution)/shard_map/ppermute | solution.py:667
  17.9 24.2 %collective-permute-start = (bf16[48,3712]{1,0:T(8,128)(2,1)}, bf16[48,3712]{1,0:T(8,128)(2,1)}, u32[]{:S(2)}, u32[]{:S(2)}) collective-permute-start(bf16[48,3712]{1,0:T(8,128)(2,1)} %concatenate.98), channel_id=1, source_target_pairs={{0,8},{8,16},{16,24},{24,0},{1,9},{9,17},{17,25},{25,1},{2,10},{10... | collective-permute-start | bytes 1069064 | tf_op jit(solution)/shard_map/ppermute | solution.py:667
  22.4 35.6 %all-to-all-start = ((bf16[8,48,3456]{2,1,0:T(8,128)(2,1)}), bf16[8,48,3456]{2,1,0:T(8,128)(2,1)S(1)}, u32[]{:S(2)}, u32[]{:S(2)}) async-start(bf16[8,48,3456]{2,1,0:T(8,128)(2,1)} %bitcast.109), calls=%async_computation | async-start | bytes 5308416 | tf_op jit(solution)/shard_map/all_to_all | solution.py:626
  26.2 177.7 %all-gather.4.cloned.1.call-start = ((), (), s32[]{:S(2)}) async-start(), calls=%async_computation.7 | async-start | bytes 4423680 | tf_op jit(solution)/shard_map/all_gather | solution.py:629
  36.0 111.3 %copy-start.35 = (f32[64,256]{1,0:T(8,128)}, f32[64,256]{1,0:T(8,128)S(1)}, u32[]{:S(2)}) copy-start(f32[64,256]{1,0:T(8,128)S(1)} %get-tuple-element.176.cos_ref) | copy-start | bytes 196612
  37.9 46.1 %copy-start.32 = (f32[256,64]{1,0:T(8,128)}, f32[256,64]{1,0:T(8,128)S(1)}, u32[]{:S(2)}) copy-start(f32[256,64]{1,0:T(8,128)S(1)} %get-tuple-element.175) | copy-start | bytes 196612
  51.7 10.1 %collective-permute-start.3 = (bf16[192,640]{1,0:T(8,128)(2,1)S(1)}, bf16[192,640]{1,0:T(8,128)(2,1)S(1)}, u32[]{:S(2)}, u32[]{:S(2)}) collective-permute-start(bf16[192,640]{1,0:T(8,128)(2,1)S(1)} %slice.222), channel_id=1, source_target_pairs={{0,4},{1,5},{2,3},{3,2},{4,0},{5,1},{6,7},{7,6},{8,12},{9,13},{10,... | collective-permute-start | bytes 737288 | tf_op jit(solution)/shard_map/ppermute | solution.py:546
  59.6 144.4 %all-gather.8.cloned.1.call-start = ((), (), s32[]{:S(2)}) async-start(), calls=%async_computation.9 | async-start | bytes 4423680 | tf_op jit(solution)/shard_map/all_gather | solution.py:629
  61.9 13.8 %collective-permute-start.7 = (bf16[384,640]{1,0:T(8,128)(2,1)S(1)}, bf16[384,640]{1,0:T(8,128)(2,1)S(1)}, u32[]{:S(2)}, u32[]{:S(2)}) collective-permute-start(bf16[384,640]{1,0:T(8,128)(2,1)S(1)} %pad_maximum_fusion.9), channel_id=1, source_target_pairs={{0,1},{1,0},{2,6},{3,7},{4,5},{5,4},{6,2},{7,3},{8,9},{9,8},{10,14... | collective-permute-start | bytes 1474568 | tf_op jit(solution)/shard_map/ppermute | solution.py:546
  63.4 13.2 %collective-permute-start.4 = (bf16[192,1536]{1,0:T(8,128)(2,1)S(1)}, bf16[192,1536]{1,0:T(8,128)(2,1)S(1)}, u32[]{:S(2)}, u32[]{:S(2)}) collective-permute-start(bf16[192,1536]{1,0:T(8,128)(2,1)S(1)} %get-tuple-element.67), channel_id=1, source_target_pairs={{0,4},{1,5},{2,3},{3,2},{4,0},{5,1},{6,7},{7,6},{8,12},{9,13},{10,... | collective-permute-start | bytes 1769480 | tf_op jit(solution)/shard_map/ppermute | solution.py:546
  75.8 3.2 collective-permute-start.8
  77.8 16.5 %collective-permute-start.5 = (bf16[384,1536]{1,0:T(8,128)(2,1)}, bf16[384,1536]{1,0:T(8,128)(2,1)}, u32[]{:S(2)}, u32[]{:S(2)}) collective-permute-start(bf16[384,1536]{1,0:T(8,128)(2,1)} %pad_maximum_fusion.5), channel_id=1, source_target_pairs={{0,1},{1,0},{2,6},{3,7},{4,5},{5,4},{6,2},{7,3},{8,9},{9,8},{10,14... | collective-permute-start | bytes 3538952 | tf_op jit(solution)/shard_map/ppermute | solution.py:546
  96.7 6.7 %collective-permute-start.9 = (bf16[256,512]{1,0:T(8,128)(2,1)}, bf16[256,512]{1,0:T(8,128)(2,1)}, u32[]{:S(2)}, u32[]{:S(2)}) collective-permute-start(bf16[256,512]{1,0:T(8,128)(2,1)} %pad_maximum_fusion.10), channel_id=1, source_target_pairs={{0,4},{1,5},{2,3},{3,2},{4,0},{5,1},{6,7},{7,6},{8,12},{9,13},{10,... | collective-permute-start | bytes 786440 | tf_op jit(solution)/shard_map/ppermute | solution.py:546
  97.8 12.0 %collective-permute-start.6 = (bf16[192,1536]{1,0:T(8,128)(2,1)S(1)}, bf16[192,1536]{1,0:T(8,128)(2,1)}, u32[]{:S(2)}, u32[]{:S(2)}) collective-permute-start(bf16[192,1536]{1,0:T(8,128)(2,1)S(1)} %copy-done.31), channel_id=1, source_target_pairs={{0,4},{1,5},{2,3},{3,2},{4,0},{5,1},{6,7},{7,6},{8,12},{9,13},{10,... | collective-permute-start | bytes 1769480 | tf_op jit(solution)/shard_map/ppermute | solution.py:546
  101.3 170.1 %all-gather.6.cloned.1.call-start = ((), (), s32[]{:S(2)}) async-start(), calls=%async_computation.8 | async-start | bytes 4423680 | tf_op jit(solution)/shard_map/all_gather | solution.py:629
  101.5 40.4 %collective-permute-start.12 = (bf16[768,1536]{1,0:T(8,128)(2,1)}, bf16[768,1536]{1,0:T(8,128)(2,1)}, u32[]{:S(2)}, u32[]{:S(2)}) collective-permute-start(bf16[768,1536]{1,0:T(8,128)(2,1)} %constant_dynamic-update-slice_fusion), channel_id=1, source_target_pairs={{0,2},{1,3},{2,0},{3,1},{4,6},{5,7},{6,4},{7,5},{8,10},{9,11},{10,... | collective-permute-start | bytes 7077896 | tf_op jit(solution)/shard_map/ppermute | solution.py:546
  110.8 9.6 %collective-permute-start.10 = (bf16[512,512]{1,0:T(8,128)(2,1)}, bf16[512,512]{1,0:T(8,128)(2,1)}, u32[]{:S(2)}, u32[]{:S(2)}) collective-permute-start(bf16[512,512]{1,0:T(8,128)(2,1)} %pad_maximum_fusion.8), channel_id=1, source_target_pairs={{0,1},{1,0},{2,6},{3,7},{4,5},{5,4},{6,2},{7,3},{8,9},{9,8},{10,14... | collective-permute-start | bytes 1572872 | tf_op jit(solution)/shard_map/ppermute | solution.py:546
  121.5 20.3 %collective-permute-start.13 = (bf16[1024,512]{1,0:T(8,128)(2,1)S(1)}, bf16[1024,512]{1,0:T(8,128)(2,1)S(1)}, u32[]{:S(2)}, u32[]{:S(2)}) collective-permute-start(bf16[1024,512]{1,0:T(8,128)(2,1)S(1)} %get-tuple-element.160), channel_id=1, source_target_pairs={{0,2},{1,3},{2,0},{3,1},{4,6},{5,7},{6,4},{7,5},{8,10},{9,11},{10,... | collective-permute-start | bytes 3145736 | tf_op jit(solution)/shard_map/ppermute | solution.py:546
  121.6 18.5 %collective-permute-start.11 = (bf16[256,1536]{1,0:T(8,128)(2,1)S(1)}, bf16[256,1536]{1,0:T(8,128)(2,1)S(1)}, u32[]{:S(2)}, u32[]{:S(2)}) collective-permute-start(bf16[256,1536]{1,0:T(8,128)(2,1)S(1)} %copy-done.9), channel_id=1, source_target_pairs={{0,4},{1,5},{2,3},{3,2},{4,0},{5,1},{6,7},{7,6},{8,12},{9,13},{10,... | collective-permute-start | bytes 2359304 | tf_op jit(solution)/shard_map/ppermute | solution.py:546
  124.1 32.5 %collective-permute-start.15 = (bf16[384,1536]{1,0:T(8,128)(2,1)S(1)}, bf16[384,1536]{1,0:T(8,128)(2,1)S(1)}, u32[]{:S(2)}, u32[]{:S(2)}) collective-permute-start(bf16[384,1536]{1,0:T(8,128)(2,1)S(1)} %constant_dynamic-update-slice_fusion.3), channel_id=1, source_target_pairs={{0,1},{1,0},{2,6},{3,7},{4,5},{5,4},{6,2},{7,3},{8,9},{9,8},{10,14... | collective-permute-start | bytes 3538952 | tf_op jit(solution)/shard_map/ppermute | solution.py:546
  140.2 22.4 %collective-permute-start.14 = (bf16[512,1536]{1,0:T(8,128)(2,1)S(1)}, bf16[512,1536]{1,0:T(8,128)(2,1)S(1)}, u32[]{:S(2)}, u32[]{:S(2)}) collective-permute-start(bf16[512,1536]{1,0:T(8,128)(2,1)S(1)} %constant_dynamic-update-slice_fusion.7), channel_id=1, source_target_pairs={{0,1},{1,0},{2,6},{3,7},{4,5},{5,4},{6,2},{7,3},{8,9},{9,8},{10,14... | collective-permute-start | bytes 4718600 | tf_op jit(solution)/shard_map/ppermute | solution.py:546
  156.8 7.1 %collective-permute-start.16 = (bf16[768,1536]{1,0:T(8,128)(2,1)S(1)}, bf16[768,1536]{1,0:T(8,128)(2,1)S(1)}, u32[]{:S(2)}, u32[]{:S(2)}) collective-permute-start(bf16[768,1536]{1,0:T(8,128)(2,1)S(1)} %pad_maximum_fusion.1), channel_id=1, source_target_pairs={{0,2},{1,3},{2,0},{3,1},{4,6},{5,7},{6,4},{7,5},{8,10},{9,11},{10,... | collective-permute-start | bytes 7077896 | tf_op jit(solution)/shard_map/ppermute | solution.py:546
  169.1 12.1 %collective-permute-start.17 = (bf16[256,1536]{1,0:T(8,128)(2,1)S(1)}, bf16[256,1536]{1,0:T(8,128)(2,1)S(1)}, u32[]{:S(2)}, u32[]{:S(2)}) collective-permute-start(bf16[256,1536]{1,0:T(8,128)(2,1)S(1)} %multiply_convert_fusion), channel_id=1, source_target_pairs={{0,4},{1,5},{2,3},{3,2},{4,0},{5,1},{6,7},{7,6},{8,12},{9,13},{10,... | collective-permute-start | bytes 2359304 | tf_op jit(solution)/shard_map/ppermute | solution.py:546
  170.2 178.0 %reduce-scatter.5.cloned.1.call-start = ((), (), s32[]{:S(2)}) async-start(), calls=%async_computation.10 | async-start | bytes 4423680 | tf_op jit(solution)/shard_map/reduce_scatter | solution.py:632
  181.3 21.0 %collective-permute-start.18 = (bf16[512,1536]{1,0:T(8,128)(2,1)S(1)}, bf16[512,1536]{1,0:T(8,128)(2,1)S(1)}, u32[]{:S(2)}, u32[]{:S(2)}) collective-permute-start(bf16[512,1536]{1,0:T(8,128)(2,1)S(1)} %pad_maximum_fusion.3), channel_id=1, source_target_pairs={{0,1},{1,0},{2,6},{3,7},{4,5},{5,4},{6,2},{7,3},{8,9},{9,8},{10,14... | collective-permute-start | bytes 4718600 | tf_op jit(solution)/shard_map/ppermute | solution.py:546
  183.9 20.1 %collective-permute-start.20 = (bf16[1024,1536]{1,0:T(8,128)(2,1)}, bf16[1024,1536]{1,0:T(8,128)(2,1)}, u32[]{:S(2)}, u32[]{:S(2)}) collective-permute-start(bf16[1024,1536]{1,0:T(8,128)(2,1)} %constant_dynamic-update-slice_fusion.12.refs_2_.cot_near), channel_id=1, source_target_pairs={{0,2},{1,3},{2,0},{3,1},{4,6},{5,7},{6,4},{7,5},{8,10},{9,11},{10,... | collective-permute-start | bytes 9437192 | tf_op jit(solution)/shard_map/ppermute | solution.py:546
  203.9 5.9 %collective-permute-start.19 = (bf16[1024,1536]{1,0:T(8,128)(2,1)S(1)}, bf16[1024,1536]{1,0:T(8,128)(2,1)}, u32[]{:S(2)}, u32[]{:S(2)}) collective-permute-start(bf16[1024,1536]{1,0:T(8,128)(2,1)S(1)} %pad_maximum_fusion.refs_0_.mid_near), channel_id=1, source_target_pairs={{0,2},{1,3},{2,0},{3,1},{4,6},{5,7},{6,4},{7,5},{8,10},{9,11},{10,... | collective-permute-start | bytes 9437192 | tf_op jit(solution)/shard_map/ppermute | solution.py:546
  271.3 145.0 %reduce-scatter.7.cloned.1.call-start = ((), (), s32[]{:S(2)}) async-start(), calls=%async_computation.11 | async-start | bytes 4423680 | tf_op jit(solution)/shard_map/reduce_scatter | solution.py:632
  296.4 8.8 %collective-permute-start.21 = (bf16[1024,1536]{1,0:T(8,128)(2,1)}, bf16[1024,1536]{1,0:T(8,128)(2,1)S(1)}, u32[]{:S(2)}, u32[]{:S(2)}) collective-permute-start(bf16[1024,1536]{1,0:T(8,128)(2,1)} %get-tuple-element.86), channel_id=1, source_target_pairs={{0,2},{1,3},{2,0},{3,1},{4,6},{5,7},{6,4},{7,5},{8,10},{9,11},{10,... | collective-permute-start | bytes 9437192 | tf_op jit(solution)/shard_map/ppermute | solution.py:546
  296.6 36.5 %collective-permute-start.23 = (bf16[1024,1536]{1,0:T(8,128)(2,1)}, bf16[1024,1536]{1,0:T(8,128)(2,1)}, u32[]{:S(2)}, u32[]{:S(2)}) collective-permute-start(bf16[1024,1536]{1,0:T(8,128)(2,1)} %get-tuple-element.91), channel_id=1, source_target_pairs={{0,2},{1,3},{2,0},{3,1},{4,6},{5,7},{6,4},{7,5},{8,10},{9,11},{10,... | collective-permute-start | bytes 9437192 | tf_op jit(solution)/shard_map/ppermute | solution.py:546
  309.5 20.9 %collective-permute-start.22 = (bf16[512,1536]{1,0:T(8,128)(2,1)S(1)}, bf16[512,1536]{1,0:T(8,128)(2,1)}, u32[]{:S(2)}, u32[]{:S(2)}) collective-permute-start(bf16[512,1536]{1,0:T(8,128)(2,1)S(1)} %get-tuple-element.129), channel_id=1, source_target_pairs={{0,1},{1,0},{2,6},{3,7},{4,5},{5,4},{6,2},{7,3},{8,9},{9,8},{10,14... | collective-permute-start | bytes 4718600 | tf_op jit(solution)/shard_map/ppermute | solution.py:546
  332.7 12.1 %collective-permute-start.24 = (bf16[256,1536]{1,0:T(8,128)(2,1)S(1)}, bf16[256,1536]{1,0:T(8,128)(2,1)S(1)}, u32[]{:S(2)}, u32[]{:S(2)}) collective-permute-start(bf16[256,1536]{1,0:T(8,128)(2,1)S(1)} %slice.242), channel_id=1, source_target_pairs={{0,4},{1,5},{2,3},{3,2},{4,0},{5,1},{6,7},{7,6},{8,12},{9,13},{10,... | collective-permute-start | bytes 2359304 | tf_op jit(solution)/shard_map/ppermute | solution.py:546
  346.2 29.7 %collective-permute-start.25 = (bf16[512,1536]{1,0:T(8,128)(2,1)}, bf16[512,1536]{1,0:T(8,128)(2,1)}, u32[]{:S(2)}, u32[]{:S(2)}) collective-permute-start(bf16[512,1536]{1,0:T(8,128)(2,1)} %slice.197), channel_id=1, source_target_pairs={{0,1},{1,0},{2,6},{3,7},{4,5},{5,4},{6,2},{7,3},{8,9},{9,8},{10,14... | collective-permute-start | bytes 4718600 | tf_op jit(solution)/shard_map/ppermute | solution.py:546
  366.1 13.4 %collective-permute-start.26 = (bf16[1024,512]{1,0:T(8,128)(2,1)}, bf16[1024,512]{1,0:T(8,128)(2,1)}, u32[]{:S(2)}, u32[]{:S(2)}) collective-permute-start(bf16[1024,512]{1,0:T(8,128)(2,1)} %get-tuple-element.98), channel_id=1, source_target_pairs={{0,2},{1,3},{2,0},{3,1},{4,6},{5,7},{6,4},{7,5},{8,10},{9,11},{10,... | collective-permute-start | bytes 3145736 | tf_op jit(solution)/shard_map/ppermute | solution.py:546
  366.8 22.8 %all-to-all-start.1 = ((bf16[8,48,1152]{2,1,0:T(8,128)(2,1)}), bf16[8,48,1152]{2,1,0:T(8,128)(2,1)}, u32[]{:S(2)}, u32[]{:S(2)}) async-start(bf16[8,48,1152]{2,1,0:T(8,128)(2,1)} %bitcast.154), calls=%async_computation.2 | async-start | bytes 1769472 | tf_op jit(solution)/shard_map/all_to_all | solution.py:626
  375.9 103.6 %reduce-scatter.9.cloned.1.call-start = ((), (), s32[]{:S(2)}) async-start(), calls=%async_computation.12 | async-start | bytes 4423680 | tf_op jit(solution)/shard_map/reduce_scatter | solution.py:632
  398.5 8.3 %collective-permute-start.28 = (bf16[768,3072]{1,0:T(8,128)(2,1)}, bf16[768,3072]{1,0:T(8,128)(2,1)}, u32[]{:S(2)}, u32[]{:S(2)}) collective-permute-start(bf16[768,3072]{1,0:T(8,128)(2,1)} %get-tuple-element.104), channel_id=1, source_target_pairs={{0,2},{1,3},{2,0},{3,1},{4,6},{5,7},{6,4},{7,5},{8,10},{9,11},{10,... | collective-permute-start | bytes 14155784 | tf_op jit(solution)/shard_map/ppermute | solution.py:546
  399.3 119.1 %reduce-scatter.11.cloned.1.call-start = ((), (), s32[]{:S(2)}) async-start(), calls=%async_computation.13 | async-start | bytes 1781760 | tf_op jit(solution)/shard_map/reduce_scatter | solution.py:632
  402.6 14.5 %collective-permute-start.29 = (bf16[512,512]{1,0:T(8,128)(2,1)}, bf16[512,512]{1,0:T(8,128)(2,1)}, u32[]{:S(2)}, u32[]{:S(2)}) collective-permute-start(bf16[512,512]{1,0:T(8,128)(2,1)} %get-tuple-element.152), channel_id=1, source_target_pairs={{0,1},{1,0},{2,6},{3,7},{4,5},{5,4},{6,2},{7,3},{8,9},{9,8},{10,14... | collective-permute-start | bytes 1572872 | tf_op jit(solution)/shard_map/ppermute | solution.py:546
  404.1 17.1 %collective-permute-start.27 = (bf16[256,1536]{1,0:T(8,128)(2,1)}, bf16[256,1536]{1,0:T(8,128)(2,1)}, u32[]{:S(2)}, u32[]{:S(2)}) collective-permute-start(bf16[256,1536]{1,0:T(8,128)(2,1)} %slice.199), channel_id=1, source_target_pairs={{0,4},{1,5},{2,3},{3,2},{4,0},{5,1},{6,7},{7,6},{8,12},{9,13},{10,... | collective-permute-start | bytes 2359304 | tf_op jit(solution)/shard_map/ppermute | solution.py:546
  418.4 9.2 %collective-permute-start.30 = (bf16[256,512]{1,0:T(8,128)(2,1)S(1)}, bf16[256,512]{1,0:T(8,128)(2,1)S(1)}, u32[]{:S(2)}, u32[]{:S(2)}) collective-permute-start(bf16[256,512]{1,0:T(8,128)(2,1)S(1)} %slice.246), channel_id=1, source_target_pairs={{0,4},{1,5},{2,3},{3,2},{4,0},{5,1},{6,7},{7,6},{8,12},{9,13},{10,... | collective-permute-start | bytes 786440 | tf_op jit(solution)/shard_map/ppermute | solution.py:546
  418.8 30.1 %collective-permute-start.31 = (bf16[384,3072]{1,0:T(8,128)(2,1)}, bf16[384,3072]{1,0:T(8,128)(2,1)}, u32[]{:S(2)}, u32[]{:S(2)}) collective-permute-start(bf16[384,3072]{1,0:T(8,128)(2,1)} %slice.250), channel_id=1, source_target_pairs={{0,1},{1,0},{2,6},{3,7},{4,5},{5,4},{6,2},{7,3},{8,9},{9,8},{10,14... | collective-permute-start | bytes 7077896 | tf_op jit(solution)/shard_map/ppermute | solution.py:546
  455.5 3.3 collective-permute-start.33
  456.5 21.5 %collective-permute-start.32 = (bf16[192,3072]{1,0:T(8,128)(2,1)S(1)}, bf16[192,3072]{1,0:T(8,128)(2,1)S(1)}, u32[]{:S(2)}, u32[]{:S(2)}) collective-permute-start(bf16[192,3072]{1,0:T(8,128)(2,1)S(1)} %slice.252), channel_id=1, source_target_pairs={{0,4},{1,5},{2,3},{3,2},{4,0},{5,1},{6,7},{7,6},{8,12},{9,13},{10,... | collective-permute-start | bytes 3538952 | tf_op jit(solution)/shard_map/ppermute | solution.py:546
  459.2 14.2 %collective-permute-start.34 = (bf16[384,640]{1,0:T(8,128)(2,1)S(1)}, bf16[384,640]{1,0:T(8,128)(2,1)S(1)}, u32[]{:S(2)}, u32[]{:S(2)}) collective-permute-start(bf16[384,640]{1,0:T(8,128)(2,1)S(1)} %slice.254), channel_id=1, source_target_pairs={{0,1},{1,0},{2,6},{3,7},{4,5},{5,4},{6,2},{7,3},{8,9},{9,8},{10,14... | collective-permute-start | bytes 1474568 | tf_op jit(solution)/shard_map/ppermute | solution.py:546
  474.2 6.6 %collective-permute-start.35 = (bf16[192,640]{1,0:T(8,128)(2,1)}, bf16[192,640]{1,0:T(8,128)(2,1)}, u32[]{:S(2)}, u32[]{:S(2)}) collective-permute-start(bf16[192,640]{1,0:T(8,128)(2,1)} %get-tuple-element.166), channel_id=1, source_target_pairs={{0,4},{1,5},{2,3},{3,2},{4,0},{5,1},{6,7},{7,6},{8,12},{9,13},{10,... | collective-permute-start | bytes 737288 | tf_op jit(solution)/shard_map/ppermute | solution.py:546
  487.1 26.8 %all-to-all-start.2 = ((bf16[8,48,2304]{2,1,0:T(8,128)(2,1)}), bf16[8,48,2304]{2,1,0:T(8,128)(2,1)}, u32[]{:S(2)}, u32[]{:S(2)}) async-start(bf16[8,48,2304]{2,1,0:T(8,128)(2,1)} %bitcast.117), calls=%async_computation.6 | async-start | bytes 3538944 | tf_op jit(solution)/shard_map/all_to_all | solution.py:626
  (52 other events, 286.4 us)
Sparse Core Ops, SparseCore 0:
  59.7 69.4 all-gather.3
  130.8 68.5 all-gather.7
  201.0 68.5 all-gather.5
  271.8 66.9 reduce-scatter.4
  341.0 66.6 reduce-scatter.6
  409.8 66.6 reduce-scatter.8
  484.5 32.6 reduce-scatter.10

commit v3 on v2

--- a/solution.py
+++ b/solution.py
@@ -364,15 +364,21 @@
             out_ref[there, at + real : at + cols] = jnp.zeros((rows, cols - real), BF16)
 
 
-def unpack_kernel(moves, cols, *refs):
+def unpack_kernel(moves, cols, total, *refs):
     in_refs, out_ref = refs[:-1], refs[-1]
     rows = out_ref.shape[0]
-    for device, chunk, kind, source, real in moves:
-        if real:
-            which = min(chunk, len(in_refs) - 1)
-            at = ((chunk - which) * 3 + kind) * cols
-            block = in_refs[which][device * rows : (device + 1) * rows, at : at + real]
-            out_ref[:, source : source + real] = block.astype(F32)
+
+    def one_kind(kind_now):
+        for device, chunk, kind, source, real in moves:
+            if real and kind == kind_now:
+                which = min(chunk, len(in_refs) - 1)
+                at = ((chunk - which) * 3 + kind) * cols
+                block = in_refs[which][device * rows : (device + 1) * rows, at : at + real]
+                start = source - kind * total
+                out_ref[:, start : start + real] = block.astype(F32)
+
+    for kind in range(3):
+        pl.when(pl.program_id(0) == kind)(functools.partial(one_kind, kind))
 
 
 def pack_slices(w_mlp, n_plane, chunks, cols):
@@ -401,10 +407,14 @@
         return wide.reshape(rows, 3 * total).astype(F32)
     moves = list(slice_moves(n_plane, chunks, cols, total))
     return pl.pallas_call(
-        functools.partial(unpack_kernel, moves, cols),
+        functools.partial(unpack_kernel, moves, cols, total),
+        grid=(3,),
         out_shape=jax.ShapeDtypeStruct((rows, 3 * total), F32),
-        in_specs=vmem_specs(len(arrays)),
-        out_specs=vmem_specs(1)[0],
+        in_specs=[
+            pl.BlockSpec(array.shape, lambda i: (0, 0), pipeline_mode=pl.Buffered(1))
+            for array in arrays
+        ],
+        out_specs=pl.BlockSpec((rows, total), lambda i: (0, i)),
         compiler_params=pltpu.CompilerParams(vmem_limit_bytes=VMEM_LIMIT),
         cost_estimate=SMALL,
     )(*arrays)

time: 534 us -> 534 us (level)
  transfers between devices with their start and end apart: 46 -> 46, of which waited for: 27 -> 26; matrix products, arithmetic and copies ran while one was open for 22% -> 22% of each run, Pallas kernels for 27% -> 27%
where the time goes in v3:
time: 534 us; the launch traced here: 527 us
  waiting for transfers between devices  173 us (32%)
  Pallas kernels  146 us (27%)
  other arithmetic  60.8 us (11%)
  local copies, waits for them, and re-layouts  59.4 us (11%)
  starting transfers between devices  53.2 us (10%)
  between operations  18.5 us (3%)
  matrix products  15.7 us (3%)
    ppermute x33, waiting for transfers between devices, swap(): return lax.ppermute(array, PLANE, pairs)  133 us
    pallas_call x2, Pallas kernels, feed_forward(): pl.pallas_call(functools.partial(ffn_kernel, cols, count, not sums, with_...  86.4 us
    all_to_all x3, waiting for transfers between devices, swap_rows(): return lax.all_to_all(array, PLANE, split_axis=0, concat_axis=0, tiled=True)  30.2 us
    ppermute x33, starting transfers between devices, swap(): return lax.ppermute(array, PLANE, pairs)  29.9 us
    convert_element_type x14, other arithmetic, fold(): return (near.astype(F32) + self.swap(far, step).astype(F32)).astype(BF16)  28.6 us
    all_to_all x3, starting transfers between devices, swap_rows(): return lax.all_to_all(array, PLANE, split_axis=0, concat_axis=0, tiled=True)  16.5 us
    unnamed x119, local copies, waits for them, and re-layouts  16 us
    dot_general x6, matrix products, dot(): lax.dot_general(left, right, (((left_dim,), (right_dim,)), ((), ())), pre...  15.7 us
  transfers between devices with their start and end apart: 46, of which 26 were waited for; matrix products, arithmetic and copies ran while one was open for 22% of the time, Pallas kernels for 27%

profile of v3, /device:TPU:0, one launch (start us, length us, event | category | flops | bytes accessed | tf_op | source)
XLA Modules:
  0.0 527.0 jit_solution(3726794549670244284)
XLA Ops:
  12.8 5.0 collective-permute-start.2
  18.9 3.5 shard_map.170
  22.4 3.9 all-to-all-start
  37.9 4.2 collective-permute-done
  43.1 5.5 %collective-permute-done.1 = bf16[48,3712]{1,0:T(8,128)(2,1)} collective-permute-done((bf16[48,3712]{1,0:T(8,128)(2,1)}, bf16[48,3712]{1,0:T(8,128)(2,1)}, u32[]{:S(2)}, u32[]{:S(2)}) %collective-permute-start.1) | collective-permute-done | bytes 356384 | tf_op jit(solution)/shard_map/ppermute | solution.py:677
  53.2 4.8 all-to-all-done
  64.3 11.4 %collective-permute-done.7 = bf16[384,640]{1,0:T(8,128)(2,1)S(1)} collective-permute-done((bf16[384,640]{1,0:T(8,128)(2,1)S(1)}, bf16[384,640]{1,0:T(8,128)(2,1)S(1)}, u32[]{:S(2)}, u32[]{:S(2)}) %collective-permute-start.7) | collective-permute-done | bytes 491552 | tf_op jit(solution)/shard_map/ppermute | solution.py:556
  86.6 7.6 %collective-permute-done.5 = bf16[384,1536]{1,0:T(8,128)(2,1)} collective-permute-done((bf16[384,1536]{1,0:T(8,128)(2,1)}, bf16[384,1536]{1,0:T(8,128)(2,1)}, u32[]{:S(2)}, u32[]{:S(2)}) %collective-permute-start.5) | collective-permute-done | bytes 1179680 | tf_op jit(solution)/shard_map/ppermute | solution.py:556
  94.3 2.4 constant_dynamic-update-slice_fusion
  105.3 4.5 collective-permute-done.6
  116.9 3.5 collective-permute-done.10
  125.0 15.1 %collective-permute-done.11 = bf16[256,1536]{1,0:T(8,128)(2,1)S(1)} collective-permute-done((bf16[256,1536]{1,0:T(8,128)(2,1)S(1)}, bf16[256,1536]{1,0:T(8,128)(2,1)S(1)}, u32[]{:S(2)}, u32[]{:S(2)}) %collective-permute-start.11) | collective-permute-done | bytes 786464 | tf_op jit(solution)/shard_map/ppermute | solution.py:556
  141.9 2.5 fusion.37
  148.6 9.6 %shard_map.171 = (bf16[1536,256]{1,0:T(8,128)(2,1)}, f32[8,1536]{1,0:T(8,128)}) custom-call(s32[8]{0:T(128)} %and_convert_fusion.need_ref, s32[2048,2]{1,0:T(8,128)} %copy.31.kinfo_ref, s32[8,256]{1,0:T(8,128)} %add_add_fusion.qinfo_ref, bf16[1536,256]{1,0:T(8,128)(2,1)} %bitcast.118, bf16[2048,512]{1,0:T(8,128)(2,1)} %copy-done.7), custom_call_target="tpu_custom_call" | custom-call | flops 1024 | bytes 1024 | tf_op jit(solution)/shard_map/pallas_call | solution.py:186
  170.3 10.9 %collective-permute-done.17 = bf16[256,1536]{1,0:T(8,128)(2,1)S(1)} collective-permute-done((bf16[256,1536]{1,0:T(8,128)(2,1)S(1)}, bf16[256,1536]{1,0:T(8,128)(2,1)S(1)}, u32[]{:S(2)}, u32[]{:S(2)}) %collective-permute-start.17) | collective-permute-done | bytes 786464 | tf_op jit(solution)/shard_map/ppermute | solution.py:556
  183.4 18.4 %collective-permute-done.18 = bf16[512,1536]{1,0:T(8,128)(2,1)S(1)} collective-permute-done((bf16[512,1536]{1,0:T(8,128)(2,1)S(1)}, bf16[512,1536]{1,0:T(8,128)(2,1)S(1)}, u32[]{:S(2)}, u32[]{:S(2)}) %collective-permute-start.18) | collective-permute-done | bytes 1572896 | tf_op jit(solution)/shard_map/ppermute | solution.py:556
  203.5 5.7 %collective-permute-done.19.refs_1_.mid_far = bf16[1024,1536]{1,0:T(8,128)(2,1)} collective-permute-done((bf16[1024,1536]{1,0:T(8,128)(2,1)S(1)}, bf16[1024,1536]{1,0:T(8,128)(2,1)}, u32[]{:S(2)}, u32[]{:S(2)}) %collective-permute-start.19) | collective-permute-done | bytes 3145760 | tf_op jit(solution)/shard_map/ppermute | solution.py:556
  209.3 61.5 %shard_map.172 = (bf16[1024,1536]{1,0:T(8,128)(2,1)}, bf16[1024,1536]{1,0:T(8,128)(2,1)}, bf16[1024,1536]{1,0:T(8,128)(2,1)}, bf16[1024,1536]{1,0:T(8,128)(2,1)}...) custom-call(bf16[1024,1536]{1,0:T(8,128)(2,1)} %copy-done.2, ...), custom_call_target="tpu_custom_call" | custom-call | flops 1024 | bytes 1024 | tf_op jit(solution)/shard_map/pallas_call | solution.py:302
  270.8 24.9 %shard_map.173 = (bf16[1024,1536]{1,0:T(8,128)(2,1)}, bf16[1024,1536]{1,0:T(8,128)(2,1)}, bf16[1024,1536]{1,0:T(8,128)(2,1)}, bf16[1024,1536]{1,0:T(8,128)(2,1)}, bf16[2048,1152]{1,0:T(8,128)(2,1)}) custom-call(bf16[1024,1536]{1,0:T(8,128)(2,1)} %copy-done.2, bf16[1024,1536]{1,0:T(8,128)(2,1)} %collective-permute-done.19.refs_1_.mid_far, ...), custom_call_target="tpu_custom_call" | custom-call | flops 1024 | bytes 1024 | tf_op jit(solution)/shard_map/pallas_call | solution.py:302
  296.3 8.6 %collective-permute-done.21 = bf16[1024,1536]{1,0:T(8,128)(2,1)S(1)} collective-permute-done((bf16[1024,1536]{1,0:T(8,128)(2,1)}, bf16[1024,1536]{1,0:T(8,128)(2,1)S(1)}, u32[]{:S(2)}, u32[]{:S(2)}) %collective-permute-start.21) | collective-permute-done | bytes 3145760 | tf_op jit(solution)/shard_map/ppermute | solution.py:556
  304.9 3.0 add_convert_fusion.2
  311.1 13.8 %shard_map.174 = bf16[1536,1152]{1,0:T(8,128)(2,1)} custom-call(bf16[1024,1536]{1,0:T(8,128)(2,1)} %copy-done.2, bf16[1024,1536]{1,0:T(8,128)(2,1)} %collective-permute-done.19.refs_1_.mid_far, bf16[1024,1536]{1,0:T(8,128)(2,1)} %constant_dynamic-update-slice_fusion.12.refs_2_.cot_near, bf16[1024,1536]{1,0:T(8,128)(2,1)} %collective-permute-done.20.refs_3_.cot_far, ...), custom_call_target="tpu_custom_call" | custom-call | flops 1024 | bytes 1024 | tf_op jit(solution)/shard_map/pallas_call | solution.py:336
  324.9 4.9 collective-permute-done.22
  334.1 3.7 add_convert_fusion.1
  337.8 6.3 %collective-permute-done.24 = bf16[256,1536]{1,0:T(8,128)(2,1)S(1)} collective-permute-done((bf16[256,1536]{1,0:T(8,128)(2,1)S(1)}, bf16[256,1536]{1,0:T(8,128)(2,1)S(1)}, u32[]{:S(2)}, u32[]{:S(2)}) %collective-permute-start.24) | collective-permute-done | bytes 786464 | tf_op jit(solution)/shard_map/ppermute | solution.py:556
  348.5 4.9 convolution_convert_fusion.do_ref
  353.5 14.1 %shard_map.175 = (bf16[256,1536]{1,0:T(8,128)(2,1)}, bf16[1024,512]{1,0:T(8,128)(2,1)}, bf16[1024,512]{1,0:T(8,128)(2,1)}) custom-call(s32[8]{0:T(128)} %and_convert_fusion.need_ref, s32[2048,2]{1,0:T(8,128)} %copy.31.kinfo_ref, s32[8,256]{1,0:T(8,128)} %add_add_fusion.qinfo_ref, f32[64,256]{1,0:T(8,128)} %copy-done.35, ...), custom_call_target="tpu_custom_call" | custom-call | flops 1024 | bytes 1024 | tf_op jit(solution)/shard_map/pallas_call | solution.py:207
  368.2 8.2 %all-to-all-start.1 = ((bf16[8,48,1152]{2,1,0:T(8,128)(2,1)}), bf16[8,48,1152]{2,1,0:T(8,128)(2,1)}, u32[]{:S(2)}, u32[]{:S(2)}) async-start(bf16[8,48,1152]{2,1,0:T(8,128)(2,1)} %bitcast.154), calls=%async_computation.2 | async-start | bytes 1769472 | tf_op jit(solution)/shard_map/all_to_all | solution.py:636
  376.5 3.5 add_convert_fusion.4
  380.0 2.6 add_convert_fusion.7
  382.6 6.8 %all-to-all-done.1 = bf16[8,48,1152]{2,1,0:T(8,128)(2,1)} async-done(((bf16[8,48,1152]{2,1,0:T(8,128)(2,1)}), bf16[8,48,1152]{2,1,0:T(8,128)(2,1)}, u32[]{:S(2)}, u32[]{:S(2)}) %all-to-all-start.1) | async-done | bytes 884768 | tf_op jit(solution)/shard_map/all_to_all | solution.py:636
  389.3 8.9 %shard_map.176 = (bf16[768,3072]{1,0:T(8,128)(2,1)}, bf16[768,3072]{1,0:T(8,128)(2,1)}) custom-call(s32[8]{0:T(128)} %stack.91.dev_ref, bf16[256,1536]{1,0:T(8,128)(2,1)} %copy-done.16, bf16[256,1536]{1,0:T(8,128)(2,1)} %get-tuple-element.100.refs_1_, bf16[256,1536]{1,0:T(8,128)(2,1)} %copy-done.28, bf16[1536,256]{1,0:T(8,128)(2,1)} %get-tuple-element.76.o_ref.refs_3_), custom_call_target="tpu_custom_call" | custom-call | flops 1024 | bytes 1024 | tf_op jit(solution)/shard_map/pallas_call | solution.py:478
  399.9 2.4 fusion.42
  406.5 5.7 %add_convert_fusion = bf16[768,3072]{1,0:T(8,128)(2,1)S(1)} fusion(bf16[768,3072]{1,0:T(8,128)(2,1)} %collective-permute-done.28, bf16[768,3072]{1,0:T(8,128)(2,1)} %get-tuple-element.103), kind=kLoop, calls=%fused_computation.2 | loop fusion | flops 9437184 | bytes 14155776 | tf_op jit(solution)/shard_map/convert_element_type | solution.py:571
  420.0 2.3 add_convert_fusion.9
  422.3 4.0 collective-permute-done.30
  432.3 5.0 fusion.5
  440.4 8.4 %collective-permute-done.31 = bf16[384,3072]{1,0:T(8,128)(2,1)} collective-permute-done((bf16[384,3072]{1,0:T(8,128)(2,1)}, bf16[384,3072]{1,0:T(8,128)(2,1)}, u32[]{:S(2)}, u32[]{:S(2)}) %collective-permute-start.31) | collective-permute-done | bytes 2359328 | tf_op jit(solution)/shard_map/ppermute | solution.py:556
  448.8 3.3 add_convert_fusion.3
  452.1 3.3 shard_map.177
  459.9 13.1 %collective-permute-done.34 = bf16[384,640]{1,0:T(8,128)(2,1)S(1)} collective-permute-done((bf16[384,640]{1,0:T(8,128)(2,1)S(1)}, bf16[384,640]{1,0:T(8,128)(2,1)S(1)}, u32[]{:S(2)}, u32[]{:S(2)}) %collective-permute-start.34) | collective-permute-done | bytes 491552 | tf_op jit(solution)/shard_map/ppermute | solution.py:556
  474.9 2.8 collective-permute-done.32
  481.5 2.5 pad_maximum_fusion.4
  484.0 2.8 pad_maximum_fusion.2
  486.7 4.4 all-to-all-start.2
  491.2 3.5 fusion.13
  494.8 18.7 %all-to-all-done.2 = bf16[8,48,2304]{2,1,0:T(8,128)(2,1)} async-done(((bf16[8,48,2304]{2,1,0:T(8,128)(2,1)}), bf16[8,48,2304]{2,1,0:T(8,128)(2,1)}, u32[]{:S(2)}, u32[]{:S(2)}) %all-to-all-start.2) | async-done | bytes 1769504 | tf_op jit(solution)/shard_map/all_to_all | solution.py:636
  513.5 4.4 shard_map.179
  (337 shorter events, 127.7 us)
Async XLA Ops:
  12.8 36.8 %collective-permute-start.2 = (bf16[48,3712]{1,0:T(8,128)(2,1)}, bf16[48,3712]{1,0:T(8,128)(2,1)}, u32[]{:S(2)}, u32[]{:S(2)}) collective-permute-start(bf16[48,3712]{1,0:T(8,128)(2,1)} %concatenate.98), channel_id=1, source_target_pairs={{0,24},{8,0},{16,8},{24,16},{1,25},{9,1},{17,9},{25,17},{2,26},{10... | collective-permute-start | bytes 1069064 | tf_op jit(solution)/shard_map/ppermute | solution.py:677
  17.9 30.7 %collective-permute-start.1 = (bf16[48,3712]{1,0:T(8,128)(2,1)}, bf16[48,3712]{1,0:T(8,128)(2,1)}, u32[]{:S(2)}, u32[]{:S(2)}) collective-permute-start(bf16[48,3712]{1,0:T(8,128)(2,1)} %concatenate.98), channel_id=1, source_target_pairs={{0,16},{8,24},{16,0},{24,8},{1,17},{9,25},{17,1},{25,9},{2,18},{10... | collective-permute-start | bytes 1069064 | tf_op jit(solution)/shard_map/ppermute | solution.py:677
  17.9 24.2 %collective-permute-start = (bf16[48,3712]{1,0:T(8,128)(2,1)}, bf16[48,3712]{1,0:T(8,128)(2,1)}, u32[]{:S(2)}, u32[]{:S(2)}) collective-permute-start(bf16[48,3712]{1,0:T(8,128)(2,1)} %concatenate.98), channel_id=1, source_target_pairs={{0,8},{8,16},{16,24},{24,0},{1,9},{9,17},{17,25},{25,1},{2,10},{10... | collective-permute-start | bytes 1069064 | tf_op jit(solution)/shard_map/ppermute | solution.py:677
  22.4 35.6 %all-to-all-start = ((bf16[8,48,3456]{2,1,0:T(8,128)(2,1)}), bf16[8,48,3456]{2,1,0:T(8,128)(2,1)S(1)}, u32[]{:S(2)}, u32[]{:S(2)}) async-start(bf16[8,48,3456]{2,1,0:T(8,128)(2,1)} %bitcast.109), calls=%async_computation | async-start | bytes 5308416 | tf_op jit(solution)/shard_map/all_to_all | solution.py:636
  26.2 177.2 %all-gather.4.cloned.1.call-start = ((), (), s32[]{:S(2)}) async-start(), calls=%async_computation.7 | async-start | bytes 4423680 | tf_op jit(solution)/shard_map/all_gather | solution.py:639
  36.0 111.3 %copy-start.35 = (f32[64,256]{1,0:T(8,128)}, f32[64,256]{1,0:T(8,128)S(1)}, u32[]{:S(2)}) copy-start(f32[64,256]{1,0:T(8,128)S(1)} %get-tuple-element.176.cos_ref) | copy-start | bytes 196612
  37.9 46.1 %copy-start.32 = (f32[256,64]{1,0:T(8,128)}, f32[256,64]{1,0:T(8,128)S(1)}, u32[]{:S(2)}) copy-start(f32[256,64]{1,0:T(8,128)S(1)} %get-tuple-element.175) | copy-start | bytes 196612
  51.7 10.1 %collective-permute-start.3 = (bf16[192,640]{1,0:T(8,128)(2,1)S(1)}, bf16[192,640]{1,0:T(8,128)(2,1)S(1)}, u32[]{:S(2)}, u32[]{:S(2)}) collective-permute-start(bf16[192,640]{1,0:T(8,128)(2,1)S(1)} %slice.222), channel_id=1, source_target_pairs={{0,4},{1,5},{2,3},{3,2},{4,0},{5,1},{6,7},{7,6},{8,12},{9,13},{10,... | collective-permute-start | bytes 737288 | tf_op jit(solution)/shard_map/ppermute | solution.py:556
  59.6 143.9 %all-gather.8.cloned.1.call-start = ((), (), s32[]{:S(2)}) async-start(), calls=%async_computation.9 | async-start | bytes 4423680 | tf_op jit(solution)/shard_map/all_gather | solution.py:639
  61.9 13.8 %collective-permute-start.7 = (bf16[384,640]{1,0:T(8,128)(2,1)S(1)}, bf16[384,640]{1,0:T(8,128)(2,1)S(1)}, u32[]{:S(2)}, u32[]{:S(2)}) collective-permute-start(bf16[384,640]{1,0:T(8,128)(2,1)S(1)} %pad_maximum_fusion.9), channel_id=1, source_target_pairs={{0,1},{1,0},{2,6},{3,7},{4,5},{5,4},{6,2},{7,3},{8,9},{9,8},{10,14... | collective-permute-start | bytes 1474568 | tf_op jit(solution)/shard_map/ppermute | solution.py:556
  63.4 13.2 %collective-permute-start.4 = (bf16[192,1536]{1,0:T(8,128)(2,1)S(1)}, bf16[192,1536]{1,0:T(8,128)(2,1)S(1)}, u32[]{:S(2)}, u32[]{:S(2)}) collective-permute-start(bf16[192,1536]{1,0:T(8,128)(2,1)S(1)} %get-tuple-element.67), channel_id=1, source_target_pairs={{0,4},{1,5},{2,3},{3,2},{4,0},{5,1},{6,7},{7,6},{8,12},{9,13},{10,... | collective-permute-start | bytes 1769480 | tf_op jit(solution)/shard_map/ppermute | solution.py:556
  75.8 3.2 collective-permute-start.8
  77.8 16.5 %collective-permute-start.5 = (bf16[384,1536]{1,0:T(8,128)(2,1)}, bf16[384,1536]{1,0:T(8,128)(2,1)}, u32[]{:S(2)}, u32[]{:S(2)}) collective-permute-start(bf16[384,1536]{1,0:T(8,128)(2,1)} %pad_maximum_fusion.5), channel_id=1, source_target_pairs={{0,1},{1,0},{2,6},{3,7},{4,5},{5,4},{6,2},{7,3},{8,9},{9,8},{10,14... | collective-permute-start | bytes 3538952 | tf_op jit(solution)/shard_map/ppermute | solution.py:556
  96.7 6.7 %collective-permute-start.9 = (bf16[256,512]{1,0:T(8,128)(2,1)}, bf16[256,512]{1,0:T(8,128)(2,1)}, u32[]{:S(2)}, u32[]{:S(2)}) collective-permute-start(bf16[256,512]{1,0:T(8,128)(2,1)} %pad_maximum_fusion.10), channel_id=1, source_target_pairs={{0,4},{1,5},{2,3},{3,2},{4,0},{5,1},{6,7},{7,6},{8,12},{9,13},{10,... | collective-permute-start | bytes 786440 | tf_op jit(solution)/shard_map/ppermute | solution.py:556
  97.8 12.0 %collective-permute-start.6 = (bf16[192,1536]{1,0:T(8,128)(2,1)S(1)}, bf16[192,1536]{1,0:T(8,128)(2,1)}, u32[]{:S(2)}, u32[]{:S(2)}) collective-permute-start(bf16[192,1536]{1,0:T(8,128)(2,1)S(1)} %copy-done.31), channel_id=1, source_target_pairs={{0,4},{1,5},{2,3},{3,2},{4,0},{5,1},{6,7},{7,6},{8,12},{9,13},{10,... | collective-permute-start | bytes 1769480 | tf_op jit(solution)/shard_map/ppermute | solution.py:556
  101.3 169.6 %all-gather.6.cloned.1.call-start = ((), (), s32[]{:S(2)}) async-start(), calls=%async_computation.8 | async-start | bytes 4423680 | tf_op jit(solution)/shard_map/all_gather | solution.py:639
  101.5 40.4 %collective-permute-start.12 = (bf16[768,1536]{1,0:T(8,128)(2,1)}, bf16[768,1536]{1,0:T(8,128)(2,1)}, u32[]{:S(2)}, u32[]{:S(2)}) collective-permute-start(bf16[768,1536]{1,0:T(8,128)(2,1)} %constant_dynamic-update-slice_fusion), channel_id=1, source_target_pairs={{0,2},{1,3},{2,0},{3,1},{4,6},{5,7},{6,4},{7,5},{8,10},{9,11},{10,... | collective-permute-start | bytes 7077896 | tf_op jit(solution)/shard_map/ppermute | solution.py:556
  110.8 9.6 %collective-permute-start.10 = (bf16[512,512]{1,0:T(8,128)(2,1)}, bf16[512,512]{1,0:T(8,128)(2,1)}, u32[]{:S(2)}, u32[]{:S(2)}) collective-permute-start(bf16[512,512]{1,0:T(8,128)(2,1)} %pad_maximum_fusion.8), channel_id=1, source_target_pairs={{0,1},{1,0},{2,6},{3,7},{4,5},{5,4},{6,2},{7,3},{8,9},{9,8},{10,14... | collective-permute-start | bytes 1572872 | tf_op jit(solution)/shard_map/ppermute | solution.py:556
  121.5 20.3 %collective-permute-start.13 = (bf16[1024,512]{1,0:T(8,128)(2,1)S(1)}, bf16[1024,512]{1,0:T(8,128)(2,1)S(1)}, u32[]{:S(2)}, u32[]{:S(2)}) collective-permute-start(bf16[1024,512]{1,0:T(8,128)(2,1)S(1)} %get-tuple-element.160), channel_id=1, source_target_pairs={{0,2},{1,3},{2,0},{3,1},{4,6},{5,7},{6,4},{7,5},{8,10},{9,11},{10,... | collective-permute-start | bytes 3145736 | tf_op jit(solution)/shard_map/ppermute | solution.py:556
  121.6 18.5 %collective-permute-start.11 = (bf16[256,1536]{1,0:T(8,128)(2,1)S(1)}, bf16[256,1536]{1,0:T(8,128)(2,1)S(1)}, u32[]{:S(2)}, u32[]{:S(2)}) collective-permute-start(bf16[256,1536]{1,0:T(8,128)(2,1)S(1)} %copy-done.9), channel_id=1, source_target_pairs={{0,4},{1,5},{2,3},{3,2},{4,0},{5,1},{6,7},{7,6},{8,12},{9,13},{10,... | collective-permute-start | bytes 2359304 | tf_op jit(solution)/shard_map/ppermute | solution.py:556
  124.1 34.1 %collective-permute-start.15 = (bf16[384,1536]{1,0:T(8,128)(2,1)S(1)}, bf16[384,1536]{1,0:T(8,128)(2,1)S(1)}, u32[]{:S(2)}, u32[]{:S(2)}) collective-permute-start(bf16[384,1536]{1,0:T(8,128)(2,1)S(1)} %constant_dynamic-update-slice_fusion.3), channel_id=1, source_target_pairs={{0,1},{1,0},{2,6},{3,7},{4,5},{5,4},{6,2},{7,3},{8,9},{9,8},{10,14... | collective-permute-start | bytes 3538952 | tf_op jit(solution)/shard_map/ppermute | solution.py:556
  140.2 22.4 %collective-permute-start.14 = (bf16[512,1536]{1,0:T(8,128)(2,1)S(1)}, bf16[512,1536]{1,0:T(8,128)(2,1)S(1)}, u32[]{:S(2)}, u32[]{:S(2)}) collective-permute-start(bf16[512,1536]{1,0:T(8,128)(2,1)S(1)} %constant_dynamic-update-slice_fusion.7), channel_id=1, source_target_pairs={{0,1},{1,0},{2,6},{3,7},{4,5},{5,4},{6,2},{7,3},{8,9},{9,8},{10,14... | collective-permute-start | bytes 4718600 | tf_op jit(solution)/shard_map/ppermute | solution.py:556
  158.4 5.6 %collective-permute-start.16 = (bf16[768,1536]{1,0:T(8,128)(2,1)S(1)}, bf16[768,1536]{1,0:T(8,128)(2,1)S(1)}, u32[]{:S(2)}, u32[]{:S(2)}) collective-permute-start(bf16[768,1536]{1,0:T(8,128)(2,1)S(1)} %pad_maximum_fusion.1), channel_id=1, source_target_pairs={{0,2},{1,3},{2,0},{3,1},{4,6},{5,7},{6,4},{7,5},{8,10},{9,11},{10,... | collective-permute-start | bytes 7077896 | tf_op jit(solution)/shard_map/ppermute | solution.py:556
  169.1 12.1 %collective-permute-start.17 = (bf16[256,1536]{1,0:T(8,128)(2,1)S(1)}, bf16[256,1536]{1,0:T(8,128)(2,1)S(1)}, u32[]{:S(2)}, u32[]{:S(2)}) collective-permute-start(bf16[256,1536]{1,0:T(8,128)(2,1)S(1)} %multiply_convert_fusion), channel_id=1, source_target_pairs={{0,4},{1,5},{2,3},{3,2},{4,0},{5,1},{6,7},{7,6},{8,12},{9,13},{10,... | collective-permute-start | bytes 2359304 | tf_op jit(solution)/shard_map/ppermute | solution.py:556
  170.2 177.3 %reduce-scatter.5.cloned.1.call-start = ((), (), s32[]{:S(2)}) async-start(), calls=%async_computation.10 | async-start | bytes 4423680 | tf_op jit(solution)/shard_map/reduce_scatter | solution.py:642
  181.3 20.5 %collective-permute-start.18 = (bf16[512,1536]{1,0:T(8,128)(2,1)S(1)}, bf16[512,1536]{1,0:T(8,128)(2,1)S(1)}, u32[]{:S(2)}, u32[]{:S(2)}) collective-permute-start(bf16[512,1536]{1,0:T(8,128)(2,1)S(1)} %pad_maximum_fusion.3), channel_id=1, source_target_pairs={{0,1},{1,0},{2,6},{3,7},{4,5},{5,4},{6,2},{7,3},{8,9},{9,8},{10,14... | collective-permute-start | bytes 4718600 | tf_op jit(solution)/shard_map/ppermute | solution.py:556
  183.4 20.1 %collective-permute-start.20 = (bf16[1024,1536]{1,0:T(8,128)(2,1)}, bf16[1024,1536]{1,0:T(8,128)(2,1)}, u32[]{:S(2)}, u32[]{:S(2)}) collective-permute-start(bf16[1024,1536]{1,0:T(8,128)(2,1)} %constant_dynamic-update-slice_fusion.12.refs_2_.cot_near), channel_id=1, source_target_pairs={{0,2},{1,3},{2,0},{3,1},{4,6},{5,7},{6,4},{7,5},{8,10},{9,11},{10,... | collective-permute-start | bytes 9437192 | tf_op jit(solution)/shard_map/ppermute | solution.py:556
  203.4 5.9 %collective-permute-start.19 = (bf16[1024,1536]{1,0:T(8,128)(2,1)S(1)}, bf16[1024,1536]{1,0:T(8,128)(2,1)}, u32[]{:S(2)}, u32[]{:S(2)}) collective-permute-start(bf16[1024,1536]{1,0:T(8,128)(2,1)S(1)} %pad_maximum_fusion.refs_0_.mid_near), channel_id=1, source_target_pairs={{0,2},{1,3},{2,0},{3,1},{4,6},{5,7},{6,4},{7,5},{8,10},{9,11},{10,... | collective-permute-start | bytes 9437192 | tf_op jit(solution)/shard_map/ppermute | solution.py:556
  270.8 145.2 %reduce-scatter.7.cloned.1.call-start = ((), (), s32[]{:S(2)}) async-start(), calls=%async_computation.11 | async-start | bytes 4423680 | tf_op jit(solution)/shard_map/reduce_scatter | solution.py:642
  295.8 9.1 %collective-permute-start.21 = (bf16[1024,1536]{1,0:T(8,128)(2,1)}, bf16[1024,1536]{1,0:T(8,128)(2,1)S(1)}, u32[]{:S(2)}, u32[]{:S(2)}) collective-permute-start(bf16[1024,1536]{1,0:T(8,128)(2,1)} %get-tuple-element.86), channel_id=1, source_target_pairs={{0,2},{1,3},{2,0},{3,1},{4,6},{5,7},{6,4},{7,5},{8,10},{9,11},{10,... | collective-permute-start | bytes 9437192 | tf_op jit(solution)/shard_map/ppermute | solution.py:556
  295.9 38.2 %collective-permute-start.23 = (bf16[1024,1536]{1,0:T(8,128)(2,1)}, bf16[1024,1536]{1,0:T(8,128)(2,1)}, u32[]{:S(2)}, u32[]{:S(2)}) collective-permute-start(bf16[1024,1536]{1,0:T(8,128)(2,1)} %get-tuple-element.91), channel_id=1, source_target_pairs={{0,2},{1,3},{2,0},{3,1},{4,6},{5,7},{6,4},{7,5},{8,10},{9,11},{10,... | collective-permute-start | bytes 9437192 | tf_op jit(solution)/shard_map/ppermute | solution.py:556
  309.3 20.5 %collective-permute-start.22 = (bf16[512,1536]{1,0:T(8,128)(2,1)S(1)}, bf16[512,1536]{1,0:T(8,128)(2,1)}, u32[]{:S(2)}, u32[]{:S(2)}) collective-permute-start(bf16[512,1536]{1,0:T(8,128)(2,1)S(1)} %get-tuple-element.129), channel_id=1, source_target_pairs={{0,1},{1,0},{2,6},{3,7},{4,5},{5,4},{6,2},{7,3},{8,9},{9,8},{10,14... | collective-permute-start | bytes 4718600 | tf_op jit(solution)/shard_map/ppermute | solution.py:556
  332.1 12.1 %collective-permute-start.24 = (bf16[256,1536]{1,0:T(8,128)(2,1)S(1)}, bf16[256,1536]{1,0:T(8,128)(2,1)S(1)}, u32[]{:S(2)}, u32[]{:S(2)}) collective-permute-start(bf16[256,1536]{1,0:T(8,128)(2,1)S(1)} %slice.242), channel_id=1, source_target_pairs={{0,4},{1,5},{2,3},{3,2},{4,0},{5,1},{6,7},{7,6},{8,12},{9,13},{10,... | collective-permute-start | bytes 2359304 | tf_op jit(solution)/shard_map/ppermute | solution.py:556
  345.7 30.8 %collective-permute-start.25 = (bf16[512,1536]{1,0:T(8,128)(2,1)}, bf16[512,1536]{1,0:T(8,128)(2,1)}, u32[]{:S(2)}, u32[]{:S(2)}) collective-permute-start(bf16[512,1536]{1,0:T(8,128)(2,1)} %slice.197), channel_id=1, source_target_pairs={{0,1},{1,0},{2,6},{3,7},{4,5},{5,4},{6,2},{7,3},{8,9},{9,8},{10,14... | collective-permute-start | bytes 4718600 | tf_op jit(solution)/shard_map/ppermute | solution.py:556
  367.6 12.4 %collective-permute-start.26 = (bf16[1024,512]{1,0:T(8,128)(2,1)}, bf16[1024,512]{1,0:T(8,128)(2,1)}, u32[]{:S(2)}, u32[]{:S(2)}) collective-permute-start(bf16[1024,512]{1,0:T(8,128)(2,1)} %get-tuple-element.98), channel_id=1, source_target_pairs={{0,2},{1,3},{2,0},{3,1},{4,6},{5,7},{6,4},{7,5},{8,10},{9,11},{10,... | collective-permute-start | bytes 3145736 | tf_op jit(solution)/shard_map/ppermute | solution.py:556
  368.2 21.1 %all-to-all-start.1 = ((bf16[8,48,1152]{2,1,0:T(8,128)(2,1)}), bf16[8,48,1152]{2,1,0:T(8,128)(2,1)}, u32[]{:S(2)}, u32[]{:S(2)}) async-start(bf16[8,48,1152]{2,1,0:T(8,128)(2,1)} %bitcast.154), calls=%async_computation.2 | async-start | bytes 1769472 | tf_op jit(solution)/shard_map/all_to_all | solution.py:636
  376.4 102.7 %reduce-scatter.9.cloned.1.call-start = ((), (), s32[]{:S(2)}) async-start(), calls=%async_computation.12 | async-start | bytes 4423680 | tf_op jit(solution)/shard_map/reduce_scatter | solution.py:642
  398.2 8.3 %collective-permute-start.28 = (bf16[768,3072]{1,0:T(8,128)(2,1)}, bf16[768,3072]{1,0:T(8,128)(2,1)}, u32[]{:S(2)}, u32[]{:S(2)}) collective-permute-start(bf16[768,3072]{1,0:T(8,128)(2,1)} %get-tuple-element.104), channel_id=1, source_target_pairs={{0,2},{1,3},{2,0},{3,1},{4,6},{5,7},{6,4},{7,5},{8,10},{9,11},{10,... | collective-permute-start | bytes 14155784 | tf_op jit(solution)/shard_map/ppermute | solution.py:556
  398.9 119.0 %reduce-scatter.11.cloned.1.call-start = ((), (), s32[]{:S(2)}) async-start(), calls=%async_computation.13 | async-start | bytes 1781760 | tf_op jit(solution)/shard_map/reduce_scatter | solution.py:642
  402.2 13.8 %collective-permute-start.29 = (bf16[512,512]{1,0:T(8,128)(2,1)}, bf16[512,512]{1,0:T(8,128)(2,1)}, u32[]{:S(2)}, u32[]{:S(2)}) collective-permute-start(bf16[512,512]{1,0:T(8,128)(2,1)} %get-tuple-element.152), channel_id=1, source_target_pairs={{0,1},{1,0},{2,6},{3,7},{4,5},{5,4},{6,2},{7,3},{8,9},{9,8},{10,14... | collective-permute-start | bytes 1572872 | tf_op jit(solution)/shard_map/ppermute | solution.py:556
  404.8 15.2 %collective-permute-start.27 = (bf16[256,1536]{1,0:T(8,128)(2,1)}, bf16[256,1536]{1,0:T(8,128)(2,1)}, u32[]{:S(2)}, u32[]{:S(2)}) collective-permute-start(bf16[256,1536]{1,0:T(8,128)(2,1)} %slice.199), channel_id=1, source_target_pairs={{0,4},{1,5},{2,3},{3,2},{4,0},{5,1},{6,7},{7,6},{8,12},{9,13},{10,... | collective-permute-start | bytes 2359304 | tf_op jit(solution)/shard_map/ppermute | solution.py:556
  417.5 8.9 %collective-permute-start.30 = (bf16[256,512]{1,0:T(8,128)(2,1)S(1)}, bf16[256,512]{1,0:T(8,128)(2,1)S(1)}, u32[]{:S(2)}, u32[]{:S(2)}) collective-permute-start(bf16[256,512]{1,0:T(8,128)(2,1)S(1)} %slice.246), channel_id=1, source_target_pairs={{0,4},{1,5},{2,3},{3,2},{4,0},{5,1},{6,7},{7,6},{8,12},{9,13},{10,... | collective-permute-start | bytes 786440 | tf_op jit(solution)/shard_map/ppermute | solution.py:556
  419.7 29.2 %collective-permute-start.31 = (bf16[384,3072]{1,0:T(8,128)(2,1)}, bf16[384,3072]{1,0:T(8,128)(2,1)}, u32[]{:S(2)}, u32[]{:S(2)}) collective-permute-start(bf16[384,3072]{1,0:T(8,128)(2,1)} %slice.250), channel_id=1, source_target_pairs={{0,1},{1,0},{2,6},{3,7},{4,5},{5,4},{6,2},{7,3},{8,9},{9,8},{10,14... | collective-permute-start | bytes 7077896 | tf_op jit(solution)/shard_map/ppermute | solution.py:556
  455.4 3.1 collective-permute-start.33
  456.2 21.5 %collective-permute-start.32 = (bf16[192,3072]{1,0:T(8,128)(2,1)S(1)}, bf16[192,3072]{1,0:T(8,128)(2,1)S(1)}, u32[]{:S(2)}, u32[]{:S(2)}) collective-permute-start(bf16[192,3072]{1,0:T(8,128)(2,1)S(1)} %slice.252), channel_id=1, source_target_pairs={{0,4},{1,5},{2,3},{3,2},{4,0},{5,1},{6,7},{7,6},{8,12},{9,13},{10,... | collective-permute-start | bytes 3538952 | tf_op jit(solution)/shard_map/ppermute | solution.py:556
  458.8 14.2 %collective-permute-start.34 = (bf16[384,640]{1,0:T(8,128)(2,1)S(1)}, bf16[384,640]{1,0:T(8,128)(2,1)S(1)}, u32[]{:S(2)}, u32[]{:S(2)}) collective-permute-start(bf16[384,640]{1,0:T(8,128)(2,1)S(1)} %slice.254), channel_id=1, source_target_pairs={{0,1},{1,0},{2,6},{3,7},{4,5},{5,4},{6,2},{7,3},{8,9},{9,8},{10,14... | collective-permute-start | bytes 1474568 | tf_op jit(solution)/shard_map/ppermute | solution.py:556
  473.9 6.6 %collective-permute-start.35 = (bf16[192,640]{1,0:T(8,128)(2,1)}, bf16[192,640]{1,0:T(8,128)(2,1)}, u32[]{:S(2)}, u32[]{:S(2)}) collective-permute-start(bf16[192,640]{1,0:T(8,128)(2,1)} %get-tuple-element.166), channel_id=1, source_target_pairs={{0,4},{1,5},{2,3},{3,2},{4,0},{5,1},{6,7},{7,6},{8,12},{9,13},{10,... | collective-permute-start | bytes 737288 | tf_op jit(solution)/shard_map/ppermute | solution.py:556
  486.7 26.7 %all-to-all-start.2 = ((bf16[8,48,2304]{2,1,0:T(8,128)(2,1)}), bf16[8,48,2304]{2,1,0:T(8,128)(2,1)}, u32[]{:S(2)}, u32[]{:S(2)}) async-start(bf16[8,48,2304]{2,1,0:T(8,128)(2,1)} %bitcast.117), calls=%async_computation.6 | async-start | bytes 3538944 | tf_op jit(solution)/shard_map/all_to_all | solution.py:636
  (52 other events, 283.8 us)
Sparse Core Ops, SparseCore 0:
  59.7 69.4 all-gather.3
  130.8 68.5 all-gather.7
  201.0 68.5 all-gather.5
  271.8 64.9 reduce-scatter.4
  339.0 66.6 reduce-scatter.6
  407.8 66.6 reduce-scatter.8
  484.1 30.6 reduce-scatter.10
